TPU v7x, 256 devices: a whole 4x4x8 slice. The times are simulated.
256 devices in a mesh: dom: 64 (over z, y, core), feat: 4 (over x).
Axes of the slice: x: 4, y: 4, z: 8, core: 2. Of those that a mesh axis runs over, the one named last changes fastest.
Arguments:
- features: float32 [262144, 256], P('dom', 'feat'), may hold values from -6 to 6
- w_self: float32 [256, 256], P(None, 'feat'), may hold values from -0.375 to 0.375
- w_neigh: float32 [256, 256], P(None, 'feat'), may hold values from -0.375 to 0.375
- out_bias: float32 [256], P('feat'), may hold values from -3 to 3
- hub_rows: int32 [64, 64], P('dom'), may hold values from 0 to 4095
- replica_send_rows: int32 [64, 64, 128], P('dom'), may hold values from 0 to 4095
- ret_rows: int32 [64, 64, 64], P('dom'), may hold values from 0 to 4096, as said below
- tile_src: int32 [64, 96], P('dom'), may hold values from 0 to 95, each once within a row
- tile_dst: int32 [64, 96], P('dom'), may hold values from 0 to 31
- tile_vals: float32 [64, 96, 128, 128], P('dom'), may hold values from 0 to 0.086752765
Outputs:
- hidden_out: float32 [262144, 256], P('dom', 'feat')
Inputs may be any that keep to these rules, and one draw needn't show every extreme that they name: `hub_rows`: rows of the partition that holds the list. replica_send_rows[q, p, s] is a row of partition q; lists may repeat rows. ret_rows[q, p, s] is a row of partition q, or 4096 for an empty slot; every block of 64 slots fills from the front with at least one row, and some blocks are full. `tile_src`: each partition's tiles use every source tile row once.
All inputs are finite; a program needn't handle non-finite values.
Results may differ from a plain program's by a relative error of at most 0.000065.
Values sent between devices are 32-bit elements; how exact they have to be, the bound alone decides.
No kernel may reach another device: no remote copies, remote signals or barrier semaphores. Data moves between devices by JAX's collectives and lax.ppermute only.
A program may use at most 64 MiB of HBM per device.

v0:
```python
import jax
import jax.numpy as jnp
from jax import lax
from jax.sharding import PartitionSpec as P


def project(left, right):
    return jnp.dot(left, right, precision=lax.Precision.HIGHEST, preferred_element_type=jnp.float32)


def spread(source, hub_rows, replica_send_rows):
    feature_width = source.shape[1]
    hub_local = jnp.take(source, hub_rows[0], axis=0)
    outgoing = jnp.take(source, replica_send_rows[0], axis=0)
    hub_table = lax.all_gather(hub_local, "dom", axis=0, tiled=True)
    received_rows = lax.all_to_all(
        outgoing, "dom", split_axis=0, concat_axis=0, tiled=True
    ).reshape(-1, feature_width)
    return jnp.concatenate([hub_table, received_rows], axis=0)


def aggregate(mirror_table, tile_src, tile_dst, tile_vals, ret_rows, row_count):
    tile_size = tile_vals.shape[-1]
    columns = mirror_table.shape[1]
    blocks = mirror_table.reshape(-1, tile_size, columns)
    picked = jnp.take(blocks, tile_src[0], axis=0)
    products = jnp.einsum(
        "tij,tjf->tif",
        tile_vals[0],
        picked,
        precision=lax.Precision.HIGHEST,
        preferred_element_type=jnp.float32,
    )
    peer_count = ret_rows.shape[1]
    slot_count = ret_rows.shape[2]
    buffer = jnp.zeros((peer_count * slot_count // tile_size, tile_size, columns), jnp.float32)
    buffer = buffer.at[tile_dst[0]].add(products)
    returned = lax.all_to_all(
        buffer.reshape(peer_count, slot_count, columns),
        "dom",
        split_axis=0,
        concat_axis=0,
        tiled=True,
    )
    summed = jnp.zeros((row_count, columns), jnp.float32)
    return summed.at[ret_rows[0].reshape(-1)].add(returned.reshape(-1, columns), mode="drop")


def per_device(
    features,
    w_self,
    w_neigh,
    out_bias,
    hub_rows,
    replica_send_rows,
    ret_rows,
    tile_src,
    tile_dst,
    tile_vals,
):
    row_count = features.shape[0]
    portion = lax.all_gather(features, "feat", axis=1, tiled=True)
    own_term = project(portion, w_self)
    projected_rows = project(portion, w_neigh)
    mirror_table = spread(projected_rows, hub_rows, replica_send_rows)
    combined = own_term + aggregate(
        mirror_table, tile_src, tile_dst, tile_vals, ret_rows, row_count
    )
    return jax.nn.relu(combined + out_bias)


def solution(mesh):
    return jax.shard_map(
        per_device,
        mesh=mesh,
        in_specs=(
            P("dom", "feat"),
            P(None, "feat"),
            P(None, "feat"),
            P("feat"),
            P("dom", None),
            P("dom", None, None),
            P("dom", None, None),
            P("dom", None),
            P("dom", None),
            P("dom", None, None, None),
        ),
        out_specs=P("dom", "feat"),
        check_vma=False,
    )
```

profile of v0, /device:TPU:1, one launch (start us, length us, event | category | flops | bytes accessed | tf_op | source)
XLA Modules:
  0.0 320.8 jit_solution(10316742575160892817)
XLA Ops:
  6.5 0.0 copy-start
  6.5 0.0 all-gather.3.cloned.1.call-start
  6.5 0.7 all-gather.3.cloned.1.call-update
  7.3 0.8 compare_and_fusion
  8.0 0.8 fusion.11
  8.8 55.0 %all-gather.3.cloned.1.call-done = f32[4096,256]{0,1:T(8,128)} async-done(((f32[4096,64]{0,1:T(8,128)}), f32[4096,256]{0,1:T(8,128)}) %all-gather.3.cloned.1.call-update) | async-done | bytes 4194320 | tf_op jit(solution)/shard_map/all_gather | solution.py:62
  63.8 0.0 copy-done
  63.8 8.5 %fusion.16 = f32[4096,64]{1,0:T(8,128)S(1)} fusion(f32[4096,256]{0,1:T(8,128)} %all-gather.3.cloned.1.call-done, f32[256,64]{0,1:T(8,128)S(1)} %copy-done), kind=kOutput, calls=%fused_computation.38 | convolution fusion | flops 805306368 | bytes 5308416 | tf_op jit(solution)/shard_map/dot_general | solution.py:8
  72.3 27.9 %gather_fusion.1 = f32[8192,64]{1,0:T(8,128)} fusion(f32[4096,64]{1,0:T(8,128)S(1)} %fusion.16, s32[8192]{0:T(1024)S(1)} %fusion.11), kind=kCustom, calls=%fused_computation.1 | custom fusion | bytes 4227072 | tf_op jit(solution)/shard_map/jit(_take)/gather | solution.py:14
  100.2 3.8 %copy.51 = f32[64,128,64]{1,2,0:T(8,128)} copy(f32[64,128,64]{2,1,0:T(8,128)} %bitcast.56) | data formatting | bytes 4194304 | tf_op jit(solution)/shard_map/jit(_take)/gather | solution.py:14
  104.0 3.4 %broadcast_select_fusion = f32[64,128,64]{1,2,0:T(8,128)} fusion(f32[64,128,64]{1,2,0:T(8,128)} %copy.51, pred[64,128]{1,0:T(8,128)(4,1)S(1)} %compare_and_fusion), kind=kLoop, calls=%fused_computation.15 | loop fusion | flops 524288 | bytes 4202496 | tf_op jit(solution)/shard_map/jit(_take)/select_n | solution.py:14
  107.4 11.0 %all-to-all-start = ((f32[64,128,64]{1,2,0:T(8,128)}), f32[64,128,64]{1,2,0:T(8,128)}, u32[]{:S(2)}, u32[]{:S(2)}) async-start(f32[64,128,64]{1,2,0:T(8,128)} %broadcast_select_fusion), calls=%async_computation | async-start | bytes 4194304 | tf_op jit(solution)/shard_map/all_to_all | solution.py:16
  118.4 0.2 all-gather.5.cloned.1.call-start
  118.7 0.0 copy-done.6
  118.7 0.6 gather_fusion
  119.3 0.7 broadcast_select_fusion.1
  120.0 0.0 all-gather.5.cloned.1.call-update
  120.0 0.0 copy-done.7
  120.1 0.0 copy-done.8
  120.1 82.4 %all-gather.5.cloned.1.call-done = f32[4096,64]{1,0:T(8,128)} async-done(((f32[64,64]{1,0:T(8,128)}), f32[4096,64]{1,0:T(8,128)}) %all-gather.5.cloned.1.call-update) | async-done | bytes 1048592 | tf_op jit(solution)/shard_map/all_gather | solution.py:15
  202.5 3.1 copy.53
  205.7 0.0 all-to-all-done
  205.7 1.8 copy_bitcast_fusion.1
  207.5 0.0 copy-done.2
  207.5 0.4 copy_bitcast_fusion
  207.9 2.4 gather_fusion.2
  210.4 15.5 %fusion.3 = f32[96,128,64]{1,2,0:T(8,128)} fusion(f32[1,96,128,128]{3,2,1,0:T(8,128)} %param.19, f32[96,128,64]{1,2,0:T(8,128)} %gather_fusion.2, pred[96]{0:T(512)(128)(4,1)S(1)} %compare_and_fusion.2), kind=kOutput, calls=%fused_computation.12 | convolution fusion | flops 1208745984 | bytes 12583008 | tf_op jit(solution)/shard_map/tij,tjf->tif/dot_general | solution.py:27
  225.9 0.1 broadcast_in_dim.39
  226.0 10.3 %scatter_fusion = f32[32,128,64]{1,2,0:T(8,128)S(1)} fusion(f32[32,128,64]{1,2,0:T(8,128)S(1)} %broadcast_in_dim.39, s32[96]{0:T(128)S(1)} %fusion.12, f32[96,128,64]{1,2,0:T(8,128)} %fusion.3), kind=kCustom, calls=%fused_computation.3 | custom fusion | flops 786432 | bytes 9437568 | tf_op jit(solution)/shard_map/scatter-add | solution.py:37
  236.3 0.6 copy.55
  236.9 0.3 reshape.173
  237.2 2.5 copy.69
  239.8 3.5 %reshape.216 = f32[64,1,4096]{2,1,0:T(1,128)} reshape(f32[64,64,64]{2,1,0:T(8,128)} %bitcast.58) | data formatting | bytes 2097152
  243.3 6.6 %all-to-all-start.1 = ((f32[64,1,4096]{2,1,0:T(1,128)}), f32[64,1,4096]{2,1,0:T(1,128)S(1)}, u32[]{:S(2)}, u32[]{:S(2)}) async-start(f32[64,1,4096]{2,1,0:T(1,128)} %reshape.216), calls=%async_computation.1 | async-start | bytes 2097152 | tf_op jit(solution)/shard_map/all_to_all | solution.py:38
  249.9 0.1 reshape_squeeze.3
  250.0 0.0 copy-done.3
  250.1 0.0 copy-done.5
  250.1 5.9 %convolution_add_fusion = f32[4096,64]{0,1:T(8,128)} fusion(f32[4096,256]{0,1:T(8,128)} %all-gather.3.cloned.1.call-done, f32[256,64]{0,1:T(8,128)S(1)} %copy-done.3, f32[64]{0:T(128)S(1)} %copy-done.5), kind=kOutput, calls=%fused_computation.7 | convolution fusion | flops 805568512 | bytes 5308672 | tf_op jit(solution)/shard_map/dot_general | solution.py:8
  256.0 1.8 copy.58
  257.8 20.1 %all-to-all-done.1 = f32[64,1,4096]{2,1,0:T(1,128)S(1)} async-done(((f32[64,1,4096]{2,1,0:T(1,128)}), f32[64,1,4096]{2,1,0:T(1,128)S(1)}, u32[]{:S(2)}, u32[]{:S(2)}) %all-to-all-start.1) | async-done | bytes 1048608 | tf_op jit(solution)/shard_map/all_to_all | solution.py:38
  277.9 1.0 copy-done.1
  278.9 0.5 broadcast.113
  279.4 4.4 %reduce = f32[64,4096]{1,0:T(8,128)S(1)} reduce(f32[64,1,4096]{2,1,0:T(1,128)} %copy-done.1, f32[]{:T(128)} %broadcast.113), dimensions={1}, to_apply=%all_to_all.7.reduce_sub_computation | reduce | bytes 2097156 | tf_op jit(solution)/shard_map/all_to_all | solution.py:38
  283.8 2.2 reshape.217
  285.9 2.9 copy.62
  288.8 23.4 %scatter_fusion.1 = f32[4096,64]{1,0:T(8,128)S(1)} fusion(f32[4096,64]{1,0:T(8,128)S(1)} %copy.58, s32[4096]{0:T(1024)S(1)} %bitcast.60, f32[4096,64]{1,0:T(8,128)} %bitcast.57), kind=kCustom, calls=%fused_computation.4 | custom fusion | flops 262144 | bytes 3162112 | tf_op jit(solution)/shard_map/scatter-add | solution.py:46
  312.3 0.6 copy.60
  312.9 1.1 broadcast_maximum_fusion
  (17 shorter events, 0.1 us)
Async XLA Ops:
  6.5 57.3 %copy-start = (f32[256,64]{0,1:T(8,128)S(1)}, f32[256,64]{0,1:T(8,128)}, u32[]{:S(2)}) copy-start(f32[256,64]{0,1:T(8,128)} %param.12) | copy-start | bytes 196612
  6.5 57.3 %all-gather.3.cloned.1.call-start = ((), (), s32[]{:S(2)}) async-start(), calls=%async_computation.2 | async-start | bytes 5242880 | tf_op jit(solution)/shard_map/all_gather | solution.py:62
  107.4 11.3 %copy-start.6 = (s32[1,64]{1,0:T(1,128)S(1)}, s32[1,64]{1,0:T(1,128)}, u32[]{:S(2)}) copy-start(s32[1,64]{1,0:T(1,128)} %param.14) | copy-start | bytes 772
  107.4 12.6 %copy-start.7 = (s32[1,96]{1,0:T(1,128)S(1)}, s32[1,96]{1,0:T(1,128)}, u32[]{:S(2)}) copy-start(s32[1,96]{1,0:T(1,128)} %param.17) | copy-start | bytes 1156
  107.4 12.7 %copy-start.8 = (s32[1,96]{1,0:T(1,128)S(1)}, s32[1,96]{1,0:T(1,128)}, u32[]{:S(2)}) copy-start(s32[1,96]{1,0:T(1,128)} %param.18) | copy-start | bytes 1156
  107.4 98.2 %all-to-all-start = ((f32[64,128,64]{1,2,0:T(8,128)}), f32[64,128,64]{1,2,0:T(8,128)}, u32[]{:S(2)}, u32[]{:S(2)}) async-start(f32[64,128,64]{1,2,0:T(8,128)} %broadcast_select_fusion), calls=%async_computation | async-start | bytes 4194304 | tf_op jit(solution)/shard_map/all_to_all | solution.py:16
  118.4 84.1 %all-gather.5.cloned.1.call-start = ((), (), s32[]{:S(2)}) async-start(), calls=%async_computation.3 | async-start | bytes 2129920 | tf_op jit(solution)/shard_map/all_gather | solution.py:15
  205.7 1.9 copy-start.2
  239.8 10.1 %copy-start.4 = (s32[1,64,64]{2,1,0:T(8,128)S(1)}, s32[1,64,64]{2,1,0:T(8,128)}, u32[]{:S(2)}) copy-start(s32[1,64,64]{2,1,0:T(8,128)} %param.16) | copy-start | bytes 49156
  239.8 10.2 %copy-start.3 = (f32[256,64]{0,1:T(8,128)S(1)}, f32[256,64]{0,1:T(8,128)}, u32[]{:S(2)}) copy-start(f32[256,64]{0,1:T(8,128)} %param.11) | copy-start | bytes 196612
  239.8 10.2 %copy-start.5 = (f32[64]{0:T(128)S(1)}, f32[64]{0:T(128)}, u32[]{:S(2)}) copy-start(f32[64]{0:T(128)} %param.13) | copy-start | bytes 772
  243.3 34.6 %all-to-all-start.1 = ((f32[64,1,4096]{2,1,0:T(1,128)}), f32[64,1,4096]{2,1,0:T(1,128)S(1)}, u32[]{:S(2)}, u32[]{:S(2)}) async-start(f32[64,1,4096]{2,1,0:T(1,128)} %reshape.216), calls=%async_computation.1 | async-start | bytes 2097152 | tf_op jit(solution)/shard_map/all_to_all | solution.py:38
  277.9 1.0 copy-start.1
Sparse Core Ops, SparseCore 0:
  9.2 54.5 all-gather.2
  122.1 80.4 all-gather.4
where the time goes:
time: 322 us; the launch traced here: 321 us
  waiting for transfers between devices  158 us (49%)
  local copies, waits for them, and re-layouts  55.9 us (17%)
  other arithmetic  45.2 us (14%)
  matrix products  30 us (9%)
  starting transfers between devices  17.9 us (6%)
  between operations  13.6 us (4%)
    all_gather x1, waiting for transfers between devices, spread(): hub_table = lax.all_gather(hub_local, 'dom', axis=0, tiled=True)  82.4 us
    all_gather x1, waiting for transfers between devices, per_device(): portion = lax.all_gather(features, 'feat', axis=1, tiled=True)  55 us
    gather x2, local copies, waits for them, and re-layouts, spread(): outgoing = jnp.take(source, replica_send_rows[0], axis=0)  31.7 us
    scatter-add x1, other arithmetic, aggregate(): summed.at[ret_rows[0].reshape(-1)]  23.4 us
    all_to_all x1, waiting for transfers between devices, aggregate(): lax.all_to_all(buffer.reshape(peer_count, slot_count, columns), 'dom', sp...  20.1 us
    dot_general x1, matrix products, aggregate(): jnp.einsum('tij,tjf->tif', tile_vals[0], picked, precision=lax.Precision....  15.5 us
    dot_general x2, matrix products, project(): jnp.dot(left, right, precision=lax.Precision.HIGHEST, preferred_element_t...  14.4 us
    all_to_all x1, starting transfers between devices, spread(): lax.all_to_all(outgoing, 'dom', split_axis=0, concat_axis=0, tiled=True)  11 us
  transfers between devices with their start and end apart: 4, of which 3 were waited for; matrix products, arithmetic and copies ran while one was open for 4% of the time, Pallas kernels for 0%

commit v1 on v0

v1 whole, which is shorter than its diff:
```python
import functools

import jax
import jax.numpy as jnp
from jax import lax
from jax.experimental import pallas as pl
from jax.experimental.pallas import tpu as pltpu
from jax.sharding import PartitionSpec as P

LANES = 128
HALF = 64


def left_half(shape):
    return lax.broadcasted_iota(jnp.int32, shape, len(shape) - 1) < HALF


def gather_kernel(rows_ref, hubs_ref, xt_ref, out_ref, table_ref, *, peers, rows, hub_rows):
    step = pl.program_id(0)

    @pl.when(step == 0)
    def _():
        width = 512
        for c in range(xt_ref.shape[1] // width):
            part = xt_ref[:, c * width : (c + 1) * width]
            table_ref[c * width : (c + 1) * width, :] = jnp.concatenate([part, part], axis=0).T

    left = left_half((1, LANES))

    def pick(first, second):
        return jnp.where(left, table_ref[pl.ds(first, 1), :], table_ref[pl.ds(second, 1), :])

    def group(g, carry):
        peer = g // (rows // 8)
        row = (g % (rows // 8)) * 8
        base = (step * peers + peer) * 2 * rows + row
        picked = [pick(rows_ref[base + i], rows_ref[base + rows + i]) for i in range(8)]
        out_ref[peer, pl.ds(pl.multiple_of(row, 8), 8), :] = jnp.concatenate(picked, axis=0)
        return carry

    lax.fori_loop(0, peers * rows // 8, group, 0, unroll=2)

    for g in range(hub_rows // 8):
        picked = [pick(hubs_ref[g * 8 + i], hubs_ref[hub_rows + g * 8 + i]) for i in range(8)]
        block = jnp.concatenate(picked, axis=0)
        for peer in range(peers):
            out_ref[peer, rows + g * 8 : rows + g * 8 + 8, :] = block


def gather_rows(xt, send_rows, hub_list):
    peer_count = send_rows.shape[0]
    rows = send_rows.shape[1] // 2
    hub_rows = hub_list.shape[0] // 2
    peers = 8
    return pl.pallas_call(
        functools.partial(gather_kernel, peers=peers, rows=rows, hub_rows=hub_rows),
        grid_spec=pltpu.PrefetchScalarGridSpec(
            num_scalar_prefetch=2,
            grid=(peer_count // peers,),
            in_specs=[pl.BlockSpec(xt.shape, lambda i, *_: (0, 0))],
            out_specs=pl.BlockSpec((peers, rows + hub_rows, LANES), lambda i, *_: (i, 0, 0)),
            scratch_shapes=[pltpu.VMEM((xt.shape[1], LANES), jnp.float32)],
        ),
        out_shape=jax.ShapeDtypeStruct((peer_count, rows + hub_rows, LANES), jnp.float32),
        compiler_params=pltpu.CompilerParams(vmem_limit_bytes=24 * 2**20),
        cost_estimate=pl.CostEstimate(flops=10**7, bytes_accessed=4 * 2**20, transcendentals=0),
    )(send_rows.reshape(-1), hub_list, xt)


def split(value):
    high = value.astype(jnp.bfloat16)
    mid = (value - high.astype(jnp.float32)).astype(jnp.bfloat16)
    return high, mid


def split_kernel(tiles_ref, out_ref):
    for i in range(tiles_ref.shape[0]):
        high, mid = split(tiles_ref[i])
        out_ref[i, :, :LANES] = high
        out_ref[i, :, LANES:] = mid


def split_tiles(tile_vals):
    tiles, size, _ = tile_vals.shape
    step = 8
    return pl.pallas_call(
        split_kernel,
        grid=(tiles // step,),
        in_specs=[pl.BlockSpec((step, size, size), lambda i: (i, 0, 0))],
        out_specs=pl.BlockSpec((step, size, 2 * size), lambda i: (i, 0, 0)),
        out_shape=jax.ShapeDtypeStruct((tiles, size, 2 * size), jnp.bfloat16),
        compiler_params=pltpu.CompilerParams(vmem_limit_bytes=24 * 2**20),
        cost_estimate=pl.CostEstimate(flops=10**7, bytes_accessed=12 * 2**20, transcendentals=0),
    )(tile_vals)


def tile_kernel(src_ref, dst_ref, tiles_ref, mirror_ref, out_ref, acc_ref, *, rows, hub_rows, hub_tiles):
    step = pl.program_id(0)

    @pl.when(step == 0)
    def _():
        acc_ref[...] = jnp.zeros_like(acc_ref)

    count = tiles_ref.shape[0]
    left = left_half((rows, LANES))
    half = rows // 2
    for i in range(count):
        source = src_ref[step * count + i]
        is_hub = source < hub_tiles
        peer = jnp.where(is_hub, 2 * source, source - hub_tiles)
        other = jnp.where(is_hub, 2 * source + 1, source - hub_tiles)
        start = pl.multiple_of(jnp.where(is_hub, rows, 0), 8)
        middle = pl.multiple_of(jnp.where(is_hub, rows, half), 8)
        packed = jnp.concatenate(
            [mirror_ref[peer, pl.ds(start, half), :], mirror_ref[other, pl.ds(middle, half), :]], axis=0
        )
        swapped = pltpu.roll(packed, HALF, 1)
        low = jnp.where(left, packed, swapped)
        high = jnp.where(left, swapped, packed)
        second = jnp.where(is_hub, high[:half], low[half:])
        third = jnp.where(is_hub, low[half:], high[:half])
        block = jnp.concatenate([low[:half], second, third, high[half:]], axis=0)
        top, mid = split(block)
        right_side = jnp.concatenate(
            [jnp.concatenate([top, mid], axis=1), jnp.concatenate([mid, top], axis=1)], axis=0
        )
        product = jnp.dot(tiles_ref[i], right_side, preferred_element_type=jnp.float32)
        acc_ref[dst_ref[step * count + i]] += product[:, :LANES] + product[:, LANES:]

    @pl.when(step == pl.num_programs(0) - 1)
    def _():
        pick = left_half((8, LANES))
        for block in range(acc_ref.shape[0]):
            for part in range(8):
                first = acc_ref[block, part * 16 : part * 16 + 8, :]
                second = acc_ref[block, part * 16 + 8 : part * 16 + 16, :]
                out_ref[block * 8 + part] = jnp.where(pick, first, second)


def tile_stage(split_vals, mirror, tile_src, tile_dst, rows, hub_rows, hub_tiles, dst_blocks):
    tiles, size, _ = split_vals.shape
    step = 8
    return pl.pallas_call(
        functools.partial(tile_kernel, rows=rows, hub_rows=hub_rows, hub_tiles=hub_tiles),
        grid_spec=pltpu.PrefetchScalarGridSpec(
            num_scalar_prefetch=2,
            grid=(tiles // step,),
            in_specs=[
                pl.BlockSpec((step, size, 2 * size), lambda i, *_: (i, 0, 0)),
                pl.BlockSpec(mirror.shape, lambda i, *_: (0, 0, 0)),
            ],
            out_specs=pl.BlockSpec((dst_blocks * 8, 8, LANES), lambda i, *_: (0, 0, 0)),
            scratch_shapes=[pltpu.VMEM((dst_blocks, size, LANES), jnp.float32)],
        ),
        out_shape=jax.ShapeDtypeStruct((dst_blocks * 8, 8, LANES), jnp.float32),
        compiler_params=pltpu.CompilerParams(vmem_limit_bytes=32 * 2**20),
        cost_estimate=pl.CostEstimate(flops=10**9, bytes_accessed=10 * 2**20, transcendentals=0),
    )(tile_src, tile_dst, split_vals, mirror)


def slots_kernel(slots_ref, weights_ref, *out_refs):
    peers = slots_ref.shape[0]
    blocks = slots_ref.shape[1]
    gathered = jnp.concatenate(
        [slots_ref[:, k].reshape(peers * 8, LANES) for k in range(blocks)], axis=1
    )
    for d, out_ref in enumerate(out_refs):
        out_ref[...] = jnp.dot(
            gathered,
            weights_ref[d],
            precision=lax.Precision.HIGHEST,
            preferred_element_type=jnp.float32,
        )


def project_slots(slots, weights):
    peers, blocks = slots.shape[:2]
    return pl.pallas_call(
        slots_kernel,
        out_shape=[jax.ShapeDtypeStruct((peers * 8, LANES), jnp.float32)] * blocks,
        compiler_params=pltpu.CompilerParams(vmem_limit_bytes=24 * 2**20),
        cost_estimate=pl.CostEstimate(flops=10**9, bytes_accessed=3 * 2**20, transcendentals=0),
    )(slots, weights)


def scatter_kernel(rows_ref, *refs, blocks):
    parts = refs[:blocks]
    own_ref, bias_ref, out_ref = refs[blocks : blocks + 3]
    sums = refs[blocks + 3 :]
    for total in sums:
        total[...] = jnp.zeros_like(total)
    left = left_half((1, LANES))
    zero = jnp.zeros((1, LANES), jnp.float32)
    lanes = len(sums) // 2
    for d, part in enumerate(parts):
        count = part.shape[0]

        def add(g, carry, part=part, d=d, count=count):
            for i in range(lanes):
                row = g * lanes + i
                value = part[pl.ds(row, 1), :]
                first = rows_ref[(d * count + row) * 2]
                second = rows_ref[(d * count + row) * 2 + 1]
                sums[2 * i][pl.ds(first, 1), :] += jnp.where(left, value, zero)
                sums[2 * i + 1][pl.ds(second, 1), :] += jnp.where(left, zero, value)
            return carry

        lax.fori_loop(0, count // lanes, add, 0, unroll=8)
    width = 512
    for c in range(out_ref.shape[1] // width):
        columns = slice(c * width, (c + 1) * width)
        whole = functools.reduce(lambda a, b: a + b, [total[columns, :] for total in sums])
        turned = whole.T
        out_ref[:, columns] = jnp.maximum(
            turned[:HALF] + turned[HALF:] + own_ref[:, columns] + bias_ref[...], 0.0
        )


def scatter_rows(parts, rows, own, bias):
    return pl.pallas_call(
        functools.partial(scatter_kernel, blocks=len(parts)),
        in_specs=[pl.BlockSpec(memory_space=pltpu.SMEM)]
        + [pl.BlockSpec(memory_space=pltpu.VMEM)] * (len(parts) + 2),
        out_specs=pl.BlockSpec(memory_space=pltpu.VMEM),
        out_shape=jax.ShapeDtypeStruct(own.shape, jnp.float32),
        scratch_shapes=[pltpu.VMEM((own.shape[1] + 8, LANES), jnp.float32)] * 4,
        compiler_params=pltpu.CompilerParams(vmem_limit_bytes=32 * 2**20),
        cost_estimate=pl.CostEstimate(flops=10**7, bytes_accessed=4 * 2**20, transcendentals=0),
    )(rows, *parts, own, bias)


def shifted(value, count, step):
    return lax.ppermute(value, "feat", [(i, (i + step) % count) for i in range(count)])


def per_device(
    features,
    w_self,
    w_neigh,
    out_bias,
    hub_rows,
    replica_send_rows,
    ret_rows,
    tile_src,
    tile_dst,
    tile_vals,
    *,
    feat,
):
    xt = features.T
    peers, slot = replica_send_rows.shape[1:]
    ret = ret_rows.shape[2]
    outgoing = gather_rows(xt, replica_send_rows[0], hub_rows[0])
    mirror = lax.all_to_all(outgoing, "dom", split_axis=0, concat_axis=0, tiled=True)

    whole = lax.all_gather(xt, "feat", axis=0, tiled=True)
    own = lax.dot_general(
        w_self,
        whole,
        (((0,), (0,)), ((), ())),
        precision=lax.Precision.HIGHEST,
        preferred_element_type=jnp.float32,
    )
    split_vals = split_tiles(tile_vals[0])
    me = lax.axis_index("feat")
    weights = []
    for d in range(feat):
        mine = w_neigh if d == 0 else shifted(w_neigh, feat, -d)
        mine = mine.reshape(feat, HALF, HALF)
        empty = jnp.zeros_like(mine)
        weights.append(
            jnp.stack([jnp.concatenate([mine, empty], 2), jnp.concatenate([empty, mine], 2)], 1).reshape(
                feat * LANES, LANES
            )
        )
    weights = jnp.stack(weights)
    quarters = ret_rows[0].reshape(peers, feat, 2, 8).transpose(1, 0, 3, 2)
    order = jnp.stack(
        [lax.dynamic_index_in_dim(quarters, (me - d) % feat, 0, False) for d in range(feat)]
    ).reshape(-1)

    hub_tiles = hub_rows.shape[1] * peers // slot
    partial = tile_stage(
        split_vals,
        mirror,
        tile_src[0],
        tile_dst[0],
        slot // 2,
        hub_rows.shape[1] // 2,
        hub_tiles,
        peers * ret // slot,
    )
    slots = lax.all_to_all(partial, ("dom", "feat"), split_axis=0, concat_axis=0, tiled=True)
    parts = project_slots(slots.reshape(peers, feat, 8, LANES), weights)
    parts = [parts[0]] + [shifted(parts[d], feat, d) for d in range(1, feat)]
    return scatter_rows(parts, order, own, out_bias[:, None]).T


def solution(mesh):
    return jax.shard_map(
        functools.partial(per_device, feat=mesh.shape["feat"]),
        mesh=mesh,
        in_specs=(
            P("dom", "feat"),
            P(None, "feat"),
            P(None, "feat"),
            P("feat"),
            P("dom", None),
            P("dom", None, None),
            P("dom", None, None),
            P("dom", None),
            P("dom", None),
            P("dom", None, None, None),
        ),
        out_specs=P("dom", "feat"),
        check_vma=False,
    )
```

time: 322 us -> 194 us (0.60)
  waiting for transfers between devices: 158 us -> 97.2 us
  other arithmetic: 45.2 us -> 0.16 us
  local copies, waits for them, and re-layouts: 55.9 us -> 13.7 us
  Pallas kernels: 0 us -> 34.2 us
  matrix products: 30 us -> 4.8 us
  starting transfers between devices: 17.9 us -> 30.3 us
    all_gather x2 -> x1, waiting for transfers between devices: 137 us -> 0.01 us  [per_device(): whole = lax.all_gather(xt, 'feat', axis=0, tiled=True)]
    all_to_all x2, waiting for transfers between devices: 20.1 us -> 83.7 us  [the longest x1 65.2 us: per_device(): lax.all_to_all(outgoing, 'dom', split_axis=0, concat_axis=0, tiled=True)]
    gather x4 -> x0, local copies, waits for them, and re-layouts: 34.7 us -> none  [the longest x2 31.7 us: spread(): outgoing = jnp.take(source, replica_send_rows[0], axis=0)]
    pallas_call x0 -> x5, Pallas kernels: none -> 34.2 us  [the longest x1 14.6 us: gather_rows(): pl.pallas_call(functools.partial(gather_kernel, peers=peers, rows=rows, h...]
    scatter-add x2 -> x0, other arithmetic: 33.7 us -> none  [the longest x1 23.4 us: aggregate(): summed.at[ret_rows[0].reshape(-1)]]
    dot_general x3 -> x1, matrix products: 30 us -> 4.8 us  [per_device(): lax.dot_general(w_self, whole, (((0,), (0,)), ((), ())), precision=lax.Pr...]
    ppermute x0 -> x6, waiting for transfers between devices: none -> 12.9 us  [shifted(): lax.ppermute(value, 'feat', [(i, (i + step) % count) for i in range(count)])]
    ppermute x0 -> x6, starting transfers between devices: none -> 8 us  [shifted(): lax.ppermute(value, 'feat', [(i, (i + step) % count) for i in range(count)])]
  transfers between devices with their start and end apart: 4 -> 9, of which waited for: 3 -> 6; matrix products, arithmetic and copies ran while one was open for 4% -> 4% of each run, Pallas kernels for 0% -> 5%
where the time goes in v1:
time: 194 us
  waiting for transfers between devices  97.2 us (50%)
  Pallas kernels  34.2 us (18%)
  starting transfers between devices  30.3 us (16%)
  local copies, waits for them, and re-layouts  13.7 us (7%)
  between operations  13.6 us (7%)
  matrix products  4.8 us (2%)
    all_to_all x1, waiting for transfers between devices, per_device(): lax.all_to_all(outgoing, 'dom', split_axis=0, concat_axis=0, tiled=True)  65.2 us
    all_to_all x1, waiting for transfers between devices, per_device(): lax.all_to_all(partial, ('dom', 'feat'), split_axis=0, concat_axis=0, til...  18.5 us
    pallas_call x1, Pallas kernels, gather_rows(): pl.pallas_call(functools.partial(gather_kernel, peers=peers, rows=rows, h...  14.6 us
    all_to_all x1, starting transfers between devices, per_device(): lax.all_to_all(outgoing, 'dom', split_axis=0, concat_axis=0, tiled=True)  13.2 us
    ppermute x6, waiting for transfers between devices, shifted(): lax.ppermute(value, 'feat', [(i, (i + step) % count) for i in range(count)])  12.9 us
    unnamed x27, local copies, waits for them, and re-layouts  11.9 us
    pallas_call x1, Pallas kernels, scatter_rows(): pl.pallas_call(functools.partial(scatter_kernel, blocks=len(parts)), in_s...  9.17 us
    all_to_all x1, starting transfers between devices, per_device(): lax.all_to_all(partial, ('dom', 'feat'), split_axis=0, concat_axis=0, til...  9.12 us
  transfers between devices with their start and end apart: 9, of which 6 were waited for; matrix products, arithmetic and copies ran while one was open for 4% of the time, Pallas kernels for 5%

profile of v1, /device:TPU:1, one launch (start us, length us, event | category | flops | bytes accessed | tf_op | source)
XLA Modules:
  0.0 193.9 jit_solution(2571341096088222766)
XLA Ops:
  6.5 1.3 copy-done.4
  7.8 0.8 copy-done.6
  8.6 0.7 copy-done.7
  9.2 14.6 %shard_map.101 = f32[64,96,128]{2,1,0:T(8,128)} custom-call(s32[8192]{0:T(1024)S(1)} %bitcast.50, s32[64]{0:T(128)S(1)} %bitcast.51, f32[64,4096]{1,0:T(8,128)S(1)} %bitcast.48), custom_call_target="tpu_custom_call" | custom-call | flops 10000000 | bytes 4194304 | tf_op jit(solution)/shard_map/pallas_call | solution.py:55
  23.9 13.2 %all-to-all-start = ((f32[64,96,128]{2,1,0:T(8,128)}), f32[64,96,128]{2,1,0:T(8,128)S(1)}, u32[]{:S(2)}, u32[]{:S(2)}) async-start(f32[64,96,128]{2,1,0:T(8,128)} %shard_map.101), calls=%async_computation | async-start | bytes 6291456 | tf_op jit(solution)/shard_map/all_to_all | solution.py:254
  37.0 0.0 all-gather.2.cloned.1.call-start
  37.1 0.7 all-gather.2.cloned.1.call-update
  37.8 0.0 copy-start.3
  37.8 2.8 %copy-done.3 = f32[1,96,128,128]{3,2,1,0:T(8,128)S(1)} copy-done((f32[1,96,128,128]{3,2,1,0:T(8,128)S(1)}, f32[1,96,128,128]{3,2,1,0:T(8,128)}, u32[]{:S(2)}) %copy-start.3) | copy-done | bytes 6291480
  40.5 1.2 shard_map.100.tiles_ref
  41.7 2.6 %copy-done.1 = bf16[96,128,256]{2,1,0:T(8,128)(2,1)} copy-done((bf16[96,128,256]{2,1,0:T(8,128)(2,1)}, bf16[96,128,256]{2,1,0:T(8,128)(2,1)S(1)}, u32[]{:S(2)}) %copy-start.1) | copy-done | bytes 6291480
  44.4 65.2 %all-to-all-done.mirror_ref = f32[64,96,128]{2,1,0:T(8,128)S(1)} async-done(((f32[64,96,128]{2,1,0:T(8,128)}), f32[64,96,128]{2,1,0:T(8,128)S(1)}, u32[]{:S(2)}, u32[]{:S(2)}) %all-to-all-start) | async-done | bytes 3145760 | tf_op jit(solution)/shard_map/all_to_all | solution.py:254
  109.6 0.0 copy-done.9
  109.6 2.8 %copy-done.2 = bf16[96,128,256]{2,1,0:T(8,128)(2,1)S(1)} copy-done((bf16[96,128,256]{2,1,0:T(8,128)(2,1)S(1)}, bf16[96,128,256]{2,1,0:T(8,128)(2,1)}, u32[]{:S(2)}) %copy-start.2) | copy-done | bytes 6291480
  112.4 5.8 %shard_map.102 = f32[256,8,128]{2,1,0:T(8,128)S(1)} custom-call(s32[96]{0:T(128)S(1)} %bitcast.52, s32[96]{0:T(128)S(1)} %bitcast.53, bf16[96,128,256]{2,1,0:T(8,128)(2,1)S(1)} %copy-done.2, f32[64,96,128]{2,1,0:T(8,128)S(1)} %all-to-all-done.mirror_ref), custom_call_target="tpu_custom_call" | custom-call | flops 1000000000 | bytes 10485760 | tf_op jit(solution)/shard_map/pallas_call | solution.py:143
  118.1 0.0 copy-start.5
  118.1 1.0 copy-done.5
  119.1 9.1 %all-to-all-start.1 = ((f32[256,8,128]{2,1,0:T(8,128)}), f32[256,8,128]{2,1,0:T(8,128)S(1)}, u32[]{:S(2)}, u32[]{:S(2)}) async-start(f32[256,8,128]{2,1,0:T(8,128)} %copy-done.5), calls=%async_computation.1 | async-start | bytes 2097152 | tf_op jit(solution)/shard_map/all_to_all | solution.py:293
  128.2 2.7 %collective-permute-start = (f32[256,64]{0,1:T(8,128)S(1)}, f32[256,64]{0,1:T(8,128)S(1)}, u32[]{:S(2)}, u32[]{:S(2)}) collective-permute-start(f32[256,64]{0,1:T(8,128)S(1)} %copy-done.10), channel_id=1, source_target_pairs={{0,3},{1,0},{2,1},{3,2},{4,7},{5,4},{6,5},{7,6},{8,11},{9,8},{10,9... | collective-permute-start | bytes 196616 | tf_op jit(solution)/shard_map/ppermute | solution.py:233
  130.9 0.6 collective-permute-start.1
  131.5 0.6 collective-permute-start.2
  132.1 0.1 copy.31
  132.2 0.1 copy.20
  132.3 0.4 copy.21
  132.7 0.5 reshape.18.rows_ref
  133.2 0.1 copy.30.refs_5_
  133.3 0.1 pad_bitcast_fusion.7
  133.4 0.0 collective-permute-done
  133.4 0.1 copy.32
  133.5 3.2 %collective-permute-done.1 = f32[256,64]{0,1:T(8,128)S(1)} collective-permute-done((f32[256,64]{0,1:T(8,128)S(1)}, f32[256,64]{0,1:T(8,128)S(1)}, u32[]{:S(2)}, u32[]{:S(2)}) %collective-permute-start.1) | collective-permute-done | bytes 65568 | tf_op jit(solution)/shard_map/ppermute | solution.py:233
  136.7 0.1 copy.33
  136.8 3.3 %collective-permute-done.2 = f32[256,64]{0,1:T(8,128)S(1)} collective-permute-done((f32[256,64]{0,1:T(8,128)S(1)}, f32[256,64]{0,1:T(8,128)S(1)}, u32[]{:S(2)}, u32[]{:S(2)}) %collective-permute-start.2) | collective-permute-done | bytes 65568 | tf_op jit(solution)/shard_map/ppermute | solution.py:233
  140.1 0.1 copy.34
  140.2 0.1 pad_bitcast_fusion.5
  140.3 0.1 pad_bitcast_fusion.3
  140.5 0.1 pad_bitcast_fusion.1
  140.6 0.1 pad_maximum_fusion.weights_ref
  140.7 18.5 %all-to-all-done.1 = f32[256,8,128]{2,1,0:T(8,128)S(1)} async-done(((f32[256,8,128]{2,1,0:T(8,128)}), f32[256,8,128]{2,1,0:T(8,128)S(1)}, u32[]{:S(2)}, u32[]{:S(2)}) %all-to-all-start.1) | async-done | bytes 1048608 | tf_op jit(solution)/shard_map/all_to_all | solution.py:293
  159.2 3.4 %shard_map.103 = (f32[512,128]{1,0:T(8,128)S(1)}, f32[512,128]{1,0:T(8,128)S(1)}, f32[512,128]{1,0:T(8,128)S(1)}, f32[512,128]{1,0:T(8,128)S(1)}) custom-call(f32[64,4,8,128]{3,2,1,0:T(8,128)S(1)} %bitcast.49, f32[4,512,128]{2,1,0:T(8,128)S(1)} %pad_maximum_fusion.weights_ref), custom_call_target="tpu_custom_call" | custom-call | flops 1000000000 | bytes 3145728 | tf_op jit(solution)/shard_map/pallas_call | solution.py:178
  162.6 0.6 collective-permute-start.3
  163.2 2.4 %collective-permute-start.4 = (f32[512,128]{1,0:T(8,128)S(1)}, f32[512,128]{1,0:T(8,128)S(1)}, u32[]{:S(2)}, u32[]{:S(2)}) collective-permute-start(f32[512,128]{1,0:T(8,128)S(1)} %get-tuple-element.11), channel_id=1, source_target_pairs={{0,2},{1,3},{2,0},{3,1},{4,6},{5,7},{6,4},{7,5},{8,10},{9,11},{10,... | collective-permute-start | bytes 786440 | tf_op jit(solution)/shard_map/ppermute | solution.py:233
  165.6 1.2 collective-permute-start.5
  166.8 0.0 copy-done
  166.8 4.8 %fusion.refs_4_ = f32[64,4096]{1,0:T(8,128)S(1)} fusion(f32[256,64]{0,1:T(8,128)S(1)} %copy-done, f32[256,4096]{1,0:T(8,128)} %all-gather.2.cloned.1.call-done), kind=kOutput, calls=%fused_computation.18 | convolution fusion | flops 805306368 | bytes 5308416 | tf_op jit(solution)/shard_map/dot_general | solution.py:257
  171.6 0.3 collective-permute-done.3.refs_1_
  171.9 6.0 %collective-permute-done.4.refs_2_ = f32[512,128]{1,0:T(8,128)S(1)} collective-permute-done((f32[512,128]{1,0:T(8,128)S(1)}, f32[512,128]{1,0:T(8,128)S(1)}, u32[]{:S(2)}, u32[]{:S(2)}) %collective-permute-start.4) | collective-permute-done | bytes 262176 | tf_op jit(solution)/shard_map/ppermute | solution.py:233
  177.9 0.0 collective-permute-done.5.refs_3_
  177.9 9.2 %shard_map.104 = f32[64,4096]{1,0:T(8,128)} custom-call(s32[4096]{0:T(1024)S(1)} %reshape.18.rows_ref, f32[512,128]{1,0:T(8,128)S(1)} %get-tuple-element.9.refs_0_, f32[512,128]{1,0:T(8,128)S(1)} %collective-permute-done.3.refs_1_, f32[512,128]{1,0:T(8,128)S(1)} %collective-permute-done.4.refs_2_, f32[512,128]{1,0:T(8,128)S(1)} %collective-permute-done.5.refs_3_, ...), custom_call_target="tpu_custom_call" | custom-call | flops 10000000 | bytes 4194304 | tf_op jit(solution)/shard_map/pallas_call | solution.py:220
  (22 shorter events, 0.1 us)
Async XLA Ops:
  6.5 160.2 %copy-start = (f32[256,64]{0,1:T(8,128)S(1)}, f32[256,64]{0,1:T(8,128)}, u32[]{:S(2)}) copy-start(f32[256,64]{0,1:T(8,128)} %param.11) | copy-start | bytes 196612
  6.5 1.3 copy-start.4
  7.8 0.8 copy-start.6
  8.6 0.7 copy-start.7
  23.9 85.7 %all-to-all-start = ((f32[64,96,128]{2,1,0:T(8,128)}), f32[64,96,128]{2,1,0:T(8,128)S(1)}, u32[]{:S(2)}, u32[]{:S(2)}) async-start(f32[64,96,128]{2,1,0:T(8,128)} %shard_map.101), calls=%async_computation | async-start | bytes 6291456 | tf_op jit(solution)/shard_map/all_to_all | solution.py:254
  37.0 129.8 %all-gather.2.cloned.1.call-start = ((), (), s32[]{:S(2)}) async-start(), calls=%async_computation.2 | async-start | bytes 5242880 | tf_op jit(solution)/shard_map/all_gather | solution.py:256
  37.8 2.8 %copy-start.3 = (f32[1,96,128,128]{3,2,1,0:T(8,128)S(1)}, f32[1,96,128,128]{3,2,1,0:T(8,128)}, u32[]{:S(2)}) copy-start(f32[1,96,128,128]{3,2,1,0:T(8,128)} %param.19) | copy-start | bytes 18874372
  40.5 69.0 %copy-start.8 = (s32[1,96]{1,0:T(1,128)S(1)}, s32[1,96]{1,0:T(1,128)}, u32[]{:S(2)}) copy-start(s32[1,96]{1,0:T(1,128)} %param.17) | copy-start | bytes 1156
  40.5 69.0 %copy-start.9 = (s32[1,96]{1,0:T(1,128)S(1)}, s32[1,96]{1,0:T(1,128)}, u32[]{:S(2)}) copy-start(s32[1,96]{1,0:T(1,128)} %param.18) | copy-start | bytes 1156
  41.7 2.6 %copy-start.1 = (bf16[96,128,256]{2,1,0:T(8,128)(2,1)}, bf16[96,128,256]{2,1,0:T(8,128)(2,1)S(1)}, u32[]{:S(2)}) copy-start(bf16[96,128,256]{2,1,0:T(8,128)(2,1)S(1)} %shard_map.100.tiles_ref) | copy-start | bytes 18874372
  109.6 2.8 %copy-start.2 = (bf16[96,128,256]{2,1,0:T(8,128)(2,1)S(1)}, bf16[96,128,256]{2,1,0:T(8,128)(2,1)}, u32[]{:S(2)}) copy-start(bf16[96,128,256]{2,1,0:T(8,128)(2,1)} %copy-done.1) | copy-start | bytes 18874372
  112.4 15.9 %copy-start.10 = (f32[256,64]{0,1:T(8,128)S(1)}, f32[256,64]{0,1:T(8,128)}, u32[]{:S(2)}) copy-start(f32[256,64]{0,1:T(8,128)} %param.12) | copy-start | bytes 196612
  112.4 19.8 %copy-start.11 = (s32[1,64,64]{2,1,0:T(8,128)S(1)}, s32[1,64,64]{2,1,0:T(8,128)}, u32[]{:S(2)}) copy-start(s32[1,64,64]{2,1,0:T(8,128)} %param.16) | copy-start | bytes 49156
  118.1 1.0 copy-start.5
  119.1 14.1 %copy-start.12 = (f32[64]{0:T(128)S(1)}, f32[64]{0:T(128)}, u32[]{:S(2)}) copy-start(f32[64]{0:T(128)} %param.13) | copy-start | bytes 772
  119.1 40.1 %all-to-all-start.1 = ((f32[256,8,128]{2,1,0:T(8,128)}), f32[256,8,128]{2,1,0:T(8,128)S(1)}, u32[]{:S(2)}, u32[]{:S(2)}) async-start(f32[256,8,128]{2,1,0:T(8,128)} %copy-done.5), calls=%async_computation.1 | async-start | bytes 2097152 | tf_op jit(solution)/shard_map/all_to_all | solution.py:293
  128.2 5.2 %collective-permute-start = (f32[256,64]{0,1:T(8,128)S(1)}, f32[256,64]{0,1:T(8,128)S(1)}, u32[]{:S(2)}, u32[]{:S(2)}) collective-permute-start(f32[256,64]{0,1:T(8,128)S(1)} %copy-done.10), channel_id=1, source_target_pairs={{0,3},{1,0},{2,1},{3,2},{4,7},{5,4},{6,5},{7,6},{8,11},{9,8},{10,9... | collective-permute-start | bytes 196616 | tf_op jit(solution)/shard_map/ppermute | solution.py:233
  130.9 5.8 %collective-permute-start.1 = (f32[256,64]{0,1:T(8,128)S(1)}, f32[256,64]{0,1:T(8,128)S(1)}, u32[]{:S(2)}, u32[]{:S(2)}) collective-permute-start(f32[256,64]{0,1:T(8,128)S(1)} %copy-done.10), channel_id=1, source_target_pairs={{0,2},{1,3},{2,0},{3,1},{4,6},{5,7},{6,4},{7,5},{8,10},{9,11},{10,... | collective-permute-start | bytes 196616 | tf_op jit(solution)/shard_map/ppermute | solution.py:233
  131.5 8.7 %collective-permute-start.2 = (f32[256,64]{0,1:T(8,128)S(1)}, f32[256,64]{0,1:T(8,128)S(1)}, u32[]{:S(2)}, u32[]{:S(2)}) collective-permute-start(f32[256,64]{0,1:T(8,128)S(1)} %copy-done.10), channel_id=1, source_target_pairs={{0,1},{1,2},{2,3},{3,0},{4,5},{5,6},{6,7},{7,4},{8,9},{9,10},{10,1... | collective-permute-start | bytes 196616 | tf_op jit(solution)/shard_map/ppermute | solution.py:233
  162.6 9.3 %collective-permute-start.3 = (f32[512,128]{1,0:T(8,128)S(1)}, f32[512,128]{1,0:T(8,128)S(1)}, u32[]{:S(2)}, u32[]{:S(2)}) collective-permute-start(f32[512,128]{1,0:T(8,128)S(1)} %get-tuple-element.10), channel_id=1, source_target_pairs={{0,1},{1,2},{2,3},{3,0},{4,5},{5,6},{6,7},{7,4},{8,9},{9,10},{10,1... | collective-permute-start | bytes 786440 | tf_op jit(solution)/shard_map/ppermute | solution.py:233
  163.2 14.7 %collective-permute-start.4 = (f32[512,128]{1,0:T(8,128)S(1)}, f32[512,128]{1,0:T(8,128)S(1)}, u32[]{:S(2)}, u32[]{:S(2)}) collective-permute-start(f32[512,128]{1,0:T(8,128)S(1)} %get-tuple-element.11), channel_id=1, source_target_pairs={{0,2},{1,3},{2,0},{3,1},{4,6},{5,7},{6,4},{7,5},{8,10},{9,11},{10,... | collective-permute-start | bytes 786440 | tf_op jit(solution)/shard_map/ppermute | solution.py:233
  165.6 12.3 %collective-permute-start.5 = (f32[512,128]{1,0:T(8,128)S(1)}, f32[512,128]{1,0:T(8,128)S(1)}, u32[]{:S(2)}, u32[]{:S(2)}) collective-permute-start(f32[512,128]{1,0:T(8,128)S(1)} %get-tuple-element.12), channel_id=1, source_target_pairs={{0,3},{1,0},{2,1},{3,2},{4,7},{5,4},{6,5},{7,6},{8,11},{9,8},{10,9... | collective-permute-start | bytes 786440 | tf_op jit(solution)/shard_map/ppermute | solution.py:233
Sparse Core Ops, SparseCore 0:
  39.7 51.7 all-gather.1

commit v2 on v1

v2 whole, which is shorter than its diff:
```python
import functools

import jax
import jax.numpy as jnp
from jax import lax
from jax.experimental import pallas as pl
from jax.experimental.pallas import tpu as pltpu
from jax.sharding import PartitionSpec as P

LANES = 128
KERNEL_VMEM = 50 * 2**20
HALF = 64


def left_half(shape):
    return lax.broadcasted_iota(jnp.int32, shape, len(shape) - 1) < HALF


def gather_kernel(rows_ref, hubs_ref, xt_hbm, out_ref, xt_ref, table_ref, hub_ref, sems, *, peers, rows, hub_rows):
    step = pl.program_id(0)
    chunks = sems.shape[0]
    width = xt_ref.shape[1] // chunks

    def fetch(c):
        columns = pl.ds(c * width, width)
        return pltpu.make_async_copy(xt_hbm.at[:, columns], xt_ref.at[:, columns], sems.at[c])

    @pl.when(step == 0)
    def _():
        for c in range(chunks):
            fetch(c).start()
        for c in range(chunks):
            fetch(c).wait()
            part = xt_ref[:, c * width : (c + 1) * width]
            table_ref[c * width : (c + 1) * width, :] = jnp.concatenate([part, part], axis=0).T

    left = left_half((1, LANES))

    def pick(first, second):
        return jnp.where(left, table_ref[pl.ds(first, 1), :], table_ref[pl.ds(second, 1), :])

    @pl.when(step == 0)
    def _():
        for half in range(2):
            start = half * 2 * hub_rows
            for i in range(hub_rows):
                hub_ref[half, i : i + 1, :] = pick(hubs_ref[start + i], hubs_ref[start + hub_rows + i])

    def one(peer, carry):
        base = (step * peers + peer) * 2 * rows
        for i in range(rows):
            out_ref[peer, i : i + 1, :] = pick(rows_ref[base + i], rows_ref[base + rows + i])
        out_ref[peer, rows : rows + hub_rows, :] = hub_ref[peer % 2]
        return carry

    lax.fori_loop(0, peers, one, 0)


def gather_rows(xt, send_rows, hub_list):
    peer_count = send_rows.shape[0]
    rows = send_rows.shape[1] // 2
    hub_rows = hub_list.shape[0] // 4
    peers = 8
    return pl.pallas_call(
        functools.partial(gather_kernel, peers=peers, rows=rows, hub_rows=hub_rows),
        grid_spec=pltpu.PrefetchScalarGridSpec(
            num_scalar_prefetch=2,
            grid=(peer_count // peers,),
            in_specs=[pl.BlockSpec(memory_space=pltpu.HBM)],
            out_specs=pl.BlockSpec((peers, rows + hub_rows, LANES), lambda i, *_: (i, 0, 0)),
            scratch_shapes=[
                pltpu.VMEM(xt.shape, jnp.float32),
                pltpu.VMEM((xt.shape[1], LANES), jnp.float32),
                pltpu.VMEM((2, hub_rows, LANES), jnp.float32),
                pltpu.SemaphoreType.DMA((8,)),
            ],
        ),
        out_shape=jax.ShapeDtypeStruct((peer_count, rows + hub_rows, LANES), jnp.float32),
        compiler_params=pltpu.CompilerParams(vmem_limit_bytes=60 * 2**20),
        cost_estimate=pl.CostEstimate(flops=10**7, bytes_accessed=4 * 2**20, transcendentals=0),
    )(send_rows.reshape(-1), hub_list, xt)


def split(value):
    high = value.astype(jnp.bfloat16)
    mid = (value - high.astype(jnp.float32)).astype(jnp.bfloat16)
    return high, mid


def split_kernel(src_ref, dst_ref, tiles_ref, out_ref, order_ref):
    count = tiles_ref.shape[0]
    for i in range(count):
        tile = pl.program_id(0) * count + i
        source = src_ref[tile]
        high, mid = split(tiles_ref[i])
        out_ref[source, :, :LANES] = high
        out_ref[source, :, LANES:] = mid
        order_ref[source] = dst_ref[tile]


def split_tiles(tile_vals, tile_src, tile_dst):
    tiles, size, _ = tile_vals.shape
    step = 8
    return pl.pallas_call(
        split_kernel,
        grid_spec=pltpu.PrefetchScalarGridSpec(
            num_scalar_prefetch=2,
            grid=(tiles // step,),
            in_specs=[pl.BlockSpec((step, size, size), lambda i, *_: (i, 0, 0))],
            out_specs=[
                pl.BlockSpec((tiles, size, 2 * size), lambda i, *_: (0, 0, 0)),
                pl.BlockSpec(memory_space=pltpu.SMEM),
            ],
        ),
        out_shape=[
            jax.ShapeDtypeStruct((tiles, size, 2 * size), jnp.bfloat16),
            jax.ShapeDtypeStruct((tiles,), jnp.int32),
        ],
        compiler_params=pltpu.CompilerParams(vmem_limit_bytes=40 * 2**20),
        cost_estimate=pl.CostEstimate(flops=10**7, bytes_accessed=12 * 2**20, transcendentals=0),
    )(tile_src, tile_dst, tile_vals)


def unpack(packed):
    left = left_half(packed.shape)
    swapped = pltpu.roll(packed, HALF, 1)
    return jnp.where(left, packed, swapped), jnp.where(left, swapped, packed)


def multiply(tile, block):
    top, mid = split(block)
    right_side = jnp.concatenate(
        [jnp.concatenate([top, mid], axis=1), jnp.concatenate([mid, top], axis=1)], axis=0
    )
    product = jnp.dot(tile, right_side, preferred_element_type=jnp.float32)
    return product[:, :LANES] + product[:, LANES:]


def packed_sums(acc_ref, block, part):
    first = acc_ref[block, part * 16 : part * 16 + 8, :]
    second = acc_ref[block, part * 16 + 8 : part * 16 + 16, :]
    return jnp.where(left_half((8, LANES)), first, second)


def listed_kernel(dst_ref, tiles_hbm, mirror_ref, out_ref, tiles_ref, acc_ref, sems, *, first, rows):
    chunks = sems.shape[0]
    count = tiles_ref.shape[0] // chunks

    def fetch(c):
        return pltpu.make_async_copy(
            tiles_hbm.at[pl.ds(first + c * count, count)], tiles_ref.at[pl.ds(c * count, count)], sems.at[c]
        )

    for c in range(chunks):
        fetch(c).start()
    acc_ref[...] = jnp.zeros_like(acc_ref)

    def chunk(c, carry):
        fetch(c).wait()
        for i in range(count):
            tile = c * count + i
            low, high = unpack(mirror_ref[tile, :rows, :])
            acc_ref[dst_ref[first + tile]] += multiply(tiles_ref[tile], jnp.concatenate([low, high], axis=0))
        return carry

    lax.fori_loop(0, chunks, chunk, 0)
    for block in range(acc_ref.shape[0]):
        for part in range(8):
            out_ref[block * 8 + part] = packed_sums(acc_ref, block, part)


def listed_tiles(split_vals, mirror, order, rows, first, dst_blocks):
    tiles, size, _ = split_vals.shape
    count = tiles - first
    whole = pl.BlockSpec(memory_space=pltpu.VMEM)
    return pl.pallas_call(
        functools.partial(listed_kernel, first=first, rows=rows),
        in_specs=[pl.BlockSpec(memory_space=pltpu.SMEM), pl.BlockSpec(memory_space=pltpu.HBM), whole],
        out_specs=whole,
        scratch_shapes=[
            pltpu.VMEM((count, size, 2 * size), jnp.bfloat16),
            pltpu.VMEM((dst_blocks, size, LANES), jnp.float32),
            pltpu.SemaphoreType.DMA((8,)),
        ],
        out_shape=jax.ShapeDtypeStruct((dst_blocks * 8, 8, LANES), jnp.float32),
        compiler_params=pltpu.CompilerParams(vmem_limit_bytes=KERNEL_VMEM),
        cost_estimate=pl.CostEstimate(flops=10**9, bytes_accessed=10 * 2**20, transcendentals=0),
    )(order, split_vals, mirror)


def hub_kernel(
    dst_ref, side_ref, tiles_hbm, own_ref, other_ref, before_ref, out_hbm, tiles_ref, hubs_ref, acc_ref, out_ref, sems, out_sems
):
    chunks = sems.shape[0]
    count = tiles_ref.shape[0] // chunks
    side = side_ref[0]

    def fetch(c):
        part = pl.ds(c * count, count)
        return pltpu.make_async_copy(tiles_hbm.at[part], tiles_ref.at[part], sems.at[c])

    for c in range(chunks):
        fetch(c).start()
    acc_ref[...] = jnp.zeros_like(acc_ref)
    hubs_ref[side] = own_ref[...]
    hubs_ref[1 - side] = other_ref[...]

    def chunk(c, carry):
        fetch(c).wait()
        for i in range(count):
            tile = c * count + i
            pieces = []
            for part in range(2):
                for half in range(2):
                    pieces.extend(unpack(hubs_ref[half, 2 * tile + part]))
            acc_ref[dst_ref[tile]] += multiply(tiles_ref[tile], jnp.concatenate(pieces, axis=0))
        return carry

    lax.fori_loop(0, chunks, chunk, 0)
    sends = out_sems.shape[0]
    blocks = acc_ref.shape[0] // sends
    results = []
    for c in range(sends):
        for block in range(c * blocks, (c + 1) * blocks):
            for part in range(8):
                out_ref[block * 8 + part] = packed_sums(acc_ref, block, part) + before_ref[block * 8 + part]
        span = pl.ds(c * blocks * 8, blocks * 8)
        results.append(pltpu.make_async_copy(out_ref.at[span], out_hbm.at[span], out_sems.at[c]))
        results[-1].start()
    for copy in results:
        copy.wait()


def hub_tiles(split_vals, own, other, before, order, side):
    _, size, _ = split_vals.shape
    blocks = before.shape[0] // 8
    scalars = pl.BlockSpec(memory_space=pltpu.SMEM)
    return pl.pallas_call(
        hub_kernel,
        in_specs=[scalars, scalars, pl.BlockSpec(memory_space=pltpu.HBM)]
        + [pl.BlockSpec(memory_space=pltpu.VMEM)] * 3,
        out_specs=pl.BlockSpec(memory_space=pltpu.HBM),
        scratch_shapes=[
            pltpu.VMEM((own.shape[0] // 2, size, 2 * size), jnp.bfloat16),
            pltpu.VMEM((2,) + own.shape, jnp.float32),
            pltpu.VMEM((blocks, size, LANES), jnp.float32),
            pltpu.VMEM(before.shape, jnp.float32),
            pltpu.SemaphoreType.DMA((4,)),
            pltpu.SemaphoreType.DMA((4,)),
        ],
        out_shape=jax.ShapeDtypeStruct(before.shape, jnp.float32),
        compiler_params=pltpu.CompilerParams(vmem_limit_bytes=KERNEL_VMEM),
        cost_estimate=pl.CostEstimate(flops=10**9, bytes_accessed=6 * 2**20, transcendentals=0),
    )(order, side, split_vals, own, other, before)


def weights_kernel(weights_ref, out_ref):
    for d in range(weights_ref.shape[0]):
        top, mid = split(weights_ref[d])
        depth = top.shape[0]
        out_ref[d, :depth, :LANES] = top
        out_ref[d, :depth, LANES:] = mid
        out_ref[d, depth:, :LANES] = mid
        out_ref[d, depth:, LANES:] = top


def split_weights(weights):
    count, depth, width = weights.shape
    return pl.pallas_call(
        weights_kernel,
        out_shape=jax.ShapeDtypeStruct((count, 2 * depth, 2 * width), jnp.bfloat16),
    )(weights)


def slots_kernel(slots_ref, weights_ref, *out_refs, targets):
    peers = slots_ref.shape[0]
    blocks = slots_ref.shape[1]
    tops, mids = [], []
    for k in range(blocks):
        top, mid = split(slots_ref[:, k].reshape(peers * 8, LANES))
        tops.append(top)
        mids.append(mid)
    whole = jnp.concatenate(tops + mids, axis=1)
    for d, out_ref in zip(targets, out_refs):
        product = jnp.dot(whole, weights_ref[d], preferred_element_type=jnp.float32)
        out_ref[...] = product[:, :LANES] + product[:, LANES:]


def project_slots(slots, weights, targets):
    peers = slots.shape[0]
    return pl.pallas_call(
        functools.partial(slots_kernel, targets=targets),
        out_shape=[jax.ShapeDtypeStruct((peers * 8, LANES), jnp.float32)] * len(targets),
        compiler_params=pltpu.CompilerParams(vmem_limit_bytes=24 * 2**20),
        cost_estimate=pl.CostEstimate(flops=10**7, bytes_accessed=16 * 2**20, transcendentals=0),
    )(slots, weights)


def scatter_kernel(rows_ref, *refs, blocks, last):
    parts = refs[:blocks]
    base_ref, bias_ref, out_ref = refs[blocks : blocks + 3]
    sums = refs[blocks + 3 :]
    for total in sums:
        total[...] = jnp.zeros_like(total)
    left = left_half((1, LANES))
    zero = jnp.zeros((1, LANES), jnp.float32)
    lanes = len(sums) // 2
    for d, part in enumerate(parts):
        count = part.shape[0]

        def add(g, carry, part=part, d=d, count=count):
            for i in range(lanes):
                row = g * lanes + i
                value = part[pl.ds(row, 1), :]
                first = rows_ref[(d * count + row) * 2]
                second = rows_ref[(d * count + row) * 2 + 1]
                sums[2 * i][pl.ds(first, 1), :] += jnp.where(left, value, zero)
                sums[2 * i + 1][pl.ds(second, 1), :] += jnp.where(left, zero, value)
            return carry

        lax.fori_loop(0, count // lanes, add, 0, unroll=8)
    width = 512
    for c in range(out_ref.shape[1] // width):
        columns = slice(c * width, (c + 1) * width)
        whole = functools.reduce(lambda a, b: a + b, [total[columns, :] for total in sums])
        turned = whole.T
        result = turned[:HALF] + turned[HALF:] + base_ref[:, columns]
        out_ref[:, columns] = jnp.maximum(result + bias_ref[...], 0.0) if last else result


def scatter_rows(parts, rows, base, bias, last):
    return pl.pallas_call(
        functools.partial(scatter_kernel, blocks=len(parts), last=last),
        in_specs=[pl.BlockSpec(memory_space=pltpu.SMEM)]
        + [pl.BlockSpec(memory_space=pltpu.VMEM)] * (len(parts) + 2),
        out_specs=pl.BlockSpec(memory_space=pltpu.VMEM),
        out_shape=jax.ShapeDtypeStruct(base.shape, jnp.float32),
        scratch_shapes=[pltpu.VMEM((base.shape[1] + 8, LANES), jnp.float32)] * 4,
        compiler_params=pltpu.CompilerParams(vmem_limit_bytes=16 * 2**20),
        cost_estimate=pl.CostEstimate(flops=10**7, bytes_accessed=16 * 2**20, transcendentals=0),
    )(rows, *parts, base, bias)


def shifted(value, count, step):
    return lax.ppermute(value, "feat", [(i, (i + step) % count) for i in range(count)])


def per_device(
    features,
    w_self,
    w_neigh,
    out_bias,
    hub_rows,
    replica_send_rows,
    ret_rows,
    tile_src,
    tile_dst,
    tile_vals,
    *,
    feat,
):
    xt = features.T
    peers, slot = replica_send_rows.shape[1:]
    ret = ret_rows.shape[2]
    outgoing = gather_rows(xt, replica_send_rows[0], hub_rows[0])
    mirror = lax.all_to_all(outgoing, "dom", split_axis=0, concat_axis=0, tiled=True)

    me = lax.axis_index("feat")
    width = xt.shape[0]
    neighbours = [w_neigh] + [shifted(w_neigh, feat, -d) for d in range(1, feat)]
    xt, tiles, neighbours = lax.optimization_barrier((xt, tile_vals[0], neighbours))
    blocks = [xt] + [shifted(xt, feat, d) for d in range(1, feat)]
    split_vals, tile_order = split_tiles(tiles, tile_src[0], tile_dst[0])

    mirror, split_vals, tile_order = lax.optimization_barrier((mirror, split_vals, tile_order))
    rows = slot // 2
    hub_count = hub_rows.shape[1] * peers // slot
    hub_half = mirror[:, rows:]
    hub_other = lax.ppermute(hub_half, "dom", [(i, i ^ 1) for i in range(peers)])
    side = (lax.axis_index("dom") % 2).astype(jnp.int32).reshape(1)
    partial = listed_tiles(split_vals, mirror, tile_order, rows, hub_count, peers * ret // slot)
    partial = hub_tiles(split_vals, hub_half, hub_other, partial, tile_order, side)
    partial, blocks, neighbours, w_self, ret_rows = lax.optimization_barrier(
        (partial, blocks, neighbours, w_self, ret_rows)
    )
    slots = lax.all_to_all(partial, ("dom", "feat"), split_axis=0, concat_axis=0, tiled=True)

    self_rows = w_self.reshape(feat, width, -1)
    self_rows = jnp.concatenate(
        [lax.dynamic_index_in_dim(self_rows, (me - d) % feat, 0, False) for d in range(feat)]
    )
    own = lax.dot_general(
        self_rows,
        jnp.concatenate(blocks),
        (((0,), (0,)), ((), ())),
        precision=lax.Precision.HIGHEST,
        preferred_element_type=jnp.float32,
    )
    weights = []
    for mine in neighbours:
        mine = mine.reshape(feat, width, width)
        empty = jnp.zeros_like(mine)
        weights.append(
            jnp.stack([jnp.concatenate([mine, empty], 2), jnp.concatenate([empty, mine], 2)], 1).reshape(
                feat * LANES, LANES
            )
        )
    weights = split_weights(jnp.stack(weights))
    quarters = ret_rows[0].reshape(peers, feat, 2, 8).transpose(1, 0, 3, 2)
    order = [
        lax.dynamic_index_in_dim(quarters, (me - d) % feat, 0, False).reshape(-1) for d in range(feat)
    ]
    far = feat // 2
    near = [d for d in range(feat - 1, 0, -1) if d != far]
    near_rows = jnp.concatenate([order[d] for d in near])
    bias = out_bias[:, None]
    slots, own, weights, near_rows, order, bias = lax.optimization_barrier(
        (slots, own, weights, near_rows, order, bias)
    )
    slots = slots.reshape(peers, feat, 8, LANES)
    parts = project_slots(slots, weights, range(feat))
    moved = {d: shifted(parts[d], feat, d) for d in near}
    total = scatter_rows([parts[0]], order[0], own, bias, False)
    last, total = lax.optimization_barrier((parts[far], total))
    moved[far] = shifted(last, feat, far)
    total = scatter_rows([moved[d] for d in near], near_rows, total, bias, False)
    return scatter_rows([moved[far]], order[far], total, bias, True).T


def solution(mesh):
    return jax.shard_map(
        functools.partial(per_device, feat=mesh.shape["feat"]),
        mesh=mesh,
        in_specs=(
            P("dom", "feat"),
            P(None, "feat"),
            P(None, "feat"),
            P("feat"),
            P("dom", None),
            P("dom", None, None),
            P("dom", None, None),
            P("dom", None),
            P("dom", None),
            P("dom", None, None, None),
        ),
        out_specs=P("dom", "feat"),
        check_vma=False,
    )
```

time: 194 us -> 164 us (0.85)
  waiting for transfers between devices: 97.2 us -> 71.1 us
  between operations: 13.6 us -> 0.41 us
  Pallas kernels: 34.2 us -> 40.3 us
  starting transfers between devices: 30.3 us -> 33.6 us
  local copies, waits for them, and re-layouts: 13.7 us -> 11.1 us
    all_to_all x1, waiting for transfers between devices: 65.2 us -> 41.5 us  [per_device(): lax.all_to_all(outgoing, 'dom', split_axis=0, concat_axis=0, tiled=True)]
    pallas_call x4 -> x8, Pallas kernels: 19.5 us -> 28.9 us  [the longest x3 12.7 us: scatter_rows(): pl.pallas_call(functools.partial(scatter_kernel, blocks=len(parts), last=...]
    unnamed x27 -> x20, local copies, waits for them, and re-layouts: 11.9 us -> 6.67 us
    pallas_call x1, Pallas kernels: 14.6 us -> 11.3 us  [gather_rows(): pl.pallas_call(functools.partial(gather_kernel, peers=peers, rows=rows, h...]
    ppermute x6 -> x9, starting transfers between devices: 8 us -> 10.9 us  [shifted(): lax.ppermute(value, 'feat', [(i, (i + step) % count) for i in range(count)])]
    ppermute x0 -> x1, starting transfers between devices: none -> 2.14 us  [per_device(): lax.ppermute(hub_half, 'dom', [(i, i ^ 1) for i in range(peers)])]
    dynamic_slice x1 -> x6, local copies, waits for them, and re-layouts: 0.01 us -> 2.03 us  [the longest x1 1.33 us: per_device(): lax.dynamic_index_in_dim(self_rows, (me - d) % feat, 0, False)]
    ppermute x6 -> x9, waiting for transfers between devices: 12.9 us -> 13 us  [shifted(): lax.ppermute(value, 'feat', [(i, (i + step) % count) for i in range(count)])]
  transfers between devices with their start and end apart: 9 -> 12, of which waited for: 6 -> 6; matrix products, arithmetic and copies ran while one was open for 4% -> 7% of each run, Pallas kernels for 5% -> 14%
where the time goes in v2:
time: 164 us; the launch traced here: 163 us
  waiting for transfers between devices  71.1 us (43%)
  Pallas kernels  40.3 us (25%)
  starting transfers between devices  33.6 us (20%)
  local copies, waits for them, and re-layouts  11.1 us (7%)
  matrix products  5.79 us (4%)
    all_to_all x1, waiting for transfers between devices, per_device(): lax.all_to_all(outgoing, 'dom', split_axis=0, concat_axis=0, tiled=True)  41.5 us
    all_to_all x1, waiting for transfers between devices, per_device(): lax.all_to_all(partial, ('dom', 'feat'), split_axis=0, concat_axis=0, til...  16.6 us
    all_to_all x1, starting transfers between devices, per_device(): lax.all_to_all(outgoing, 'dom', split_axis=0, concat_axis=0, tiled=True)  13.2 us
    ppermute x9, waiting for transfers between devices, shifted(): lax.ppermute(value, 'feat', [(i, (i + step) % count) for i in range(count)])  13 us
    pallas_call x3, Pallas kernels, scatter_rows(): pl.pallas_call(functools.partial(scatter_kernel, blocks=len(parts), last=...  12.7 us
    pallas_call x1, Pallas kernels, gather_rows(): pl.pallas_call(functools.partial(gather_kernel, peers=peers, rows=rows, h...  11.3 us
    ppermute x9, starting transfers between devices, shifted(): lax.ppermute(value, 'feat', [(i, (i + step) % count) for i in range(count)])  10.9 us
    all_to_all x1, starting transfers between devices, per_device(): lax.all_to_all(partial, ('dom', 'feat'), split_axis=0, concat_axis=0, til...  7.47 us
  transfers between devices with their start and end apart: 12, of which 6 were waited for; matrix products, arithmetic and copies ran while one was open for 7% of the time, Pallas kernels for 14%

profile of v2, /device:TPU:1, one launch (start us, length us, event | category | flops | bytes accessed | tf_op | source)
XLA Modules:
  0.0 163.4 jit_solution(15786072363689522203)
XLA Ops:
  0.0 11.3 %shard_map.100 = f32[64,80,128]{2,1,0:T(8,128)} custom-call(s32[8192]{0:T(1024)} %bitcast.75, s32[64]{0:T(128)} %bitcast.81, f32[64,4096]{1,0:T(8,128)} %bitcast.61), custom_call_target="tpu_custom_call" | custom-call | flops 10000000 | bytes 4194304 | tf_op jit(solution)/shard_map/pallas_call | solution.py:64
  11.4 13.2 %all-to-all-start = ((f32[64,80,128]{2,1,0:T(8,128)}), f32[64,80,128]{2,1,0:T(8,128)S(1)}, u32[]{:S(2)}, u32[]{:S(2)}) async-start(f32[64,80,128]{2,1,0:T(8,128)} %shard_map.100), calls=%async_computation | async-start | bytes 5242880 | tf_op jit(solution)/shard_map/all_to_all | solution.py:366
  24.5 2.6 %collective-permute-start = (f32[256,64]{0,1:T(8,128)S(1)}, f32[256,64]{0,1:T(8,128)S(1)}, u32[]{:S(2)}, u32[]{:S(2)}) collective-permute-start(f32[256,64]{0,1:T(8,128)S(1)} %copy-done.7), channel_id=1, source_target_pairs={{0,3},{1,0},{2,1},{3,2},{4,7},{5,4},{6,5},{7,6},{8,11},{9,8},{10,9... | collective-permute-start | bytes 196616 | tf_op jit(solution)/shard_map/ppermute | solution.py:345
  27.1 0.5 collective-permute-start.1
  27.6 0.6 collective-permute-start.2
  28.2 0.2 collective-permute-done
  28.4 3.6 %collective-permute-done.1 = f32[256,64]{0,1:T(8,128)S(1)} collective-permute-done((f32[256,64]{0,1:T(8,128)S(1)}, f32[256,64]{0,1:T(8,128)S(1)}, u32[]{:S(2)}, u32[]{:S(2)}) %collective-permute-start.1) | collective-permute-done | bytes 65568 | tf_op jit(solution)/shard_map/ppermute | solution.py:345
  32.0 0.9 collective-permute-done.2
  32.9 1.5 collective-permute-start.5
  34.4 1.9 %collective-permute-start.6 = (f32[64,4096]{1,0:T(8,128)}, f32[64,4096]{1,0:T(8,128)}, u32[]{:S(2)}, u32[]{:S(2)}) collective-permute-start(f32[64,4096]{1,0:T(8,128)} %bitcast.64), channel_id=1, source_target_pairs={{0,3},{1,0},{2,1},{3,2},{4,7},{5,4},{6,5},{7,6},{8,11},{9,8},{10,9... | collective-permute-start | bytes 3145736 | tf_op jit(solution)/shard_map/ppermute | solution.py:345
  36.3 2.8 %copy-done.2 = f32[1,96,128,128]{3,2,1,0:T(8,128)S(1)} copy-done((f32[1,96,128,128]{3,2,1,0:T(8,128)S(1)}, f32[1,96,128,128]{3,2,1,0:T(8,128)}, u32[]{:S(2)}) %copy-start.2) | copy-done | bytes 6291480
  39.0 2.4 %shard_map.101 = (bf16[96,128,256]{2,1,0:T(8,128)(2,1)S(1)}, s32[96]{0:T(128)S(1)}) custom-call(s32[96]{0:T(128)S(1)} %bitcast.59, s32[96]{0:T(128)S(1)} %bitcast.60, f32[96,128,128]{2,1,0:T(8,128)S(1)} %bitcast.57), custom_call_target="tpu_custom_call" | custom-call | flops 10000000 | bytes 12582912 | tf_op jit(solution)/shard_map/pallas_call | solution.py:104
  41.4 2.6 %copy-done = bf16[96,128,256]{2,1,0:T(8,128)(2,1)} copy-done((bf16[96,128,256]{2,1,0:T(8,128)(2,1)}, bf16[96,128,256]{2,1,0:T(8,128)(2,1)S(1)}, u32[]{:S(2)}) %copy-start) | copy-done | bytes 6291480
  44.1 41.5 %all-to-all-done.mirror_ref = f32[64,80,128]{2,1,0:T(8,128)S(1)} async-done(((f32[64,80,128]{2,1,0:T(8,128)}), f32[64,80,128]{2,1,0:T(8,128)S(1)}, u32[]{:S(2)}, u32[]{:S(2)}) %all-to-all-start) | async-done | bytes 2621472 | tf_op jit(solution)/shard_map/all_to_all | solution.py:366
  85.6 2.1 %collective-permute-start.3 = (f32[64,16,128]{2,1,0:T(8,128)S(1)}, f32[64,16,128]{2,1,0:T(8,128)}, u32[]{:S(2)}, u32[]{:S(2)}) collective-permute-start(f32[64,16,128]{2,1,0:T(8,128)S(1)} %slice.3.own_ref), channel_id=1, source_target_pairs={{0,4},{4,0},{8,12},{12,8},{16,20},{20,16},{24,28},{28,24},{32,36},... | collective-permute-start | bytes 1572872 | tf_op jit(solution)/shard_map/ppermute | solution.py:379
  87.7 4.9 %shard_map.102.before_ref = f32[256,8,128]{2,1,0:T(8,128)S(1)} custom-call(s32[96]{0:T(128)S(1)} %get-tuple-element.43.dst_ref, bf16[96,128,256]{2,1,0:T(8,128)(2,1)} %copy-done, f32[64,80,128]{2,1,0:T(8,128)S(1)} %all-to-all-done.mirror_ref), custom_call_target="tpu_custom_call" | custom-call | flops 1000000000 | bytes 10485760 | tf_op jit(solution)/shard_map/pallas_call | solution.py:176
  92.7 4.8 %shard_map.103 = f32[256,8,128]{2,1,0:T(8,128)} custom-call(s32[96]{0:T(128)S(1)} %get-tuple-element.43.dst_ref, s32[1]{0:T(128)} %bitcast.6.side_ref, bf16[96,128,256]{2,1,0:T(8,128)(2,1)} %copy-done, f32[64,16,128]{2,1,0:T(8,128)S(1)} %slice.3.own_ref, f32[64,16,128]{2,1,0:T(8,128)} %collective-permute-done.3.other_ref, ...), custom_call_target="tpu_custom_call" | custom-call | flops 1000000000 | bytes 6291456 | tf_op jit(solution)/shard_map/pallas_call | solution.py:238
  97.5 7.5 %all-to-all-start.1 = ((f32[256,8,128]{2,1,0:T(8,128)}), f32[256,8,128]{2,1,0:T(8,128)S(1)}, u32[]{:S(2)}, u32[]{:S(2)}) async-start(f32[256,8,128]{2,1,0:T(8,128)} %shard_map.103), calls=%async_computation.1 | async-start | bytes 2097152 | tf_op jit(solution)/shard_map/all_to_all | solution.py:386
  105.1 0.7 reshape.38
  105.9 0.1 copy.40
  106.0 0.1 copy.39
  106.1 0.1 copy.38
  106.2 0.1 pad_bitcast_fusion.1
  106.4 0.1 pad_bitcast_fusion.3
  106.5 0.1 pad_bitcast_fusion.5
  106.6 0.1 pad_bitcast_fusion.7
  106.8 1.1 pad_maximum_fusion.weights_ref
  107.8 2.9 %shard_map.104.weights_ref = bf16[4,1024,256]{2,1,0:T(8,128)(2,1)} custom-call(f32[4,512,128]{2,1,0:T(8,128)} %pad_maximum_fusion.weights_ref), custom_call_target="tpu_custom_call" | custom-call | tf_op jit(solution)/shard_map/pallas_call | solution.py:269
  110.8 0.2 copy.32
  111.0 0.2 reshape.44
  111.2 0.2 copy.31
  111.3 0.2 reshape.43
  111.5 0.2 copy.33
  111.7 0.2 reshape.45.rows_ref
  111.9 0.2 copy.34
  112.1 0.2 reshape.46.rows_ref
  112.2 1.3 constant_dynamic-slice_fusion.3
  113.6 5.8 %fusion.refs_1_ = f32[64,4096]{1,0:T(8,128)} fusion(f32[64,4096]{1,0:T(8,128)} %collective-permute-done.6, f32[64,4096]{1,0:T(8,128)} %collective-permute-done.5, f32[64,4096]{1,0:T(8,128)} %collective-permute-done.4, f32[64,4096]{1,0:T(8,128)} %bitcast.65, f32[64,64]{0,1:T(8,128)S(1)} %bitcast.77, f32[64,64]{0,1:T(8,128)S(1)} %bitcast.78, ...), kind=kOutput, calls=%fused_computation | convolution fusion | flops 808501248 | bytes 5308416 | tf_op jit(solution)/shard_map/dot_general | solution.py:392
  119.4 16.6 %all-to-all-done.1 = f32[256,8,128]{2,1,0:T(8,128)S(1)} async-done(((f32[256,8,128]{2,1,0:T(8,128)}), f32[256,8,128]{2,1,0:T(8,128)S(1)}, u32[]{:S(2)}, u32[]{:S(2)}) %all-to-all-start.1) | async-done | bytes 1048608 | tf_op jit(solution)/shard_map/all_to_all | solution.py:386
  135.9 0.1 copy.35.refs_2_.refs_3_
  136.0 1.2 shard_map.105
  137.3 1.8 %collective-permute-start.8 = (f32[512,128]{1,0:T(8,128)S(1)}, f32[512,128]{1,0:T(8,128)S(1)}, u32[]{:S(2)}, u32[]{:S(2)}) collective-permute-start(f32[512,128]{1,0:T(8,128)S(1)} %get-tuple-element.72), channel_id=1, source_target_pairs={{0,3},{1,0},{2,1},{3,2},{4,7},{5,4},{6,5},{7,6},{8,11},{9,8},{10,9... | collective-permute-start | bytes 786440 | tf_op jit(solution)/shard_map/ppermute | solution.py:345
  139.1 1.2 copy-done.3
  140.4 3.2 %shard_map.106.refs_2_ = f32[64,4096]{1,0:T(8,128)S(1)} custom-call(s32[1024]{0:T(1024)S(1)} %reshape.45.rows_ref, f32[512,128]{1,0:T(8,128)S(1)} %get-tuple-element.67.refs_0_, f32[64,4096]{1,0:T(8,128)S(1)} %copy-done.3, f32[64,1]{1,0:T(8,128)S(1)} %copy.35.refs_2_.refs_3_), custom_call_target="tpu_custom_call" | custom-call | flops 10000000 | bytes 16777216 | tf_op jit(solution)/shard_map/pallas_call | solution.py:332
  143.6 2.0 %collective-permute-start.7 = (f32[512,128]{1,0:T(8,128)S(1)}, f32[512,128]{1,0:T(8,128)S(1)}, u32[]{:S(2)}, u32[]{:S(2)}) collective-permute-start(f32[512,128]{1,0:T(8,128)S(1)} %get-tuple-element.70), channel_id=1, source_target_pairs={{0,2},{1,3},{2,0},{3,1},{4,6},{5,7},{6,4},{7,5},{8,10},{9,11},{10,... | collective-permute-start | bytes 786440 | tf_op jit(solution)/shard_map/ppermute | solution.py:345
  145.6 8.3 %collective-permute-done.9.refs_1_ = f32[512,128]{1,0:T(8,128)S(1)} collective-permute-done((f32[512,128]{1,0:T(8,128)S(1)}, f32[512,128]{1,0:T(8,128)S(1)}, u32[]{:S(2)}, u32[]{:S(2)}) %collective-permute-start.9) | collective-permute-done | bytes 262176 | tf_op jit(solution)/shard_map/ppermute | solution.py:345
  153.9 5.1 %shard_map.107.refs_1_ = f32[64,4096]{1,0:T(8,128)S(1)} custom-call(s32[2048]{0:T(1024)S(1)} %pad_add_fusion.rows_ref, f32[512,128]{1,0:T(8,128)S(1)} %collective-permute-done.8.refs_0_, f32[512,128]{1,0:T(8,128)S(1)} %collective-permute-done.9.refs_1_, f32[64,4096]{1,0:T(8,128)S(1)} %shard_map.106.refs_2_, f32[64,1]{1,0:T(8,128)S(1)} %copy.35.refs_2_.refs_3_), custom_call_target="tpu_custom_call" | custom-call | flops 10000000 | bytes 16777216 | tf_op jit(solution)/shard_map/pallas_call | solution.py:332
  159.0 4.4 %shard_map.108 = f32[64,4096]{1,0:T(8,128)} custom-call(s32[1024]{0:T(1024)S(1)} %reshape.46.rows_ref, f32[512,128]{1,0:T(8,128)S(1)} %collective-permute-done.7.refs_0_, f32[64,4096]{1,0:T(8,128)S(1)} %shard_map.107.refs_1_, f32[64,1]{1,0:T(8,128)S(1)} %copy.35.refs_2_.refs_3_), custom_call_target="tpu_custom_call" | custom-call | flops 10000000 | bytes 16777216 | tf_op jit(solution)/shard_map/pallas_call | solution.py:332
  (34 shorter events, 0.3 us)
Async XLA Ops:
  0.0 24.5 %copy-start.7 = (f32[256,64]{0,1:T(8,128)S(1)}, f32[256,64]{0,1:T(8,128)}, u32[]{:S(2)}) copy-start(f32[256,64]{0,1:T(8,128)} %param.12) | copy-start | bytes 196612
  0.0 36.3 %copy-start.4 = (s32[1,96]{1,0:T(1,128)S(1)}, s32[1,96]{1,0:T(1,128)}, u32[]{:S(2)}) copy-start(s32[1,96]{1,0:T(1,128)} %param.17) | copy-start | bytes 1156
  0.0 36.3 %copy-start.5 = (s32[1,96]{1,0:T(1,128)S(1)}, s32[1,96]{1,0:T(1,128)}, u32[]{:S(2)}) copy-start(s32[1,96]{1,0:T(1,128)} %param.18) | copy-start | bytes 1156
  11.4 74.2 %all-to-all-start = ((f32[64,80,128]{2,1,0:T(8,128)}), f32[64,80,128]{2,1,0:T(8,128)S(1)}, u32[]{:S(2)}, u32[]{:S(2)}) async-start(f32[64,80,128]{2,1,0:T(8,128)} %shard_map.100), calls=%async_computation | async-start | bytes 5242880 | tf_op jit(solution)/shard_map/all_to_all | solution.py:366
  24.5 3.9 %collective-permute-start = (f32[256,64]{0,1:T(8,128)S(1)}, f32[256,64]{0,1:T(8,128)S(1)}, u32[]{:S(2)}, u32[]{:S(2)}) collective-permute-start(f32[256,64]{0,1:T(8,128)S(1)} %copy-done.7), channel_id=1, source_target_pairs={{0,3},{1,0},{2,1},{3,2},{4,7},{5,4},{6,5},{7,6},{8,11},{9,8},{10,9... | collective-permute-start | bytes 196616 | tf_op jit(solution)/shard_map/ppermute | solution.py:345
  27.1 4.9 %collective-permute-start.1 = (f32[256,64]{0,1:T(8,128)S(1)}, f32[256,64]{0,1:T(8,128)S(1)}, u32[]{:S(2)}, u32[]{:S(2)}) collective-permute-start(f32[256,64]{0,1:T(8,128)S(1)} %copy-done.7), channel_id=1, source_target_pairs={{0,2},{1,3},{2,0},{3,1},{4,6},{5,7},{6,4},{7,5},{8,10},{9,11},{10,... | collective-permute-start | bytes 196616 | tf_op jit(solution)/shard_map/ppermute | solution.py:345
  27.6 5.3 %collective-permute-start.2 = (f32[256,64]{0,1:T(8,128)S(1)}, f32[256,64]{0,1:T(8,128)S(1)}, u32[]{:S(2)}, u32[]{:S(2)}) collective-permute-start(f32[256,64]{0,1:T(8,128)S(1)} %copy-done.7), channel_id=1, source_target_pairs={{0,1},{1,2},{2,3},{3,0},{4,5},{5,6},{6,7},{7,4},{8,9},{9,10},{10,1... | collective-permute-start | bytes 196616 | tf_op jit(solution)/shard_map/ppermute | solution.py:345
  32.9 64.6 %collective-permute-start.4 = (f32[64,4096]{1,0:T(8,128)}, f32[64,4096]{1,0:T(8,128)}, u32[]{:S(2)}, u32[]{:S(2)}) collective-permute-start(f32[64,4096]{1,0:T(8,128)} %bitcast.62), channel_id=1, source_target_pairs={{0,1},{1,2},{2,3},{3,0},{4,5},{5,6},{6,7},{7,4},{8,9},{9,10},{10,1... | collective-permute-start | bytes 3145736 | tf_op jit(solution)/shard_map/ppermute | solution.py:345
  32.9 64.6 %collective-permute-start.5 = (f32[64,4096]{1,0:T(8,128)}, f32[64,4096]{1,0:T(8,128)}, u32[]{:S(2)}, u32[]{:S(2)}) collective-permute-start(f32[64,4096]{1,0:T(8,128)} %bitcast.63), channel_id=1, source_target_pairs={{0,2},{1,3},{2,0},{3,1},{4,6},{5,7},{6,4},{7,5},{8,10},{9,11},{10,... | collective-permute-start | bytes 3145736 | tf_op jit(solution)/shard_map/ppermute | solution.py:345
  34.4 63.2 %collective-permute-start.6 = (f32[64,4096]{1,0:T(8,128)}, f32[64,4096]{1,0:T(8,128)}, u32[]{:S(2)}, u32[]{:S(2)}) collective-permute-start(f32[64,4096]{1,0:T(8,128)} %bitcast.64), channel_id=1, source_target_pairs={{0,3},{1,0},{2,1},{3,2},{4,7},{5,4},{6,5},{7,6},{8,11},{9,8},{10,9... | collective-permute-start | bytes 3145736 | tf_op jit(solution)/shard_map/ppermute | solution.py:345
  36.3 2.8 %copy-start.2 = (f32[1,96,128,128]{3,2,1,0:T(8,128)S(1)}, f32[1,96,128,128]{3,2,1,0:T(8,128)}, u32[]{:S(2)}) copy-start(f32[1,96,128,128]{3,2,1,0:T(8,128)} %param.19) | copy-start | bytes 18874372
  41.4 2.6 %copy-start = (bf16[96,128,256]{2,1,0:T(8,128)(2,1)}, bf16[96,128,256]{2,1,0:T(8,128)(2,1)S(1)}, u32[]{:S(2)}) copy-start(bf16[96,128,256]{2,1,0:T(8,128)(2,1)S(1)} %get-tuple-element.44.tiles_hbm) | copy-start | bytes 18874372
  85.6 7.1 %collective-permute-start.3 = (f32[64,16,128]{2,1,0:T(8,128)S(1)}, f32[64,16,128]{2,1,0:T(8,128)}, u32[]{:S(2)}, u32[]{:S(2)}) collective-permute-start(f32[64,16,128]{2,1,0:T(8,128)S(1)} %slice.3.own_ref), channel_id=1, source_target_pairs={{0,4},{4,0},{8,12},{12,8},{16,20},{20,16},{24,28},{28,24},{32,36},... | collective-permute-start | bytes 1572872 | tf_op jit(solution)/shard_map/ppermute | solution.py:379
  92.7 12.4 %copy-start.6 = (f32[256,64]{0,1:T(8,128)S(1)}, f32[256,64]{0,1:T(8,128)}, u32[]{:S(2)}) copy-start(f32[256,64]{0,1:T(8,128)} %param.11) | copy-start | bytes 196612
  97.5 38.4 %all-to-all-start.1 = ((f32[256,8,128]{2,1,0:T(8,128)}), f32[256,8,128]{2,1,0:T(8,128)S(1)}, u32[]{:S(2)}, u32[]{:S(2)}) async-start(f32[256,8,128]{2,1,0:T(8,128)} %shard_map.103), calls=%async_computation.1 | async-start | bytes 2097152 | tf_op jit(solution)/shard_map/all_to_all | solution.py:386
  106.3 4.4 %copy-start.8 = (s32[1,64,64]{2,1,0:T(8,128)S(1)}, s32[1,64,64]{2,1,0:T(8,128)}, u32[]{:S(2)}) copy-start(s32[1,64,64]{2,1,0:T(8,128)} %param.16) | copy-start | bytes 49156
  111.7 24.3 %copy-start.9 = (f32[64]{0:T(128)S(1)}, f32[64]{0:T(128)}, u32[]{:S(2)}) copy-start(f32[64]{0:T(128)} %param.13) | copy-start | bytes 772
  111.7 24.3 %copy-start.1 = (bf16[4,1024,256]{2,1,0:T(8,128)(2,1)S(1)}, bf16[4,1024,256]{2,1,0:T(8,128)(2,1)}, u32[]{:S(2)}) copy-start(bf16[4,1024,256]{2,1,0:T(8,128)(2,1)} %shard_map.104.weights_ref) | copy-start | bytes 6291460
  137.3 8.3 %collective-permute-start.8 = (f32[512,128]{1,0:T(8,128)S(1)}, f32[512,128]{1,0:T(8,128)S(1)}, u32[]{:S(2)}, u32[]{:S(2)}) collective-permute-start(f32[512,128]{1,0:T(8,128)S(1)} %get-tuple-element.72), channel_id=1, source_target_pairs={{0,3},{1,0},{2,1},{3,2},{4,7},{5,4},{6,5},{7,6},{8,11},{9,8},{10,9... | collective-permute-start | bytes 786440 | tf_op jit(solution)/shard_map/ppermute | solution.py:345
  139.1 14.8 %collective-permute-start.9 = (f32[512,128]{1,0:T(8,128)S(1)}, f32[512,128]{1,0:T(8,128)S(1)}, u32[]{:S(2)}, u32[]{:S(2)}) collective-permute-start(f32[512,128]{1,0:T(8,128)S(1)} %get-tuple-element.73), channel_id=1, source_target_pairs={{0,1},{1,2},{2,3},{3,0},{4,5},{5,6},{6,7},{7,4},{8,9},{9,10},{10,1... | collective-permute-start | bytes 786440 | tf_op jit(solution)/shard_map/ppermute | solution.py:345
  139.1 1.2 copy-start.3
  143.6 15.4 %collective-permute-start.7 = (f32[512,128]{1,0:T(8,128)S(1)}, f32[512,128]{1,0:T(8,128)S(1)}, u32[]{:S(2)}, u32[]{:S(2)}) collective-permute-start(f32[512,128]{1,0:T(8,128)S(1)} %get-tuple-element.70), channel_id=1, source_target_pairs={{0,2},{1,3},{2,0},{3,1},{4,6},{5,7},{6,4},{7,5},{8,10},{9,11},{10,... | collective-permute-start | bytes 786440 | tf_op jit(solution)/shard_map/ppermute | solution.py:345

commit v3 on v2

--- a/solution.py
+++ b/solution.py
@@ -151,11 +151,16 @@
             tiles_hbm.at[pl.ds(first + c * count, count)], tiles_ref.at[pl.ds(c * count, count)], sems.at[c]
         )
 
-    for c in range(chunks):
+    ahead = 2
+    for c in range(ahead):
         fetch(c).start()
     acc_ref[...] = jnp.zeros_like(acc_ref)
 
     def chunk(c, carry):
+        @pl.when(c + ahead < chunks)
+        def _():
+            fetch(c + ahead).start()
+
         fetch(c).wait()
         for i in range(count):
             tile = c * count + i
@@ -296,10 +301,11 @@
     )(slots, weights)
 
 
-def scatter_kernel(rows_ref, *refs, blocks, last):
+def scatter_kernel(rows_ref, *refs, blocks, bases, last):
     parts = refs[:blocks]
-    base_ref, bias_ref, out_ref = refs[blocks : blocks + 3]
-    sums = refs[blocks + 3 :]
+    base_refs = refs[blocks : blocks + bases]
+    bias_ref = refs[blocks + bases] if last else None
+    out_ref, *sums = refs[blocks + bases + last :]
     for total in sums:
         total[...] = jnp.zeros_like(total)
     left = left_half((1, LANES))
@@ -324,21 +330,24 @@
         columns = slice(c * width, (c + 1) * width)
         whole = functools.reduce(lambda a, b: a + b, [total[columns, :] for total in sums])
         turned = whole.T
-        result = turned[:HALF] + turned[HALF:] + base_ref[:, columns]
+        result = turned[:HALF] + turned[HALF:]
+        for base in base_refs:
+            result = result + base[:, columns]
         out_ref[:, columns] = jnp.maximum(result + bias_ref[...], 0.0) if last else result
 
 
-def scatter_rows(parts, rows, base, bias, last):
-    return pl.pallas_call(
-        functools.partial(scatter_kernel, blocks=len(parts), last=last),
-        in_specs=[pl.BlockSpec(memory_space=pltpu.SMEM)]
-        + [pl.BlockSpec(memory_space=pltpu.VMEM)] * (len(parts) + 2),
-        out_specs=pl.BlockSpec(memory_space=pltpu.VMEM),
-        out_shape=jax.ShapeDtypeStruct(base.shape, jnp.float32),
-        scratch_shapes=[pltpu.VMEM((base.shape[1] + 8, LANES), jnp.float32)] * 4,
+def scatter_rows(parts, rows, bases, row_count, bias=None):
+    last = bias is not None
+    vmem = pl.BlockSpec(memory_space=pltpu.VMEM)
+    return pl.pallas_call(
+        functools.partial(scatter_kernel, blocks=len(parts), bases=len(bases), last=last),
+        in_specs=[pl.BlockSpec(memory_space=pltpu.SMEM)] + [vmem] * (len(parts) + len(bases) + last),
+        out_specs=vmem,
+        out_shape=jax.ShapeDtypeStruct((HALF, row_count), jnp.float32),
+        scratch_shapes=[pltpu.VMEM((row_count + 8, LANES), jnp.float32)] * 4,
         compiler_params=pltpu.CompilerParams(vmem_limit_bytes=16 * 2**20),
         cost_estimate=pl.CostEstimate(flops=10**7, bytes_accessed=16 * 2**20, transcendentals=0),
-    )(rows, *parts, base, bias)
+    )(rows, *parts, *bases, *([bias] if last else []))
 
 
 def shifted(value, count, step):
@@ -412,19 +421,21 @@
     ]
     far = feat // 2
     near = [d for d in range(feat - 1, 0, -1) if d != far]
-    near_rows = jnp.concatenate([order[d] for d in near])
+    tail = (*near[1:], far)
+    tail_rows = jnp.concatenate([order[d] for d in tail])
     bias = out_bias[:, None]
-    slots, own, weights, near_rows, order, bias = lax.optimization_barrier(
-        (slots, own, weights, near_rows, order, bias)
+    row_count = features.shape[0]
+    slots, own, weights, tail_rows, order, bias = lax.optimization_barrier(
+        (slots, own, weights, tail_rows, order, bias)
     )
     slots = slots.reshape(peers, feat, 8, LANES)
     parts = project_slots(slots, weights, range(feat))
     moved = {d: shifted(parts[d], feat, d) for d in near}
-    total = scatter_rows([parts[0]], order[0], own, bias, False)
+    total = scatter_rows([parts[0]], order[0], [], row_count)
     last, total = lax.optimization_barrier((parts[far], total))
     moved[far] = shifted(last, feat, far)
-    total = scatter_rows([moved[d] for d in near], near_rows, total, bias, False)
-    return scatter_rows([moved[far]], order[far], total, bias, True).T
+    total = scatter_rows([moved[near[0]]], order[near[0]], [total], row_count)
+    return scatter_rows([moved[d] for d in tail], tail_rows, [total, own], row_count, bias).T
 
 
 def solution(mesh):

time: 164 us -> 163 us (level); the launches traced: 163 us -> 160 us
  waiting for transfers between devices: 71.1 us -> 65.9 us
    ppermute x9, waiting for transfers between devices: 13 us -> 9.25 us  [shifted(): lax.ppermute(value, 'feat', [(i, (i + step) % count) for i in range(count)])]
    unnamed x20 -> x24, local copies, waits for them, and re-layouts: 6.67 us -> 5.46 us
  transfers between devices with their start and end apart: 12 -> 12, of which waited for: 6 -> 7; matrix products, arithmetic and copies ran while one was open for 7% -> 8% of each run, Pallas kernels for 14% -> 14%
where the time goes in v3:
time: 163 us; the launch traced here: 160 us
  waiting for transfers between devices  65.9 us (40%)
  Pallas kernels  41.5 us (25%)
  starting transfers between devices  33.6 us (21%)
  local copies, waits for them, and re-layouts  10.6 us (7%)
  matrix products  5.79 us (4%)
  other arithmetic  1.83 us (1%)
    all_to_all x1, waiting for transfers between devices, per_device(): lax.all_to_all(outgoing, 'dom', split_axis=0, concat_axis=0, tiled=True)  41.5 us
    all_to_all x1, waiting for transfers between devices, per_device(): lax.all_to_all(partial, ('dom', 'feat'), split_axis=0, concat_axis=0, til...  15.2 us
    all_to_all x1, starting transfers between devices, per_device(): lax.all_to_all(outgoing, 'dom', split_axis=0, concat_axis=0, tiled=True)  13.2 us
    pallas_call x3, Pallas kernels, scatter_rows(): pl.pallas_call(functools.partial(scatter_kernel, blocks=len(parts), bases...  12.7 us
    pallas_call x1, Pallas kernels, gather_rows(): pl.pallas_call(functools.partial(gather_kernel, peers=peers, rows=rows, h...  11.3 us
    ppermute x9, starting transfers between devices, shifted(): lax.ppermute(value, 'feat', [(i, (i + step) % count) for i in range(count)])  10.8 us
    ppermute x9, waiting for transfers between devices, shifted(): lax.ppermute(value, 'feat', [(i, (i + step) % count) for i in range(count)])  9.25 us
    all_to_all x1, starting transfers between devices, per_device(): lax.all_to_all(partial, ('dom', 'feat'), split_axis=0, concat_axis=0, til...  7.47 us
  transfers between devices with their start and end apart: 12, of which 7 were waited for; matrix products, arithmetic and copies ran while one was open for 8% of the time, Pallas kernels for 14%

profile of v3, /device:TPU:1, one launch (start us, length us, event | category | flops | bytes accessed | tf_op | source)
XLA Modules:
  0.0 159.6 jit_solution(5672444815435006242)
XLA Ops:
  0.0 11.3 %shard_map.100 = f32[64,80,128]{2,1,0:T(8,128)} custom-call(s32[8192]{0:T(1024)} %bitcast.75, s32[64]{0:T(128)} %bitcast.81, f32[64,4096]{1,0:T(8,128)} %bitcast.61), custom_call_target="tpu_custom_call" | custom-call | flops 10000000 | bytes 4194304 | tf_op jit(solution)/shard_map/pallas_call | solution.py:64
  11.3 13.2 %all-to-all-start = ((f32[64,80,128]{2,1,0:T(8,128)}), f32[64,80,128]{2,1,0:T(8,128)S(1)}, u32[]{:S(2)}, u32[]{:S(2)}) async-start(f32[64,80,128]{2,1,0:T(8,128)} %shard_map.100), calls=%async_computation | async-start | bytes 5242880 | tf_op jit(solution)/shard_map/all_to_all | solution.py:375
  24.5 2.6 %collective-permute-start = (f32[256,64]{0,1:T(8,128)S(1)}, f32[256,64]{0,1:T(8,128)S(1)}, u32[]{:S(2)}, u32[]{:S(2)}) collective-permute-start(f32[256,64]{0,1:T(8,128)S(1)} %copy-done.7), channel_id=1, source_target_pairs={{0,3},{1,0},{2,1},{3,2},{4,7},{5,4},{6,5},{7,6},{8,11},{9,8},{10,9... | collective-permute-start | bytes 196616 | tf_op jit(solution)/shard_map/ppermute | solution.py:354
  27.1 0.5 collective-permute-start.1
  27.6 0.6 collective-permute-start.2
  28.2 0.2 collective-permute-done
  28.4 3.6 %collective-permute-done.1 = f32[256,64]{0,1:T(8,128)S(1)} collective-permute-done((f32[256,64]{0,1:T(8,128)S(1)}, f32[256,64]{0,1:T(8,128)S(1)}, u32[]{:S(2)}, u32[]{:S(2)}) %collective-permute-start.1) | collective-permute-done | bytes 65568 | tf_op jit(solution)/shard_map/ppermute | solution.py:354
  32.0 0.9 collective-permute-done.2
  32.9 1.5 collective-permute-start.5
  34.3 1.9 %collective-permute-start.6 = (f32[64,4096]{1,0:T(8,128)}, f32[64,4096]{1,0:T(8,128)}, u32[]{:S(2)}, u32[]{:S(2)}) collective-permute-start(f32[64,4096]{1,0:T(8,128)} %bitcast.64), channel_id=1, source_target_pairs={{0,3},{1,0},{2,1},{3,2},{4,7},{5,4},{6,5},{7,6},{8,11},{9,8},{10,9... | collective-permute-start | bytes 3145736 | tf_op jit(solution)/shard_map/ppermute | solution.py:354
  36.2 2.8 %copy-done.2 = f32[1,96,128,128]{3,2,1,0:T(8,128)S(1)} copy-done((f32[1,96,128,128]{3,2,1,0:T(8,128)S(1)}, f32[1,96,128,128]{3,2,1,0:T(8,128)}, u32[]{:S(2)}) %copy-start.2) | copy-done | bytes 6291480
  39.0 2.4 %shard_map.101 = (bf16[96,128,256]{2,1,0:T(8,128)(2,1)S(1)}, s32[96]{0:T(128)S(1)}) custom-call(s32[96]{0:T(128)S(1)} %bitcast.59, s32[96]{0:T(128)S(1)} %bitcast.60, f32[96,128,128]{2,1,0:T(8,128)S(1)} %bitcast.57), custom_call_target="tpu_custom_call" | custom-call | flops 10000000 | bytes 12582912 | tf_op jit(solution)/shard_map/pallas_call | solution.py:104
  41.4 2.6 %copy-done = bf16[96,128,256]{2,1,0:T(8,128)(2,1)} copy-done((bf16[96,128,256]{2,1,0:T(8,128)(2,1)}, bf16[96,128,256]{2,1,0:T(8,128)(2,1)S(1)}, u32[]{:S(2)}) %copy-start) | copy-done | bytes 6291480
  44.0 41.5 %all-to-all-done.mirror_ref = f32[64,80,128]{2,1,0:T(8,128)S(1)} async-done(((f32[64,80,128]{2,1,0:T(8,128)}), f32[64,80,128]{2,1,0:T(8,128)S(1)}, u32[]{:S(2)}, u32[]{:S(2)}) %all-to-all-start) | async-done | bytes 2621472 | tf_op jit(solution)/shard_map/all_to_all | solution.py:375
  85.6 2.1 %collective-permute-start.3 = (f32[64,16,128]{2,1,0:T(8,128)S(1)}, f32[64,16,128]{2,1,0:T(8,128)}, u32[]{:S(2)}, u32[]{:S(2)}) collective-permute-start(f32[64,16,128]{2,1,0:T(8,128)S(1)} %slice.3.own_ref), channel_id=1, source_target_pairs={{0,4},{4,0},{8,12},{12,8},{16,20},{20,16},{24,28},{28,24},{32,36},... | collective-permute-start | bytes 1572872 | tf_op jit(solution)/shard_map/ppermute | solution.py:388
  87.7 5.5 %shard_map.102.before_ref = f32[256,8,128]{2,1,0:T(8,128)S(1)} custom-call(s32[96]{0:T(128)S(1)} %get-tuple-element.43.dst_ref, bf16[96,128,256]{2,1,0:T(8,128)(2,1)} %copy-done, f32[64,80,128]{2,1,0:T(8,128)S(1)} %all-to-all-done.mirror_ref), custom_call_target="tpu_custom_call" | custom-call | flops 1000000000 | bytes 10485760 | tf_op jit(solution)/shard_map/pallas_call | solution.py:181
  93.3 4.8 %shard_map.103 = f32[256,8,128]{2,1,0:T(8,128)} custom-call(s32[96]{0:T(128)S(1)} %get-tuple-element.43.dst_ref, s32[1]{0:T(128)} %bitcast.6.side_ref, bf16[96,128,256]{2,1,0:T(8,128)(2,1)} %copy-done, f32[64,16,128]{2,1,0:T(8,128)S(1)} %slice.3.own_ref, f32[64,16,128]{2,1,0:T(8,128)} %collective-permute-done.3.other_ref, ...), custom_call_target="tpu_custom_call" | custom-call | flops 1000000000 | bytes 6291456 | tf_op jit(solution)/shard_map/pallas_call | solution.py:243
  98.1 7.5 %all-to-all-start.1 = ((f32[256,8,128]{2,1,0:T(8,128)}), f32[256,8,128]{2,1,0:T(8,128)S(1)}, u32[]{:S(2)}, u32[]{:S(2)}) async-start(f32[256,8,128]{2,1,0:T(8,128)} %shard_map.103), calls=%async_computation.1 | async-start | bytes 2097152 | tf_op jit(solution)/shard_map/all_to_all | solution.py:395
  105.7 0.1 reshape.38
  106.2 0.1 pad_bitcast_fusion.1
  106.3 0.1 pad_bitcast_fusion.3
  106.4 0.1 pad_bitcast_fusion.5
  106.5 0.1 pad_bitcast_fusion.7
  106.7 1.1 pad_maximum_fusion.weights_ref
  107.8 2.9 %shard_map.104.weights_ref = bf16[4,1024,256]{2,1,0:T(8,128)(2,1)} custom-call(f32[4,512,128]{2,1,0:T(8,128)} %pad_maximum_fusion.weights_ref), custom_call_target="tpu_custom_call" | custom-call | tf_op jit(solution)/shard_map/pallas_call | solution.py:274
  110.8 0.6 dynamic-slice_bitcast_fusion
  111.4 0.2 copy.30
  111.5 0.8 reshape.44
  112.3 0.2 copy.29
  112.5 0.8 reshape.43
  113.2 0.2 copy.31
  113.4 0.2 reshape.45.rows_ref
  113.6 1.0 copy.32
  114.6 0.2 reshape.46.rows_ref
  114.7 0.7 pad_add_fusion.rows_ref
  115.4 0.1 constant_dynamic-slice_fusion.3
  115.6 5.8 %fusion.refs_3_ = f32[64,4096]{1,0:T(8,128)} fusion(f32[64,4096]{1,0:T(8,128)} %collective-permute-done.6, f32[64,4096]{1,0:T(8,128)} %collective-permute-done.5, f32[64,4096]{1,0:T(8,128)} %collective-permute-done.4, f32[64,4096]{1,0:T(8,128)} %bitcast.65, f32[64,64]{0,1:T(8,128)S(1)} %bitcast.77, f32[64,64]{0,1:T(8,128)S(1)} %bitcast.78, ...), kind=kOutput, calls=%fused_computation | convolution fusion | flops 808501248 | bytes 5308416 | tf_op jit(solution)/shard_map/dot_general | solution.py:401
  121.4 15.2 %all-to-all-done.1 = f32[256,8,128]{2,1,0:T(8,128)S(1)} async-done(((f32[256,8,128]{2,1,0:T(8,128)}), f32[256,8,128]{2,1,0:T(8,128)S(1)}, u32[]{:S(2)}, u32[]{:S(2)}) %all-to-all-start.1) | async-done | bytes 1048608 | tf_op jit(solution)/shard_map/all_to_all | solution.py:395
  136.5 1.9 %shard_map.105 = (f32[512,128]{1,0:T(8,128)S(1)}, f32[512,128]{1,0:T(8,128)}, f32[512,128]{1,0:T(8,128)S(1)}, f32[512,128]{1,0:T(8,128)}) custom-call(f32[64,4,8,128]{3,2,1,0:T(8,128)S(1)} %bitcast.58, bf16[4,1024,256]{2,1,0:T(8,128)(2,1)S(1)} %copy-done.1), custom_call_target="tpu_custom_call" | custom-call | flops 10000000 | bytes 16777216 | tf_op jit(solution)/shard_map/pallas_call | solution.py:296
  138.5 0.5 collective-permute-start.7
  139.0 2.2 %collective-permute-start.9 = (f32[512,128]{1,0:T(8,128)}, f32[512,128]{1,0:T(8,128)S(1)}, u32[]{:S(2)}, u32[]{:S(2)}) collective-permute-start(f32[512,128]{1,0:T(8,128)} %get-tuple-element.71), channel_id=1, source_target_pairs={{0,3},{1,0},{2,1},{3,2},{4,7},{5,4},{6,5},{7,6},{8,11},{9,8},{10,9... | collective-permute-start | bytes 786440 | tf_op jit(solution)/shard_map/ppermute | solution.py:354
  141.2 3.2 %shard_map.106.refs_1_ = f32[64,4096]{1,0:T(8,128)S(1)} custom-call(s32[1024]{0:T(1024)S(1)} %reshape.45.rows_ref, f32[512,128]{1,0:T(8,128)S(1)} %get-tuple-element.68.refs_0_), custom_call_target="tpu_custom_call" | custom-call | flops 10000000 | bytes 16777216 | tf_op jit(solution)/shard_map/pallas_call | solution.py:342
  144.3 1.1 collective-permute-start.8
  145.4 0.1 copy.33.refs_4_
  145.5 1.7 %collective-permute-done.9.refs_0_ = f32[512,128]{1,0:T(8,128)S(1)} collective-permute-done((f32[512,128]{1,0:T(8,128)}, f32[512,128]{1,0:T(8,128)S(1)}, u32[]{:S(2)}, u32[]{:S(2)}) %collective-permute-start.9) | collective-permute-done | bytes 262176 | tf_op jit(solution)/shard_map/ppermute | solution.py:354
  147.2 3.2 %shard_map.107.refs_2_ = f32[64,4096]{1,0:T(8,128)S(1)} custom-call(s32[1024]{0:T(1024)S(1)} %reshape.46.rows_ref, f32[512,128]{1,0:T(8,128)S(1)} %collective-permute-done.9.refs_0_, f32[64,4096]{1,0:T(8,128)S(1)} %shard_map.106.refs_1_), custom_call_target="tpu_custom_call" | custom-call | flops 10000000 | bytes 16777216 | tf_op jit(solution)/shard_map/pallas_call | solution.py:342
  150.4 2.9 %collective-permute-done.8.refs_1_ = f32[512,128]{1,0:T(8,128)S(1)} collective-permute-done((f32[512,128]{1,0:T(8,128)S(1)}, f32[512,128]{1,0:T(8,128)S(1)}, u32[]{:S(2)}, u32[]{:S(2)}) %collective-permute-start.8) | collective-permute-done | bytes 262176 | tf_op jit(solution)/shard_map/ppermute | solution.py:354
  153.3 6.3 %shard_map.108 = f32[64,4096]{1,0:T(8,128)} custom-call(s32[2048]{0:T(1024)S(1)} %pad_add_fusion.rows_ref, f32[512,128]{1,0:T(8,128)S(1)} %collective-permute-done.7.refs_0_, f32[512,128]{1,0:T(8,128)S(1)} %collective-permute-done.8.refs_1_, f32[64,4096]{1,0:T(8,128)S(1)} %shard_map.107.refs_2_, f32[64,4096]{1,0:T(8,128)S(1)} %copy-done.3, ...), custom_call_target="tpu_custom_call" | custom-call | flops 10000000 | bytes 16777216 | tf_op jit(solution)/shard_map/pallas_call | solution.py:342
  (38 shorter events, 0.6 us)
Async XLA Ops:
  0.0 24.5 %copy-start.7 = (f32[256,64]{0,1:T(8,128)S(1)}, f32[256,64]{0,1:T(8,128)}, u32[]{:S(2)}) copy-start(f32[256,64]{0,1:T(8,128)} %param.12) | copy-start | bytes 196612
  0.0 36.2 %copy-start.4 = (s32[1,96]{1,0:T(1,128)S(1)}, s32[1,96]{1,0:T(1,128)}, u32[]{:S(2)}) copy-start(s32[1,96]{1,0:T(1,128)} %param.17) | copy-start | bytes 1156
  0.0 36.2 %copy-start.5 = (s32[1,96]{1,0:T(1,128)S(1)}, s32[1,96]{1,0:T(1,128)}, u32[]{:S(2)}) copy-start(s32[1,96]{1,0:T(1,128)} %param.18) | copy-start | bytes 1156
  11.3 74.2 %all-to-all-start = ((f32[64,80,128]{2,1,0:T(8,128)}), f32[64,80,128]{2,1,0:T(8,128)S(1)}, u32[]{:S(2)}, u32[]{:S(2)}) async-start(f32[64,80,128]{2,1,0:T(8,128)} %shard_map.100), calls=%async_computation | async-start | bytes 5242880 | tf_op jit(solution)/shard_map/all_to_all | solution.py:375
  24.5 3.9 %collective-permute-start = (f32[256,64]{0,1:T(8,128)S(1)}, f32[256,64]{0,1:T(8,128)S(1)}, u32[]{:S(2)}, u32[]{:S(2)}) collective-permute-start(f32[256,64]{0,1:T(8,128)S(1)} %copy-done.7), channel_id=1, source_target_pairs={{0,3},{1,0},{2,1},{3,2},{4,7},{5,4},{6,5},{7,6},{8,11},{9,8},{10,9... | collective-permute-start | bytes 196616 | tf_op jit(solution)/shard_map/ppermute | solution.py:354
  27.1 4.9 %collective-permute-start.1 = (f32[256,64]{0,1:T(8,128)S(1)}, f32[256,64]{0,1:T(8,128)S(1)}, u32[]{:S(2)}, u32[]{:S(2)}) collective-permute-start(f32[256,64]{0,1:T(8,128)S(1)} %copy-done.7), channel_id=1, source_target_pairs={{0,2},{1,3},{2,0},{3,1},{4,6},{5,7},{6,4},{7,5},{8,10},{9,11},{10,... | collective-permute-start | bytes 196616 | tf_op jit(solution)/shard_map/ppermute | solution.py:354
  27.6 5.3 %collective-permute-start.2 = (f32[256,64]{0,1:T(8,128)S(1)}, f32[256,64]{0,1:T(8,128)S(1)}, u32[]{:S(2)}, u32[]{:S(2)}) collective-permute-start(f32[256,64]{0,1:T(8,128)S(1)} %copy-done.7), channel_id=1, source_target_pairs={{0,1},{1,2},{2,3},{3,0},{4,5},{5,6},{6,7},{7,4},{8,9},{9,10},{10,1... | collective-permute-start | bytes 196616 | tf_op jit(solution)/shard_map/ppermute | solution.py:354
  32.9 52.7 %copy-start.8 = (f32[256,64]{0,1:T(8,128)}, f32[256,64]{0,1:T(8,128)S(1)}, u32[]{:S(2)}) copy-start(f32[256,64]{0,1:T(8,128)S(1)} %collective-permute-done.2) | copy-start | bytes 196612
  32.9 65.2 %collective-permute-start.4 = (f32[64,4096]{1,0:T(8,128)}, f32[64,4096]{1,0:T(8,128)}, u32[]{:S(2)}, u32[]{:S(2)}) collective-permute-start(f32[64,4096]{1,0:T(8,128)} %bitcast.62), channel_id=1, source_target_pairs={{0,1},{1,2},{2,3},{3,0},{4,5},{5,6},{6,7},{7,4},{8,9},{9,10},{10,1... | collective-permute-start | bytes 3145736 | tf_op jit(solution)/shard_map/ppermute | solution.py:354
  32.9 65.2 %collective-permute-start.5 = (f32[64,4096]{1,0:T(8,128)}, f32[64,4096]{1,0:T(8,128)}, u32[]{:S(2)}, u32[]{:S(2)}) collective-permute-start(f32[64,4096]{1,0:T(8,128)} %bitcast.63), channel_id=1, source_target_pairs={{0,2},{1,3},{2,0},{3,1},{4,6},{5,7},{6,4},{7,5},{8,10},{9,11},{10,... | collective-permute-start | bytes 3145736 | tf_op jit(solution)/shard_map/ppermute | solution.py:354
  34.3 63.8 %collective-permute-start.6 = (f32[64,4096]{1,0:T(8,128)}, f32[64,4096]{1,0:T(8,128)}, u32[]{:S(2)}, u32[]{:S(2)}) collective-permute-start(f32[64,4096]{1,0:T(8,128)} %bitcast.64), channel_id=1, source_target_pairs={{0,3},{1,0},{2,1},{3,2},{4,7},{5,4},{6,5},{7,6},{8,11},{9,8},{10,9... | collective-permute-start | bytes 3145736 | tf_op jit(solution)/shard_map/ppermute | solution.py:354
  36.2 2.8 %copy-start.2 = (f32[1,96,128,128]{3,2,1,0:T(8,128)S(1)}, f32[1,96,128,128]{3,2,1,0:T(8,128)}, u32[]{:S(2)}) copy-start(f32[1,96,128,128]{3,2,1,0:T(8,128)} %param.19) | copy-start | bytes 18874372
  41.4 2.6 %copy-start = (bf16[96,128,256]{2,1,0:T(8,128)(2,1)}, bf16[96,128,256]{2,1,0:T(8,128)(2,1)S(1)}, u32[]{:S(2)}) copy-start(bf16[96,128,256]{2,1,0:T(8,128)(2,1)S(1)} %get-tuple-element.44.tiles_hbm) | copy-start | bytes 18874372
  85.6 7.7 %collective-permute-start.3 = (f32[64,16,128]{2,1,0:T(8,128)S(1)}, f32[64,16,128]{2,1,0:T(8,128)}, u32[]{:S(2)}, u32[]{:S(2)}) collective-permute-start(f32[64,16,128]{2,1,0:T(8,128)S(1)} %slice.3.own_ref), channel_id=1, source_target_pairs={{0,4},{4,0},{8,12},{12,8},{16,20},{20,16},{24,28},{28,24},{32,36},... | collective-permute-start | bytes 1572872 | tf_op jit(solution)/shard_map/ppermute | solution.py:388
  93.3 12.4 %copy-start.6 = (f32[256,64]{0,1:T(8,128)S(1)}, f32[256,64]{0,1:T(8,128)}, u32[]{:S(2)}) copy-start(f32[256,64]{0,1:T(8,128)} %param.11) | copy-start | bytes 196612
  93.3 12.5 %copy-start.9 = (f32[256,64]{0,1:T(8,128)S(1)}, f32[256,64]{0,1:T(8,128)}, u32[]{:S(2)}) copy-start(f32[256,64]{0,1:T(8,128)} %copy-done.8) | copy-start | bytes 196612
  98.1 38.4 %all-to-all-start.1 = ((f32[256,8,128]{2,1,0:T(8,128)}), f32[256,8,128]{2,1,0:T(8,128)S(1)}, u32[]{:S(2)}, u32[]{:S(2)}) async-start(f32[256,8,128]{2,1,0:T(8,128)} %shard_map.103), calls=%async_computation.1 | async-start | bytes 2097152 | tf_op jit(solution)/shard_map/all_to_all | solution.py:395
  106.3 4.4 %copy-start.10 = (s32[1,64,64]{2,1,0:T(8,128)S(1)}, s32[1,64,64]{2,1,0:T(8,128)}, u32[]{:S(2)}) copy-start(s32[1,64,64]{2,1,0:T(8,128)} %param.16) | copy-start | bytes 49156
  113.4 23.1 %copy-start.1 = (bf16[4,1024,256]{2,1,0:T(8,128)(2,1)S(1)}, bf16[4,1024,256]{2,1,0:T(8,128)(2,1)}, u32[]{:S(2)}) copy-start(bf16[4,1024,256]{2,1,0:T(8,128)(2,1)} %shard_map.104.weights_ref) | copy-start | bytes 6291460
  115.6 29.8 %copy-start.11 = (f32[64]{0:T(128)S(1)}, f32[64]{0:T(128)}, u32[]{:S(2)}) copy-start(f32[64]{0:T(128)} %param.13) | copy-start | bytes 772
  138.5 14.8 %copy-start.3 = (f32[64,4096]{1,0:T(8,128)S(1)}, f32[64,4096]{1,0:T(8,128)}, u32[]{:S(2)}) copy-start(f32[64,4096]{1,0:T(8,128)} %fusion.refs_3_) | copy-start | bytes 3145732
  138.5 12.0 %collective-permute-start.7 = (f32[512,128]{1,0:T(8,128)}, f32[512,128]{1,0:T(8,128)S(1)}, u32[]{:S(2)}, u32[]{:S(2)}) collective-permute-start(f32[512,128]{1,0:T(8,128)} %get-tuple-element.65), channel_id=1, source_target_pairs={{0,1},{1,2},{2,3},{3,0},{4,5},{5,6},{6,7},{7,4},{8,9},{9,10},{10,1... | collective-permute-start | bytes 786440 | tf_op jit(solution)/shard_map/ppermute | solution.py:354
  139.0 8.2 %collective-permute-start.9 = (f32[512,128]{1,0:T(8,128)}, f32[512,128]{1,0:T(8,128)S(1)}, u32[]{:S(2)}, u32[]{:S(2)}) collective-permute-start(f32[512,128]{1,0:T(8,128)} %get-tuple-element.71), channel_id=1, source_target_pairs={{0,3},{1,0},{2,1},{3,2},{4,7},{5,4},{6,5},{7,6},{8,11},{9,8},{10,9... | collective-permute-start | bytes 786440 | tf_op jit(solution)/shard_map/ppermute | solution.py:354
  144.3 9.0 %collective-permute-start.8 = (f32[512,128]{1,0:T(8,128)S(1)}, f32[512,128]{1,0:T(8,128)S(1)}, u32[]{:S(2)}, u32[]{:S(2)}) collective-permute-start(f32[512,128]{1,0:T(8,128)S(1)} %get-tuple-element.69), channel_id=1, source_target_pairs={{0,2},{1,3},{2,0},{3,1},{4,6},{5,7},{6,4},{7,5},{8,10},{9,11},{10,... | collective-permute-start | bytes 786440 | tf_op jit(solution)/shard_map/ppermute | solution.py:354

commit v4 on v3

--- a/solution.py
+++ b/solution.py
@@ -8,7 +8,7 @@
 from jax.sharding import PartitionSpec as P
 
 LANES = 128
-KERNEL_VMEM = 50 * 2**20
+KERNEL_VMEM = 48 * 2**20
 HALF = 64
 
 
@@ -142,7 +142,9 @@
     return jnp.where(left_half((8, LANES)), first, second)
 
 
-def listed_kernel(dst_ref, tiles_hbm, mirror_ref, out_ref, tiles_ref, acc_ref, sems, *, first, rows):
+def listed_kernel(
+    dst_ref, tiles_hbm, mirror_ref, out_ref, hub_tiles_ref, tiles_ref, acc_ref, sems, hub_sem, *, first, rows
+):
     chunks = sems.shape[0]
     count = tiles_ref.shape[0] // chunks
 
@@ -151,16 +153,13 @@
             tiles_hbm.at[pl.ds(first + c * count, count)], tiles_ref.at[pl.ds(c * count, count)], sems.at[c]
         )
 
-    ahead = 2
-    for c in range(ahead):
+    for c in range(chunks):
         fetch(c).start()
+    hubs = pltpu.make_async_copy(tiles_hbm.at[pl.ds(0, first)], hub_tiles_ref, hub_sem)
+    hubs.start()
     acc_ref[...] = jnp.zeros_like(acc_ref)
 
     def chunk(c, carry):
-        @pl.when(c + ahead < chunks)
-        def _():
-            fetch(c + ahead).start()
-
         fetch(c).wait()
         for i in range(count):
             tile = c * count + i
@@ -172,6 +171,7 @@
     for block in range(acc_ref.shape[0]):
         for part in range(8):
             out_ref[block * 8 + part] = packed_sums(acc_ref, block, part)
+    hubs.wait()
 
 
 def listed_tiles(split_vals, mirror, order, rows, first, dst_blocks):
@@ -181,37 +181,33 @@
     return pl.pallas_call(
         functools.partial(listed_kernel, first=first, rows=rows),
         in_specs=[pl.BlockSpec(memory_space=pltpu.SMEM), pl.BlockSpec(memory_space=pltpu.HBM), whole],
-        out_specs=whole,
+        out_specs=[whole, whole],
         scratch_shapes=[
             pltpu.VMEM((count, size, 2 * size), jnp.bfloat16),
             pltpu.VMEM((dst_blocks, size, LANES), jnp.float32),
             pltpu.SemaphoreType.DMA((8,)),
+            pltpu.SemaphoreType.DMA,
         ],
-        out_shape=jax.ShapeDtypeStruct((dst_blocks * 8, 8, LANES), jnp.float32),
+        out_shape=[
+            jax.ShapeDtypeStruct((dst_blocks * 8, 8, LANES), jnp.float32),
+            jax.ShapeDtypeStruct((first, size, 2 * size), jnp.bfloat16),
+        ],
         compiler_params=pltpu.CompilerParams(vmem_limit_bytes=KERNEL_VMEM),
         cost_estimate=pl.CostEstimate(flops=10**9, bytes_accessed=10 * 2**20, transcendentals=0),
     )(order, split_vals, mirror)
 
 
 def hub_kernel(
-    dst_ref, side_ref, tiles_hbm, own_ref, other_ref, before_ref, out_hbm, tiles_ref, hubs_ref, acc_ref, out_ref, sems, out_sems
+    dst_ref, side_ref, tiles_ref, own_ref, other_ref, before_ref, out_hbm, hubs_ref, acc_ref, out_ref, out_sems
 ):
-    chunks = sems.shape[0]
-    count = tiles_ref.shape[0] // chunks
+    count = 8
+    chunks = tiles_ref.shape[0] // count
     side = side_ref[0]
-
-    def fetch(c):
-        part = pl.ds(c * count, count)
-        return pltpu.make_async_copy(tiles_hbm.at[part], tiles_ref.at[part], sems.at[c])
-
-    for c in range(chunks):
-        fetch(c).start()
     acc_ref[...] = jnp.zeros_like(acc_ref)
     hubs_ref[side] = own_ref[...]
     hubs_ref[1 - side] = other_ref[...]
 
     def chunk(c, carry):
-        fetch(c).wait()
         for i in range(count):
             tile = c * count + i
             pieces = []
@@ -242,15 +238,12 @@
     scalars = pl.BlockSpec(memory_space=pltpu.SMEM)
     return pl.pallas_call(
         hub_kernel,
-        in_specs=[scalars, scalars, pl.BlockSpec(memory_space=pltpu.HBM)]
-        + [pl.BlockSpec(memory_space=pltpu.VMEM)] * 3,
+        in_specs=[scalars, scalars] + [pl.BlockSpec(memory_space=pltpu.VMEM)] * 4,
         out_specs=pl.BlockSpec(memory_space=pltpu.HBM),
         scratch_shapes=[
-            pltpu.VMEM((own.shape[0] // 2, size, 2 * size), jnp.bfloat16),
             pltpu.VMEM((2,) + own.shape, jnp.float32),
             pltpu.VMEM((blocks, size, LANES), jnp.float32),
             pltpu.VMEM(before.shape, jnp.float32),
-            pltpu.SemaphoreType.DMA((4,)),
             pltpu.SemaphoreType.DMA((4,)),
         ],
         out_shape=jax.ShapeDtypeStruct(before.shape, jnp.float32),
@@ -296,7 +289,7 @@
     return pl.pallas_call(
         functools.partial(slots_kernel, targets=targets),
         out_shape=[jax.ShapeDtypeStruct((peers * 8, LANES), jnp.float32)] * len(targets),
-        compiler_params=pltpu.CompilerParams(vmem_limit_bytes=24 * 2**20),
+        compiler_params=pltpu.CompilerParams(vmem_limit_bytes=12 * 2**20),
         cost_estimate=pl.CostEstimate(flops=10**7, bytes_accessed=16 * 2**20, transcendentals=0),
     )(slots, weights)
 
@@ -345,7 +338,7 @@
         out_specs=vmem,
         out_shape=jax.ShapeDtypeStruct((HALF, row_count), jnp.float32),
         scratch_shapes=[pltpu.VMEM((row_count + 8, LANES), jnp.float32)] * 4,
-        compiler_params=pltpu.CompilerParams(vmem_limit_bytes=16 * 2**20),
+        compiler_params=pltpu.CompilerParams(vmem_limit_bytes=13 * 2**20),
         cost_estimate=pl.CostEstimate(flops=10**7, bytes_accessed=16 * 2**20, transcendentals=0),
     )(rows, *parts, *bases, *([bias] if last else []))
 
@@ -387,8 +380,8 @@
     hub_half = mirror[:, rows:]
     hub_other = lax.ppermute(hub_half, "dom", [(i, i ^ 1) for i in range(peers)])
     side = (lax.axis_index("dom") % 2).astype(jnp.int32).reshape(1)
-    partial = listed_tiles(split_vals, mirror, tile_order, rows, hub_count, peers * ret // slot)
-    partial = hub_tiles(split_vals, hub_half, hub_other, partial, tile_order, side)
+    partial, hub_vals = listed_tiles(split_vals, mirror, tile_order, rows, hub_count, peers * ret // slot)
+    partial = hub_tiles(hub_vals, hub_half, hub_other, partial, tile_order, side)
     partial, blocks, neighbours, w_self, ret_rows = lax.optimization_barrier(
         (partial, blocks, neighbours, w_self, ret_rows)
     )
@@ -421,7 +414,7 @@
     ]
     far = feat // 2
     near = [d for d in range(feat - 1, 0, -1) if d != far]
-    tail = (*near[1:], far)
+    tail = (far, *near)
     tail_rows = jnp.concatenate([order[d] for d in tail])
     bias = out_bias[:, None]
     row_count = features.shape[0]
@@ -430,12 +423,9 @@
     )
     slots = slots.reshape(peers, feat, 8, LANES)
     parts = project_slots(slots, weights, range(feat))
-    moved = {d: shifted(parts[d], feat, d) for d in near}
-    total = scatter_rows([parts[0]], order[0], [], row_count)
-    last, total = lax.optimization_barrier((parts[far], total))
-    moved[far] = shifted(last, feat, far)
-    total = scatter_rows([moved[near[0]]], order[near[0]], [total], row_count)
-    return scatter_rows([moved[d] for d in tail], tail_rows, [total, own], row_count, bias).T
+    moved = {d: shifted(parts[d], feat, d) for d in tail}
+    total = scatter_rows([parts[0]], order[0], [own], row_count)
+    return scatter_rows([moved[d] for d in tail], tail_rows, [total], row_count, bias).T
 
 
 def solution(mesh):

time: 163 us -> 161 us (0.988); the launches traced: 160 us -> 160 us
  waiting for transfers between devices: 65.9 us -> 69.5 us
  Pallas kernels: 41.5 us -> 38.5 us
    ppermute x9, waiting for transfers between devices: 9.25 us -> 12.2 us  [shifted(): lax.ppermute(value, 'feat', [(i, (i + step) % count) for i in range(count)])]
    pallas_call x3 -> x2, Pallas kernels: 12.7 us -> 11 us  [scatter_rows(): pl.pallas_call(functools.partial(scatter_kernel, blocks=len(parts), bases...]
    unnamed x24 -> x20, local copies, waits for them, and re-layouts: 5.46 us -> 6.66 us
  transfers between devices with their start and end apart: 12 -> 12, of which waited for: 7 -> 8; matrix products, arithmetic and copies ran while one was open for 8% -> 8% of each run, Pallas kernels for 14% -> 11%
where the time goes in v4:
time: 161 us; the launch traced here: 160 us
  waiting for transfers between devices  69.5 us (43%)
  Pallas kernels  38.5 us (24%)
  starting transfers between devices  33.3 us (21%)
  local copies, waits for them, and re-layouts  11 us (7%)
  matrix products  5.79 us (4%)
  other arithmetic  1.99 us (1%)
    all_to_all x1, waiting for transfers between devices, per_device(): lax.all_to_all(outgoing, 'dom', split_axis=0, concat_axis=0, tiled=True)  41.5 us
    all_to_all x1, waiting for transfers between devices, per_device(): lax.all_to_all(partial, ('dom', 'feat'), split_axis=0, concat_axis=0, til...  15.8 us
    all_to_all x1, starting transfers between devices, per_device(): lax.all_to_all(outgoing, 'dom', split_axis=0, concat_axis=0, tiled=True)  13.2 us
    ppermute x9, waiting for transfers between devices, shifted(): lax.ppermute(value, 'feat', [(i, (i + step) % count) for i in range(count)])  12.2 us
    pallas_call x1, Pallas kernels, gather_rows(): pl.pallas_call(functools.partial(gather_kernel, peers=peers, rows=rows, h...  11.3 us
    pallas_call x2, Pallas kernels, scatter_rows(): pl.pallas_call(functools.partial(scatter_kernel, blocks=len(parts), bases...  11 us
    ppermute x9, starting transfers between devices, shifted(): lax.ppermute(value, 'feat', [(i, (i + step) % count) for i in range(count)])  10.5 us
    all_to_all x1, starting transfers between devices, per_device(): lax.all_to_all(partial, ('dom', 'feat'), split_axis=0, concat_axis=0, til...  7.48 us
  transfers between devices with their start and end apart: 12, of which 8 were waited for; matrix products, arithmetic and copies ran while one was open for 8% of the time, Pallas kernels for 11%

profile of v4, /device:TPU:1, one launch (start us, length us, event | category | flops | bytes accessed | tf_op | source)
XLA Modules:
  0.0 160.5 jit_solution(6927206196670818682)
XLA Ops:
  0.0 11.3 %shard_map.100 = f32[64,80,128]{2,1,0:T(8,128)} custom-call(s32[8192]{0:T(1024)} %bitcast.75, s32[64]{0:T(128)} %bitcast.81, f32[64,4096]{1,0:T(8,128)} %bitcast.61), custom_call_target="tpu_custom_call" | custom-call | flops 10000000 | bytes 4194304 | tf_op jit(solution)/shard_map/pallas_call | solution.py:64
  11.3 13.2 %all-to-all-start = ((f32[64,80,128]{2,1,0:T(8,128)}), f32[64,80,128]{2,1,0:T(8,128)S(1)}, u32[]{:S(2)}, u32[]{:S(2)}) async-start(f32[64,80,128]{2,1,0:T(8,128)} %shard_map.100), calls=%async_computation | async-start | bytes 5242880 | tf_op jit(solution)/shard_map/all_to_all | solution.py:368
  24.5 2.6 %collective-permute-start = (f32[256,64]{0,1:T(8,128)S(1)}, f32[256,64]{0,1:T(8,128)S(1)}, u32[]{:S(2)}, u32[]{:S(2)}) collective-permute-start(f32[256,64]{0,1:T(8,128)S(1)} %copy-done.6), channel_id=1, source_target_pairs={{0,3},{1,0},{2,1},{3,2},{4,7},{5,4},{6,5},{7,6},{8,11},{9,8},{10,9... | collective-permute-start | bytes 196616 | tf_op jit(solution)/shard_map/ppermute | solution.py:347
  27.1 0.5 collective-permute-start.1
  27.6 0.6 collective-permute-start.2
  28.2 0.2 collective-permute-done
  28.4 3.6 %collective-permute-done.1 = f32[256,64]{0,1:T(8,128)S(1)} collective-permute-done((f32[256,64]{0,1:T(8,128)S(1)}, f32[256,64]{0,1:T(8,128)S(1)}, u32[]{:S(2)}, u32[]{:S(2)}) %collective-permute-start.1) | collective-permute-done | bytes 65568 | tf_op jit(solution)/shard_map/ppermute | solution.py:347
  32.0 0.9 collective-permute-done.2
  32.9 1.5 collective-permute-start.5
  34.4 1.9 %collective-permute-start.6 = (f32[64,4096]{1,0:T(8,128)}, f32[64,4096]{1,0:T(8,128)}, u32[]{:S(2)}, u32[]{:S(2)}) collective-permute-start(f32[64,4096]{1,0:T(8,128)} %bitcast.64), channel_id=1, source_target_pairs={{0,3},{1,0},{2,1},{3,2},{4,7},{5,4},{6,5},{7,6},{8,11},{9,8},{10,9... | collective-permute-start | bytes 3145736 | tf_op jit(solution)/shard_map/ppermute | solution.py:347
  36.3 2.8 %copy-done.2 = f32[1,96,128,128]{3,2,1,0:T(8,128)S(1)} copy-done((f32[1,96,128,128]{3,2,1,0:T(8,128)S(1)}, f32[1,96,128,128]{3,2,1,0:T(8,128)}, u32[]{:S(2)}) %copy-start.2) | copy-done | bytes 6291480
  39.0 2.4 %shard_map.101 = (bf16[96,128,256]{2,1,0:T(8,128)(2,1)S(1)}, s32[96]{0:T(128)S(1)}) custom-call(s32[96]{0:T(128)S(1)} %bitcast.59, s32[96]{0:T(128)S(1)} %bitcast.60, f32[96,128,128]{2,1,0:T(8,128)S(1)} %bitcast.57), custom_call_target="tpu_custom_call" | custom-call | flops 10000000 | bytes 12582912 | tf_op jit(solution)/shard_map/pallas_call | solution.py:104
  41.4 2.6 %copy-done.1 = bf16[96,128,256]{2,1,0:T(8,128)(2,1)} copy-done((bf16[96,128,256]{2,1,0:T(8,128)(2,1)}, bf16[96,128,256]{2,1,0:T(8,128)(2,1)S(1)}, u32[]{:S(2)}) %copy-start.1) | copy-done | bytes 6291480
  44.0 41.5 %all-to-all-done.mirror_ref = f32[64,80,128]{2,1,0:T(8,128)S(1)} async-done(((f32[64,80,128]{2,1,0:T(8,128)}), f32[64,80,128]{2,1,0:T(8,128)S(1)}, u32[]{:S(2)}, u32[]{:S(2)}) %all-to-all-start) | async-done | bytes 2621472 | tf_op jit(solution)/shard_map/all_to_all | solution.py:368
  85.6 2.1 %collective-permute-start.3 = (f32[64,16,128]{2,1,0:T(8,128)S(1)}, f32[64,16,128]{2,1,0:T(8,128)}, u32[]{:S(2)}, u32[]{:S(2)}) collective-permute-start(f32[64,16,128]{2,1,0:T(8,128)S(1)} %slice.3.own_ref), channel_id=1, source_target_pairs={{0,4},{4,0},{8,12},{12,8},{16,20},{20,16},{24,28},{28,24},{32,36},... | collective-permute-start | bytes 1572872 | tf_op jit(solution)/shard_map/ppermute | solution.py:381
  87.7 4.9 %shard_map.102 = (f32[256,8,128]{2,1,0:T(8,128)S(1)}, bf16[32,128,256]{2,1,0:T(8,128)(2,1)S(1)}) custom-call(s32[96]{0:T(128)S(1)} %get-tuple-element.42.dst_ref, bf16[96,128,256]{2,1,0:T(8,128)(2,1)} %copy-done.1, f32[64,80,128]{2,1,0:T(8,128)S(1)} %all-to-all-done.mirror_ref), custom_call_target="tpu_custom_call" | custom-call | flops 1000000000 | bytes 10485760 | tf_op jit(solution)/shard_map/pallas_call | solution.py:181
  92.7 3.9 %shard_map.103 = f32[256,8,128]{2,1,0:T(8,128)} custom-call(s32[96]{0:T(128)S(1)} %get-tuple-element.42.dst_ref, s32[1]{0:T(128)} %bitcast.6.side_ref, bf16[32,128,256]{2,1,0:T(8,128)(2,1)S(1)} %get-tuple-element.45.tiles_ref, f32[64,16,128]{2,1,0:T(8,128)S(1)} %slice.3.own_ref, f32[64,16,128]{2,1,0:T(8,128)} %collective-permute-done.3.other_ref, ...), custom_call_target="tpu_custom_call" | custom-call | flops 1000000000 | bytes 6291456 | tf_op jit(solution)/shard_map/pallas_call | solution.py:239
  96.6 7.5 %all-to-all-start.1 = ((f32[256,8,128]{2,1,0:T(8,128)}), f32[256,8,128]{2,1,0:T(8,128)S(1)}, u32[]{:S(2)}, u32[]{:S(2)}) async-start(f32[256,8,128]{2,1,0:T(8,128)} %shard_map.103), calls=%async_computation.1 | async-start | bytes 2097152 | tf_op jit(solution)/shard_map/all_to_all | solution.py:388
  104.3 0.2 copy.29
  104.5 0.8 reshape.43
  105.2 0.2 copy.30
  105.4 0.8 reshape.44
  106.2 0.2 copy.31
  106.4 0.8 reshape.45
  107.5 0.1 pad_bitcast_fusion.7
  107.6 0.1 pad_bitcast_fusion.5
  107.7 0.1 pad_bitcast_fusion.3
  107.8 0.1 pad_bitcast_fusion.1
  108.1 1.1 pad_maximum_fusion.weights_ref
  109.1 2.9 %shard_map.104.weights_ref = bf16[4,1024,256]{2,1,0:T(8,128)(2,1)} custom-call(f32[4,512,128]{2,1,0:T(8,128)} %pad_maximum_fusion.weights_ref), custom_call_target="tpu_custom_call" | custom-call | tf_op jit(solution)/shard_map/pallas_call | solution.py:267
  112.0 0.1 reshape.38
  112.1 0.2 copy.32
  112.3 0.2 reshape.46.rows_ref
  112.5 0.9 pad_add_fusion.rows_ref
  113.3 0.1 constant_dynamic-slice_fusion.3
  113.5 5.8 %fusion.refs_1_ = f32[64,4096]{1,0:T(8,128)} fusion(f32[64,4096]{1,0:T(8,128)} %collective-permute-done.6, f32[64,4096]{1,0:T(8,128)} %collective-permute-done.5, f32[64,4096]{1,0:T(8,128)} %collective-permute-done.4, f32[64,4096]{1,0:T(8,128)} %bitcast.65, f32[64,64]{0,1:T(8,128)S(1)} %bitcast.77, f32[64,64]{0,1:T(8,128)S(1)} %bitcast.78, ...), kind=kOutput, calls=%fused_computation | convolution fusion | flops 808501248 | bytes 5308416 | tf_op jit(solution)/shard_map/dot_general | solution.py:394
  119.2 15.8 %all-to-all-done.1 = f32[256,8,128]{2,1,0:T(8,128)S(1)} async-done(((f32[256,8,128]{2,1,0:T(8,128)}), f32[256,8,128]{2,1,0:T(8,128)S(1)}, u32[]{:S(2)}, u32[]{:S(2)}) %all-to-all-start.1) | async-done | bytes 1048608 | tf_op jit(solution)/shard_map/all_to_all | solution.py:388
  135.1 2.0 %shard_map.105 = (f32[512,128]{1,0:T(8,128)S(1)}, f32[512,128]{1,0:T(8,128)}, f32[512,128]{1,0:T(8,128)}, f32[512,128]{1,0:T(8,128)}) custom-call(f32[64,4,8,128]{3,2,1,0:T(8,128)S(1)} %bitcast.58, bf16[4,1024,256]{2,1,0:T(8,128)(2,1)S(1)} %copy-done), custom_call_target="tpu_custom_call" | custom-call | flops 10000000 | bytes 16777216 | tf_op jit(solution)/shard_map/pallas_call | solution.py:289
  137.1 2.0 %collective-permute-start.7 = (f32[512,128]{1,0:T(8,128)}, f32[512,128]{1,0:T(8,128)S(1)}, u32[]{:S(2)}, u32[]{:S(2)}) collective-permute-start(f32[512,128]{1,0:T(8,128)} %get-tuple-element.66), channel_id=1, source_target_pairs={{0,2},{1,3},{2,0},{3,1},{4,6},{5,7},{6,4},{7,5},{8,10},{9,11},{10,... | collective-permute-start | bytes 786440 | tf_op jit(solution)/shard_map/ppermute | solution.py:347
  139.1 0.9 collective-permute-start.8
  140.0 0.6 collective-permute-start.9
  140.6 0.1 copy.33.refs_4_
  140.7 1.2 copy-done.3
  141.9 3.2 %shard_map.106.refs_3_ = f32[64,4096]{1,0:T(8,128)S(1)} custom-call(s32[1024]{0:T(1024)S(1)} %reshape.46.rows_ref, f32[512,128]{1,0:T(8,128)S(1)} %get-tuple-element.70.refs_0_, f32[64,4096]{1,0:T(8,128)S(1)} %copy-done.3), custom_call_target="tpu_custom_call" | custom-call | flops 10000000 | bytes 16777216 | tf_op jit(solution)/shard_map/pallas_call | solution.py:335
  145.1 1.7 %collective-permute-done.7.refs_0_ = f32[512,128]{1,0:T(8,128)S(1)} collective-permute-done((f32[512,128]{1,0:T(8,128)}, f32[512,128]{1,0:T(8,128)S(1)}, u32[]{:S(2)}, u32[]{:S(2)}) %collective-permute-start.7) | collective-permute-done | bytes 262176 | tf_op jit(solution)/shard_map/ppermute | solution.py:347
  146.9 5.1 %collective-permute-done.8.refs_1_ = f32[512,128]{1,0:T(8,128)S(1)} collective-permute-done((f32[512,128]{1,0:T(8,128)}, f32[512,128]{1,0:T(8,128)S(1)}, u32[]{:S(2)}, u32[]{:S(2)}) %collective-permute-start.8) | collective-permute-done | bytes 262176 | tf_op jit(solution)/shard_map/ppermute | solution.py:347
  152.0 0.7 collective-permute-done.9.refs_2_
  152.7 7.8 %shard_map.107 = f32[64,4096]{1,0:T(8,128)} custom-call(s32[3072]{0:T(1024)S(1)} %pad_add_fusion.rows_ref, f32[512,128]{1,0:T(8,128)S(1)} %collective-permute-done.7.refs_0_, f32[512,128]{1,0:T(8,128)S(1)} %collective-permute-done.8.refs_1_, f32[512,128]{1,0:T(8,128)S(1)} %collective-permute-done.9.refs_2_, f32[64,4096]{1,0:T(8,128)S(1)} %shard_map.106.refs_3_, ...), custom_call_target="tpu_custom_call" | custom-call | flops 10000000 | bytes 16777216 | tf_op jit(solution)/shard_map/pallas_call | solution.py:335
  (33 shorter events, 0.6 us)
Async XLA Ops:
  0.0 24.5 %copy-start.6 = (f32[256,64]{0,1:T(8,128)S(1)}, f32[256,64]{0,1:T(8,128)}, u32[]{:S(2)}) copy-start(f32[256,64]{0,1:T(8,128)} %param.12) | copy-start | bytes 196612
  0.0 36.2 %copy-start.4 = (s32[1,96]{1,0:T(1,128)S(1)}, s32[1,96]{1,0:T(1,128)}, u32[]{:S(2)}) copy-start(s32[1,96]{1,0:T(1,128)} %param.17) | copy-start | bytes 1156
  0.0 36.2 %copy-start.5 = (s32[1,96]{1,0:T(1,128)S(1)}, s32[1,96]{1,0:T(1,128)}, u32[]{:S(2)}) copy-start(s32[1,96]{1,0:T(1,128)} %param.18) | copy-start | bytes 1156
  11.3 74.2 %all-to-all-start = ((f32[64,80,128]{2,1,0:T(8,128)}), f32[64,80,128]{2,1,0:T(8,128)S(1)}, u32[]{:S(2)}, u32[]{:S(2)}) async-start(f32[64,80,128]{2,1,0:T(8,128)} %shard_map.100), calls=%async_computation | async-start | bytes 5242880 | tf_op jit(solution)/shard_map/all_to_all | solution.py:368
  24.5 3.9 %collective-permute-start = (f32[256,64]{0,1:T(8,128)S(1)}, f32[256,64]{0,1:T(8,128)S(1)}, u32[]{:S(2)}, u32[]{:S(2)}) collective-permute-start(f32[256,64]{0,1:T(8,128)S(1)} %copy-done.6), channel_id=1, source_target_pairs={{0,3},{1,0},{2,1},{3,2},{4,7},{5,4},{6,5},{7,6},{8,11},{9,8},{10,9... | collective-permute-start | bytes 196616 | tf_op jit(solution)/shard_map/ppermute | solution.py:347
  27.1 4.9 %collective-permute-start.1 = (f32[256,64]{0,1:T(8,128)S(1)}, f32[256,64]{0,1:T(8,128)S(1)}, u32[]{:S(2)}, u32[]{:S(2)}) collective-permute-start(f32[256,64]{0,1:T(8,128)S(1)} %copy-done.6), channel_id=1, source_target_pairs={{0,2},{1,3},{2,0},{3,1},{4,6},{5,7},{6,4},{7,5},{8,10},{9,11},{10,... | collective-permute-start | bytes 196616 | tf_op jit(solution)/shard_map/ppermute | solution.py:347
  27.6 5.3 %collective-permute-start.2 = (f32[256,64]{0,1:T(8,128)S(1)}, f32[256,64]{0,1:T(8,128)S(1)}, u32[]{:S(2)}, u32[]{:S(2)}) collective-permute-start(f32[256,64]{0,1:T(8,128)S(1)} %copy-done.6), channel_id=1, source_target_pairs={{0,1},{1,2},{2,3},{3,0},{4,5},{5,6},{6,7},{7,4},{8,9},{9,10},{10,1... | collective-permute-start | bytes 196616 | tf_op jit(solution)/shard_map/ppermute | solution.py:347
  32.9 63.7 %collective-permute-start.4 = (f32[64,4096]{1,0:T(8,128)}, f32[64,4096]{1,0:T(8,128)}, u32[]{:S(2)}, u32[]{:S(2)}) collective-permute-start(f32[64,4096]{1,0:T(8,128)} %bitcast.62), channel_id=1, source_target_pairs={{0,1},{1,2},{2,3},{3,0},{4,5},{5,6},{6,7},{7,4},{8,9},{9,10},{10,1... | collective-permute-start | bytes 3145736 | tf_op jit(solution)/shard_map/ppermute | solution.py:347
  32.9 63.7 %collective-permute-start.5 = (f32[64,4096]{1,0:T(8,128)}, f32[64,4096]{1,0:T(8,128)}, u32[]{:S(2)}, u32[]{:S(2)}) collective-permute-start(f32[64,4096]{1,0:T(8,128)} %bitcast.63), channel_id=1, source_target_pairs={{0,2},{1,3},{2,0},{3,1},{4,6},{5,7},{6,4},{7,5},{8,10},{9,11},{10,... | collective-permute-start | bytes 3145736 | tf_op jit(solution)/shard_map/ppermute | solution.py:347
  34.4 62.3 %collective-permute-start.6 = (f32[64,4096]{1,0:T(8,128)}, f32[64,4096]{1,0:T(8,128)}, u32[]{:S(2)}, u32[]{:S(2)}) collective-permute-start(f32[64,4096]{1,0:T(8,128)} %bitcast.64), channel_id=1, source_target_pairs={{0,3},{1,0},{2,1},{3,2},{4,7},{5,4},{6,5},{7,6},{8,11},{9,8},{10,9... | collective-permute-start | bytes 3145736 | tf_op jit(solution)/shard_map/ppermute | solution.py:347
  36.2 2.8 %copy-start.2 = (f32[1,96,128,128]{3,2,1,0:T(8,128)S(1)}, f32[1,96,128,128]{3,2,1,0:T(8,128)}, u32[]{:S(2)}) copy-start(f32[1,96,128,128]{3,2,1,0:T(8,128)} %param.19) | copy-start | bytes 18874372
  41.4 2.6 %copy-start.1 = (bf16[96,128,256]{2,1,0:T(8,128)(2,1)}, bf16[96,128,256]{2,1,0:T(8,128)(2,1)S(1)}, u32[]{:S(2)}) copy-start(bf16[96,128,256]{2,1,0:T(8,128)(2,1)S(1)} %get-tuple-element.43.tiles_hbm) | copy-start | bytes 18874372
  85.6 7.1 %collective-permute-start.3 = (f32[64,16,128]{2,1,0:T(8,128)S(1)}, f32[64,16,128]{2,1,0:T(8,128)}, u32[]{:S(2)}, u32[]{:S(2)}) collective-permute-start(f32[64,16,128]{2,1,0:T(8,128)S(1)} %slice.3.own_ref), channel_id=1, source_target_pairs={{0,4},{4,0},{8,12},{12,8},{16,20},{20,16},{24,28},{28,24},{32,36},... | collective-permute-start | bytes 1572872 | tf_op jit(solution)/shard_map/ppermute | solution.py:381
  92.7 11.5 %copy-start.8 = (s32[1,64,64]{2,1,0:T(8,128)S(1)}, s32[1,64,64]{2,1,0:T(8,128)}, u32[]{:S(2)}) copy-start(s32[1,64,64]{2,1,0:T(8,128)} %param.16) | copy-start | bytes 49156
  96.6 38.4 %all-to-all-start.1 = ((f32[256,8,128]{2,1,0:T(8,128)}), f32[256,8,128]{2,1,0:T(8,128)S(1)}, u32[]{:S(2)}, u32[]{:S(2)}) async-start(f32[256,8,128]{2,1,0:T(8,128)} %shard_map.103), calls=%async_computation.1 | async-start | bytes 2097152 | tf_op jit(solution)/shard_map/all_to_all | solution.py:388
  107.6 4.4 %copy-start.7 = (f32[256,64]{0,1:T(8,128)S(1)}, f32[256,64]{0,1:T(8,128)}, u32[]{:S(2)}) copy-start(f32[256,64]{0,1:T(8,128)} %param.11) | copy-start | bytes 196612
  112.0 23.1 %copy-start = (bf16[4,1024,256]{2,1,0:T(8,128)(2,1)S(1)}, bf16[4,1024,256]{2,1,0:T(8,128)(2,1)}, u32[]{:S(2)}) copy-start(bf16[4,1024,256]{2,1,0:T(8,128)(2,1)} %shard_map.104.weights_ref) | copy-start | bytes 6291460
  113.4 27.2 %copy-start.9 = (f32[64]{0:T(128)S(1)}, f32[64]{0:T(128)}, u32[]{:S(2)}) copy-start(f32[64]{0:T(128)} %param.13) | copy-start | bytes 772
  137.1 9.8 %collective-permute-start.7 = (f32[512,128]{1,0:T(8,128)}, f32[512,128]{1,0:T(8,128)S(1)}, u32[]{:S(2)}, u32[]{:S(2)}) collective-permute-start(f32[512,128]{1,0:T(8,128)} %get-tuple-element.66), channel_id=1, source_target_pairs={{0,2},{1,3},{2,0},{3,1},{4,6},{5,7},{6,4},{7,5},{8,10},{9,11},{10,... | collective-permute-start | bytes 786440 | tf_op jit(solution)/shard_map/ppermute | solution.py:347
  139.1 12.9 %collective-permute-start.8 = (f32[512,128]{1,0:T(8,128)}, f32[512,128]{1,0:T(8,128)S(1)}, u32[]{:S(2)}, u32[]{:S(2)}) collective-permute-start(f32[512,128]{1,0:T(8,128)} %get-tuple-element.67), channel_id=1, source_target_pairs={{0,3},{1,0},{2,1},{3,2},{4,7},{5,4},{6,5},{7,6},{8,11},{9,8},{10,9... | collective-permute-start | bytes 786440 | tf_op jit(solution)/shard_map/ppermute | solution.py:347
  140.0 12.7 %collective-permute-start.9 = (f32[512,128]{1,0:T(8,128)}, f32[512,128]{1,0:T(8,128)S(1)}, u32[]{:S(2)}, u32[]{:S(2)}) collective-permute-start(f32[512,128]{1,0:T(8,128)} %get-tuple-element.68), channel_id=1, source_target_pairs={{0,1},{1,2},{2,3},{3,0},{4,5},{5,6},{6,7},{7,4},{8,9},{9,10},{10,1... | collective-permute-start | bytes 786440 | tf_op jit(solution)/shard_map/ppermute | solution.py:347
  140.7 1.2 copy-start.3

commit v5 on v4

--- a/solution.py
+++ b/solution.py
@@ -16,8 +16,16 @@
     return lax.broadcasted_iota(jnp.int32, shape, len(shape) - 1) < HALF
 
 
-def gather_kernel(rows_ref, hubs_ref, xt_hbm, out_ref, xt_ref, table_ref, hub_ref, sems, *, peers, rows, hub_rows):
-    step = pl.program_id(0)
+def gather_kernel(
+    rows_hbm, hubs_hbm, xt_hbm, out_hbm, rows_ref, hubs_ref, xt_ref, table_ref, hub_ref, out_ref, sems, list_sems, out_sems,
+    *, rows, hub_rows
+):
+    lists = [
+        pltpu.make_async_copy(rows_hbm, rows_ref, list_sems.at[0]),
+        pltpu.make_async_copy(hubs_hbm, hubs_ref, list_sems.at[1]),
+    ]
+    for copy in lists:
+        copy.start()
     chunks = sems.shape[0]
     width = xt_ref.shape[1] // chunks
 
@@ -25,57 +33,70 @@
         columns = pl.ds(c * width, width)
         return pltpu.make_async_copy(xt_hbm.at[:, columns], xt_ref.at[:, columns], sems.at[c])
 
-    @pl.when(step == 0)
-    def _():
-        for c in range(chunks):
-            fetch(c).start()
-        for c in range(chunks):
-            fetch(c).wait()
-            part = xt_ref[:, c * width : (c + 1) * width]
-            table_ref[c * width : (c + 1) * width, :] = jnp.concatenate([part, part], axis=0).T
+    for c in range(chunks):
+        fetch(c).start()
+    for c in range(chunks):
+        fetch(c).wait()
+        part = xt_ref[:, c * width : (c + 1) * width]
+        table_ref[c * width : (c + 1) * width, :] = jnp.concatenate([part, part], axis=0).T
+    for copy in lists:
+        copy.wait()
 
     left = left_half((1, LANES))
 
     def pick(first, second):
         return jnp.where(left, table_ref[pl.ds(first, 1), :], table_ref[pl.ds(second, 1), :])
 
-    @pl.when(step == 0)
-    def _():
-        for half in range(2):
-            start = half * 2 * hub_rows
-            for i in range(hub_rows):
-                hub_ref[half, i : i + 1, :] = pick(hubs_ref[start + i], hubs_ref[start + hub_rows + i])
+    for half in range(2):
+        start = half * 2 * hub_rows
+        for i in range(hub_rows):
+            hub_ref[half, i : i + 1, :] = pick(hubs_ref[start + i], hubs_ref[start + hub_rows + i])
 
     def one(peer, carry):
-        base = (step * peers + peer) * 2 * rows
+        base = peer * 2 * rows
         for i in range(rows):
             out_ref[peer, i : i + 1, :] = pick(rows_ref[base + i], rows_ref[base + rows + i])
-        out_ref[peer, rows : rows + hub_rows, :] = hub_ref[peer % 2]
+        out_ref[peer, rows : rows + hub_rows, :] = hub_ref[lax.rem(peer, 2)]
         return carry
 
-    lax.fori_loop(0, peers, one, 0)
+    groups = out_sems.shape[0]
+    peers = out_ref.shape[0] // groups
+
+    def send(g):
+        span = pl.ds(g * peers, peers)
+        return pltpu.make_async_copy(out_ref.at[span], out_hbm.at[span], out_sems.at[g])
+
+    def group(g, carry):
+        lax.fori_loop(g * peers, (g + 1) * peers, one, 0)
+        send(g).start()
+        return carry
+
+    lax.fori_loop(0, groups, group, 0)
+    for g in range(groups):
+        send(g).wait()
 
 
 def gather_rows(xt, send_rows, hub_list):
     peer_count = send_rows.shape[0]
     rows = send_rows.shape[1] // 2
     hub_rows = hub_list.shape[0] // 4
-    peers = 8
-    return pl.pallas_call(
-        functools.partial(gather_kernel, peers=peers, rows=rows, hub_rows=hub_rows),
-        grid_spec=pltpu.PrefetchScalarGridSpec(
-            num_scalar_prefetch=2,
-            grid=(peer_count // peers,),
-            in_specs=[pl.BlockSpec(memory_space=pltpu.HBM)],
-            out_specs=pl.BlockSpec((peers, rows + hub_rows, LANES), lambda i, *_: (i, 0, 0)),
-            scratch_shapes=[
-                pltpu.VMEM(xt.shape, jnp.float32),
-                pltpu.VMEM((xt.shape[1], LANES), jnp.float32),
-                pltpu.VMEM((2, hub_rows, LANES), jnp.float32),
-                pltpu.SemaphoreType.DMA((8,)),
-            ],
-        ),
-        out_shape=jax.ShapeDtypeStruct((peer_count, rows + hub_rows, LANES), jnp.float32),
+    shape = (peer_count, rows + hub_rows, LANES)
+    return pl.pallas_call(
+        functools.partial(gather_kernel, rows=rows, hub_rows=hub_rows),
+        in_specs=[pl.BlockSpec(memory_space=pltpu.HBM)] * 3,
+        out_specs=pl.BlockSpec(memory_space=pltpu.HBM),
+        scratch_shapes=[
+            pltpu.SMEM((send_rows.size,), jnp.int32),
+            pltpu.SMEM(hub_list.shape, jnp.int32),
+            pltpu.VMEM(xt.shape, jnp.float32),
+            pltpu.VMEM((xt.shape[1], LANES), jnp.float32),
+            pltpu.VMEM((2, hub_rows, LANES), jnp.float32),
+            pltpu.VMEM(shape, jnp.float32),
+            pltpu.SemaphoreType.DMA((8,)),
+            pltpu.SemaphoreType.DMA((2,)),
+            pltpu.SemaphoreType.DMA((16,)),
+        ],
+        out_shape=jax.ShapeDtypeStruct(shape, jnp.float32),
         compiler_params=pltpu.CompilerParams(vmem_limit_bytes=60 * 2**20),
         cost_estimate=pl.CostEstimate(flops=10**7, bytes_accessed=4 * 2**20, transcendentals=0),
     )(send_rows.reshape(-1), hub_list, xt)
@@ -153,8 +174,11 @@
             tiles_hbm.at[pl.ds(first + c * count, count)], tiles_ref.at[pl.ds(c * count, count)], sems.at[c]
         )
 
-    for c in range(chunks):
-        fetch(c).start()
+    piece = count // 4
+    for c in range(chunks * 4):
+        pltpu.make_async_copy(
+            tiles_hbm.at[pl.ds(first + c * piece, piece)], tiles_ref.at[pl.ds(c * piece, piece)], sems.at[c // 4]
+        ).start()
     hubs = pltpu.make_async_copy(tiles_hbm.at[pl.ds(0, first)], hub_tiles_ref, hub_sem)
     hubs.start()
     acc_ref[...] = jnp.zeros_like(acc_ref)
@@ -270,7 +294,9 @@
     )(weights)
 
 
-def slots_kernel(slots_ref, weights_ref, *out_refs, targets):
+def slots_kernel(slots_ref, weights_ref, kept_ref, *refs, targets):
+    moved = len(targets)
+    out_refs, (held_ref, sems) = refs[:moved], refs[moved:]
     peers = slots_ref.shape[0]
     blocks = slots_ref.shape[1]
     tops, mids = [], []
@@ -279,18 +305,37 @@
         tops.append(top)
         mids.append(mid)
     whole = jnp.concatenate(tops + mids, axis=1)
-    for d, out_ref in zip(targets, out_refs):
-        product = jnp.dot(whole, weights_ref[d], preferred_element_type=jnp.float32)
-        out_ref[...] = product[:, :LANES] + product[:, LANES:]
+
+    def product(d):
+        both = jnp.dot(whole, weights_ref[d], preferred_element_type=jnp.float32)
+        return both[:, :LANES] + both[:, LANES:]
+
+    copies = []
+    for i, d in enumerate(targets):
+        held_ref[i] = product(d)
+        copies.append(pltpu.make_async_copy(held_ref.at[i], out_refs[i], sems.at[i]))
+        copies[-1].start()
+    kept_ref[...] = product(0)
+    for copy in copies:
+        copy.wait()
 
 
 def project_slots(slots, weights, targets):
     peers = slots.shape[0]
+    moved = len(targets)
+    shape = jax.ShapeDtypeStruct((peers * 8, LANES), jnp.float32)
+    vmem = pl.BlockSpec(memory_space=pltpu.VMEM)
     return pl.pallas_call(
         functools.partial(slots_kernel, targets=targets),
-        out_shape=[jax.ShapeDtypeStruct((peers * 8, LANES), jnp.float32)] * len(targets),
+        in_specs=[vmem, vmem],
+        out_specs=[vmem] + [pl.BlockSpec(memory_space=pltpu.HBM)] * moved,
+        out_shape=[shape] * (moved + 1),
+        scratch_shapes=[
+            pltpu.VMEM((moved,) + shape.shape, jnp.float32),
+            pltpu.SemaphoreType.DMA((moved,)),
+        ],
         compiler_params=pltpu.CompilerParams(vmem_limit_bytes=12 * 2**20),
-        cost_estimate=pl.CostEstimate(flops=10**7, bytes_accessed=16 * 2**20, transcendentals=0),
+        cost_estimate=pl.CostEstimate(flops=10**7, bytes_accessed=4 * 2**20, transcendentals=0),
     )(slots, weights)
 
 
@@ -298,7 +343,11 @@
     parts = refs[:blocks]
     base_refs = refs[blocks : blocks + bases]
     bias_ref = refs[blocks + bases] if last else None
-    out_ref, *sums = refs[blocks + bases + last :]
+    refs = refs[blocks + bases + last :]
+    if last:
+        out_hbm, *sums, out_ref, sems = refs
+    else:
+        out_ref, *sums = refs
     for total in sums:
         total[...] = jnp.zeros_like(total)
     left = left_half((1, LANES))
@@ -319,6 +368,7 @@
 
         lax.fori_loop(0, count // lanes, add, 0, unroll=8)
     width = 512
+    copies = []
     for c in range(out_ref.shape[1] // width):
         columns = slice(c * width, (c + 1) * width)
         whole = functools.reduce(lambda a, b: a + b, [total[columns, :] for total in sums])
@@ -327,6 +377,11 @@
         for base in base_refs:
             result = result + base[:, columns]
         out_ref[:, columns] = jnp.maximum(result + bias_ref[...], 0.0) if last else result
+        if last:
+            copies.append(pltpu.make_async_copy(out_ref.at[:, columns], out_hbm.at[:, columns], sems.at[c]))
+            copies[-1].start()
+    for copy in copies:
+        copy.wait()
 
 
 def scatter_rows(parts, rows, bases, row_count, bias=None):
@@ -335,9 +390,10 @@
     return pl.pallas_call(
         functools.partial(scatter_kernel, blocks=len(parts), bases=len(bases), last=last),
         in_specs=[pl.BlockSpec(memory_space=pltpu.SMEM)] + [vmem] * (len(parts) + len(bases) + last),
-        out_specs=vmem,
+        out_specs=pl.BlockSpec(memory_space=pltpu.HBM) if last else vmem,
         out_shape=jax.ShapeDtypeStruct((HALF, row_count), jnp.float32),
-        scratch_shapes=[pltpu.VMEM((row_count + 8, LANES), jnp.float32)] * 4,
+        scratch_shapes=[pltpu.VMEM((row_count + 8, LANES), jnp.float32)] * 4
+        + ([pltpu.VMEM((HALF, row_count), jnp.float32), pltpu.SemaphoreType.DMA((8,))] if last else []),
         compiler_params=pltpu.CompilerParams(vmem_limit_bytes=13 * 2**20),
         cost_estimate=pl.CostEstimate(flops=10**7, bytes_accessed=16 * 2**20, transcendentals=0),
     )(rows, *parts, *bases, *([bias] if last else []))
@@ -414,18 +470,19 @@
     ]
     far = feat // 2
     near = [d for d in range(feat - 1, 0, -1) if d != far]
-    tail = (far, *near)
-    tail_rows = jnp.concatenate([order[d] for d in tail])
+    near_rows = jnp.concatenate([order[d] for d in near])
     bias = out_bias[:, None]
     row_count = features.shape[0]
-    slots, own, weights, tail_rows, order, bias = lax.optimization_barrier(
-        (slots, own, weights, tail_rows, order, bias)
+    slots, own, weights, near_rows, order, bias = lax.optimization_barrier(
+        (slots, own, weights, near_rows, order, bias)
     )
     slots = slots.reshape(peers, feat, 8, LANES)
-    parts = project_slots(slots, weights, range(feat))
-    moved = {d: shifted(parts[d], feat, d) for d in tail}
-    total = scatter_rows([parts[0]], order[0], [own], row_count)
-    return scatter_rows([moved[d] for d in tail], tail_rows, [total], row_count, bias).T
+    targets = (far, *near)
+    kept, *parts = project_slots(slots, weights, targets)
+    moved = {d: shifted(part, feat, d) for d, part in zip(targets, parts)}
+    total = scatter_rows([kept], order[0], [own], row_count)
+    total = scatter_rows([moved[far]], order[far], [total], row_count)
+    return scatter_rows([moved[d] for d in near], near_rows, [total], row_count, bias).T
 
 
 def solution(mesh):

time: 161 us -> 158 us (0.981)
  waiting for transfers between devices: 69.5 us -> 66.7 us
    ppermute x9, waiting for transfers between devices: 12.2 us -> 8.77 us  [shifted(): lax.ppermute(value, 'feat', [(i, (i + step) % count) for i in range(count)])]
    pallas_call x2 -> x3, Pallas kernels: 11 us -> 12.7 us  [scatter_rows(): pl.pallas_call(functools.partial(scatter_kernel, blocks=len(parts), bases...]
  transfers between devices with their start and end apart: 12 -> 12, of which waited for: 8 -> 8; matrix products, arithmetic and copies ran while one was open for 8% -> 7% of each run, Pallas kernels for 11% -> 13%
where the time goes in v5:
time: 158 us
  waiting for transfers between devices  66.7 us (42%)
  Pallas kernels  38.9 us (25%)
  starting transfers between devices  33.4 us (21%)
  local copies, waits for them, and re-layouts  10.4 us (7%)
  matrix products  5.79 us (4%)
  other arithmetic  1.93 us (1%)
    all_to_all x1, waiting for transfers between devices, per_device(): lax.all_to_all(outgoing, 'dom', split_axis=0, concat_axis=0, tiled=True)  41.5 us
    all_to_all x1, waiting for transfers between devices, per_device(): lax.all_to_all(partial, ('dom', 'feat'), split_axis=0, concat_axis=0, til...  16.4 us
    all_to_all x1, starting transfers between devices, per_device(): lax.all_to_all(outgoing, 'dom', split_axis=0, concat_axis=0, tiled=True)  13.2 us
    pallas_call x3, Pallas kernels, scatter_rows(): pl.pallas_call(functools.partial(scatter_kernel, blocks=len(parts), bases...  12.7 us
    ppermute x9, starting transfers between devices, shifted(): lax.ppermute(value, 'feat', [(i, (i + step) % count) for i in range(count)])  10.6 us
    pallas_call x1, Pallas kernels, gather_rows(): pl.pallas_call(functools.partial(gather_kernel, rows=rows, hub_rows=hub_r...  10 us
    ppermute x9, waiting for transfers between devices, shifted(): lax.ppermute(value, 'feat', [(i, (i + step) % count) for i in range(count)])  8.77 us
    all_to_all x1, starting transfers between devices, per_device(): lax.all_to_all(partial, ('dom', 'feat'), split_axis=0, concat_axis=0, til...  7.49 us
  transfers between devices with their start and end apart: 12, of which 8 were waited for; matrix products, arithmetic and copies ran while one was open for 7% of the time, Pallas kernels for 13%

profile of v5, /device:TPU:1, one launch (start us, length us, event | category | flops | bytes accessed | tf_op | source)
XLA Modules:
  0.0 157.7 jit_solution(9339630808346921080)
XLA Ops:
  0.0 10.0 %shard_map.100 = f32[64,80,128]{2,1,0:T(8,128)} custom-call(s32[8192]{0:T(1024)} %bitcast.75, s32[64]{0:T(128)} %bitcast.81, f32[64,4096]{1,0:T(8,128)} %bitcast.61), custom_call_target="tpu_custom_call" | custom-call | flops 10000000 | bytes 4194304 | tf_op jit(solution)/shard_map/pallas_call | solution.py:84
  10.0 13.2 %all-to-all-start = ((f32[64,80,128]{2,1,0:T(8,128)}), f32[64,80,128]{2,1,0:T(8,128)S(1)}, u32[]{:S(2)}, u32[]{:S(2)}) async-start(f32[64,80,128]{2,1,0:T(8,128)} %shard_map.100), calls=%async_computation | async-start | bytes 5242880 | tf_op jit(solution)/shard_map/all_to_all | solution.py:424
  23.2 2.6 %collective-permute-start = (f32[256,64]{0,1:T(8,128)S(1)}, f32[256,64]{0,1:T(8,128)S(1)}, u32[]{:S(2)}, u32[]{:S(2)}) collective-permute-start(f32[256,64]{0,1:T(8,128)S(1)} %copy-done.6), channel_id=1, source_target_pairs={{0,3},{1,0},{2,1},{3,2},{4,7},{5,4},{6,5},{7,6},{8,11},{9,8},{10,9... | collective-permute-start | bytes 196616 | tf_op jit(solution)/shard_map/ppermute | solution.py:403
  25.8 0.5 collective-permute-start.1
  26.3 0.6 collective-permute-start.2
  26.9 0.2 collective-permute-done
  27.1 3.6 %collective-permute-done.1 = f32[256,64]{0,1:T(8,128)S(1)} collective-permute-done((f32[256,64]{0,1:T(8,128)S(1)}, f32[256,64]{0,1:T(8,128)S(1)}, u32[]{:S(2)}, u32[]{:S(2)}) %collective-permute-start.1) | collective-permute-done | bytes 65568 | tf_op jit(solution)/shard_map/ppermute | solution.py:403
  30.7 0.9 collective-permute-done.2
  31.6 1.5 collective-permute-start.5
  33.1 1.9 %collective-permute-start.6 = (f32[64,4096]{1,0:T(8,128)}, f32[64,4096]{1,0:T(8,128)}, u32[]{:S(2)}, u32[]{:S(2)}) collective-permute-start(f32[64,4096]{1,0:T(8,128)} %bitcast.64), channel_id=1, source_target_pairs={{0,3},{1,0},{2,1},{3,2},{4,7},{5,4},{6,5},{7,6},{8,11},{9,8},{10,9... | collective-permute-start | bytes 3145736 | tf_op jit(solution)/shard_map/ppermute | solution.py:403
  35.0 2.8 %copy-done.2 = f32[1,96,128,128]{3,2,1,0:T(8,128)S(1)} copy-done((f32[1,96,128,128]{3,2,1,0:T(8,128)S(1)}, f32[1,96,128,128]{3,2,1,0:T(8,128)}, u32[]{:S(2)}) %copy-start.2) | copy-done | bytes 6291480
  37.7 2.4 %shard_map.101 = (bf16[96,128,256]{2,1,0:T(8,128)(2,1)S(1)}, s32[96]{0:T(128)S(1)}) custom-call(s32[96]{0:T(128)S(1)} %bitcast.59, s32[96]{0:T(128)S(1)} %bitcast.60, f32[96,128,128]{2,1,0:T(8,128)S(1)} %bitcast.57), custom_call_target="tpu_custom_call" | custom-call | flops 10000000 | bytes 12582912 | tf_op jit(solution)/shard_map/pallas_call | solution.py:125
  40.1 2.6 %copy-done.1 = bf16[96,128,256]{2,1,0:T(8,128)(2,1)} copy-done((bf16[96,128,256]{2,1,0:T(8,128)(2,1)}, bf16[96,128,256]{2,1,0:T(8,128)(2,1)S(1)}, u32[]{:S(2)}) %copy-start.1) | copy-done | bytes 6291480
  42.7 41.5 %all-to-all-done.mirror_ref = f32[64,80,128]{2,1,0:T(8,128)S(1)} async-done(((f32[64,80,128]{2,1,0:T(8,128)}), f32[64,80,128]{2,1,0:T(8,128)S(1)}, u32[]{:S(2)}, u32[]{:S(2)}) %all-to-all-start) | async-done | bytes 2621472 | tf_op jit(solution)/shard_map/all_to_all | solution.py:424
  84.3 2.1 %collective-permute-start.3 = (f32[64,16,128]{2,1,0:T(8,128)S(1)}, f32[64,16,128]{2,1,0:T(8,128)}, u32[]{:S(2)}, u32[]{:S(2)}) collective-permute-start(f32[64,16,128]{2,1,0:T(8,128)S(1)} %slice.3.own_ref), channel_id=1, source_target_pairs={{0,4},{4,0},{8,12},{12,8},{16,20},{20,16},{24,28},{28,24},{32,36},... | collective-permute-start | bytes 1572872 | tf_op jit(solution)/shard_map/ppermute | solution.py:437
  86.4 5.0 %shard_map.102 = (f32[256,8,128]{2,1,0:T(8,128)S(1)}, bf16[32,128,256]{2,1,0:T(8,128)(2,1)S(1)}) custom-call(s32[96]{0:T(128)S(1)} %get-tuple-element.43.dst_ref, bf16[96,128,256]{2,1,0:T(8,128)(2,1)} %copy-done.1, f32[64,80,128]{2,1,0:T(8,128)S(1)} %all-to-all-done.mirror_ref), custom_call_target="tpu_custom_call" | custom-call | flops 1000000000 | bytes 10485760 | tf_op jit(solution)/shard_map/pallas_call | solution.py:205
  91.5 3.9 %shard_map.103 = f32[256,8,128]{2,1,0:T(8,128)} custom-call(s32[96]{0:T(128)S(1)} %get-tuple-element.43.dst_ref, s32[1]{0:T(128)} %bitcast.6.side_ref, bf16[32,128,256]{2,1,0:T(8,128)(2,1)S(1)} %get-tuple-element.46.tiles_ref, f32[64,16,128]{2,1,0:T(8,128)S(1)} %slice.3.own_ref, f32[64,16,128]{2,1,0:T(8,128)} %collective-permute-done.3.other_ref, ...), custom_call_target="tpu_custom_call" | custom-call | flops 1000000000 | bytes 6291456 | tf_op jit(solution)/shard_map/pallas_call | solution.py:263
  95.4 7.5 %all-to-all-start.1 = ((f32[256,8,128]{2,1,0:T(8,128)}), f32[256,8,128]{2,1,0:T(8,128)S(1)}, u32[]{:S(2)}, u32[]{:S(2)}) async-start(f32[256,8,128]{2,1,0:T(8,128)} %shard_map.103), calls=%async_computation.1 | async-start | bytes 2097152 | tf_op jit(solution)/shard_map/all_to_all | solution.py:444
  103.1 0.2 copy.29
  103.2 0.8 reshape.43
  104.0 0.2 copy.30
  104.2 0.8 reshape.44
  105.3 0.1 pad_bitcast_fusion.7
  105.5 0.1 pad_bitcast_fusion.5
  105.6 0.1 pad_bitcast_fusion.3
  105.7 0.1 pad_bitcast_fusion.1
  105.9 1.1 pad_maximum_fusion.weights_ref
  106.9 2.9 %shard_map.104.weights_ref = bf16[4,1024,256]{2,1,0:T(8,128)(2,1)} custom-call(f32[4,512,128]{2,1,0:T(8,128)} %pad_maximum_fusion.weights_ref), custom_call_target="tpu_custom_call" | custom-call | tf_op jit(solution)/shard_map/pallas_call | solution.py:291
  109.8 0.1 reshape.38
  109.9 0.2 copy.31
  110.1 0.2 reshape.45.rows_ref
  110.3 0.2 copy.32
  110.5 0.2 reshape.46.rows_ref
  110.6 0.8 pad_add_fusion.rows_ref
  111.4 0.1 constant_dynamic-slice_fusion.3
  111.6 5.8 %fusion.refs_1_ = f32[64,4096]{1,0:T(8,128)} fusion(f32[64,4096]{1,0:T(8,128)} %collective-permute-done.6, f32[64,4096]{1,0:T(8,128)} %collective-permute-done.5, f32[64,4096]{1,0:T(8,128)} %collective-permute-done.4, f32[64,4096]{1,0:T(8,128)} %bitcast.65, f32[64,64]{0,1:T(8,128)S(1)} %bitcast.77, f32[64,64]{0,1:T(8,128)S(1)} %bitcast.78, ...), kind=kOutput, calls=%fused_computation | convolution fusion | flops 808501248 | bytes 5308416 | tf_op jit(solution)/shard_map/dot_general | solution.py:450
  117.4 16.4 %all-to-all-done.1 = f32[256,8,128]{2,1,0:T(8,128)S(1)} async-done(((f32[256,8,128]{2,1,0:T(8,128)}), f32[256,8,128]{2,1,0:T(8,128)S(1)}, u32[]{:S(2)}, u32[]{:S(2)}) %all-to-all-start.1) | async-done | bytes 1048608 | tf_op jit(solution)/shard_map/all_to_all | solution.py:444
  133.8 2.0 %shard_map.105 = (f32[512,128]{1,0:T(8,128)S(1)}, f32[512,128]{1,0:T(8,128)}, f32[512,128]{1,0:T(8,128)}, f32[512,128]{1,0:T(8,128)}) custom-call(f32[64,4,8,128]{3,2,1,0:T(8,128)S(1)} %bitcast.58, bf16[4,1024,256]{2,1,0:T(8,128)(2,1)S(1)} %copy-done), custom_call_target="tpu_custom_call" | custom-call | flops 10000000 | bytes 4194304 | tf_op jit(solution)/shard_map/pallas_call | solution.py:328
  135.8 2.1 %collective-permute-start.9 = (f32[512,128]{1,0:T(8,128)}, f32[512,128]{1,0:T(8,128)S(1)}, u32[]{:S(2)}, u32[]{:S(2)}) collective-permute-start(f32[512,128]{1,0:T(8,128)} %get-tuple-element.70), channel_id=1, source_target_pairs={{0,2},{1,3},{2,0},{3,1},{4,6},{5,7},{6,4},{7,5},{8,10},{9,11},{10,... | collective-permute-start | bytes 786440 | tf_op jit(solution)/shard_map/ppermute | solution.py:403
  137.9 0.9 collective-permute-start.7
  138.8 0.6 collective-permute-start.8
  139.5 1.2 copy-done.3
  140.7 3.2 %shard_map.106.refs_1_ = f32[64,4096]{1,0:T(8,128)S(1)} custom-call(s32[1024]{0:T(1024)S(1)} %reshape.45.rows_ref, f32[512,128]{1,0:T(8,128)S(1)} %get-tuple-element.72.refs_0_, f32[64,4096]{1,0:T(8,128)S(1)} %copy-done.3), custom_call_target="tpu_custom_call" | custom-call | flops 10000000 | bytes 16777216 | tf_op jit(solution)/shard_map/pallas_call | solution.py:390
  143.9 1.8 %collective-permute-done.9.refs_0_ = f32[512,128]{1,0:T(8,128)S(1)} collective-permute-done((f32[512,128]{1,0:T(8,128)}, f32[512,128]{1,0:T(8,128)S(1)}, u32[]{:S(2)}, u32[]{:S(2)}) %collective-permute-start.9) | collective-permute-done | bytes 262176 | tf_op jit(solution)/shard_map/ppermute | solution.py:403
  145.7 3.4 %shard_map.107.refs_2_ = f32[64,4096]{1,0:T(8,128)S(1)} custom-call(s32[1024]{0:T(1024)S(1)} %reshape.46.rows_ref, f32[512,128]{1,0:T(8,128)S(1)} %collective-permute-done.9.refs_0_, f32[64,4096]{1,0:T(8,128)S(1)} %shard_map.106.refs_1_), custom_call_target="tpu_custom_call" | custom-call | flops 10000000 | bytes 16777216 | tf_op jit(solution)/shard_map/pallas_call | solution.py:390
  149.1 1.7 %collective-permute-done.7.refs_0_ = f32[512,128]{1,0:T(8,128)S(1)} collective-permute-done((f32[512,128]{1,0:T(8,128)}, f32[512,128]{1,0:T(8,128)S(1)}, u32[]{:S(2)}, u32[]{:S(2)}) %collective-permute-start.7) | collective-permute-done | bytes 262176 | tf_op jit(solution)/shard_map/ppermute | solution.py:403
  150.8 0.7 collective-permute-done.8.refs_1_
  151.5 6.1 %shard_map.108 = f32[64,4096]{1,0:T(8,128)} custom-call(s32[2048]{0:T(1024)S(1)} %pad_add_fusion.rows_ref, f32[512,128]{1,0:T(8,128)S(1)} %collective-permute-done.7.refs_0_, f32[512,128]{1,0:T(8,128)S(1)} %collective-permute-done.8.refs_1_, f32[64,4096]{1,0:T(8,128)S(1)} %shard_map.107.refs_2_, f32[64,1]{1,0:T(8,128)S(1)} %copy.33.refs_3_), custom_call_target="tpu_custom_call" | custom-call | flops 10000000 | bytes 16777216 | tf_op jit(solution)/shard_map/pallas_call | solution.py:390
  (34 shorter events, 0.7 us)
Async XLA Ops:
  0.0 23.2 %copy-start.6 = (f32[256,64]{0,1:T(8,128)S(1)}, f32[256,64]{0,1:T(8,128)}, u32[]{:S(2)}) copy-start(f32[256,64]{0,1:T(8,128)} %param.12) | copy-start | bytes 196612
  0.0 34.9 %copy-start.4 = (s32[1,96]{1,0:T(1,128)S(1)}, s32[1,96]{1,0:T(1,128)}, u32[]{:S(2)}) copy-start(s32[1,96]{1,0:T(1,128)} %param.17) | copy-start | bytes 1156
  0.0 34.9 %copy-start.5 = (s32[1,96]{1,0:T(1,128)S(1)}, s32[1,96]{1,0:T(1,128)}, u32[]{:S(2)}) copy-start(s32[1,96]{1,0:T(1,128)} %param.18) | copy-start | bytes 1156
  10.0 74.2 %all-to-all-start = ((f32[64,80,128]{2,1,0:T(8,128)}), f32[64,80,128]{2,1,0:T(8,128)S(1)}, u32[]{:S(2)}, u32[]{:S(2)}) async-start(f32[64,80,128]{2,1,0:T(8,128)} %shard_map.100), calls=%async_computation | async-start | bytes 5242880 | tf_op jit(solution)/shard_map/all_to_all | solution.py:424
  23.2 3.9 %collective-permute-start = (f32[256,64]{0,1:T(8,128)S(1)}, f32[256,64]{0,1:T(8,128)S(1)}, u32[]{:S(2)}, u32[]{:S(2)}) collective-permute-start(f32[256,64]{0,1:T(8,128)S(1)} %copy-done.6), channel_id=1, source_target_pairs={{0,3},{1,0},{2,1},{3,2},{4,7},{5,4},{6,5},{7,6},{8,11},{9,8},{10,9... | collective-permute-start | bytes 196616 | tf_op jit(solution)/shard_map/ppermute | solution.py:403
  25.8 4.9 %collective-permute-start.1 = (f32[256,64]{0,1:T(8,128)S(1)}, f32[256,64]{0,1:T(8,128)S(1)}, u32[]{:S(2)}, u32[]{:S(2)}) collective-permute-start(f32[256,64]{0,1:T(8,128)S(1)} %copy-done.6), channel_id=1, source_target_pairs={{0,2},{1,3},{2,0},{3,1},{4,6},{5,7},{6,4},{7,5},{8,10},{9,11},{10,... | collective-permute-start | bytes 196616 | tf_op jit(solution)/shard_map/ppermute | solution.py:403
  26.3 5.3 %collective-permute-start.2 = (f32[256,64]{0,1:T(8,128)S(1)}, f32[256,64]{0,1:T(8,128)S(1)}, u32[]{:S(2)}, u32[]{:S(2)}) collective-permute-start(f32[256,64]{0,1:T(8,128)S(1)} %copy-done.6), channel_id=1, source_target_pairs={{0,1},{1,2},{2,3},{3,0},{4,5},{5,6},{6,7},{7,4},{8,9},{9,10},{10,1... | collective-permute-start | bytes 196616 | tf_op jit(solution)/shard_map/ppermute | solution.py:403
  31.6 63.8 %collective-permute-start.4 = (f32[64,4096]{1,0:T(8,128)}, f32[64,4096]{1,0:T(8,128)}, u32[]{:S(2)}, u32[]{:S(2)}) collective-permute-start(f32[64,4096]{1,0:T(8,128)} %bitcast.62), channel_id=1, source_target_pairs={{0,1},{1,2},{2,3},{3,0},{4,5},{5,6},{6,7},{7,4},{8,9},{9,10},{10,1... | collective-permute-start | bytes 3145736 | tf_op jit(solution)/shard_map/ppermute | solution.py:403
  31.6 63.8 %collective-permute-start.5 = (f32[64,4096]{1,0:T(8,128)}, f32[64,4096]{1,0:T(8,128)}, u32[]{:S(2)}, u32[]{:S(2)}) collective-permute-start(f32[64,4096]{1,0:T(8,128)} %bitcast.63), channel_id=1, source_target_pairs={{0,2},{1,3},{2,0},{3,1},{4,6},{5,7},{6,4},{7,5},{8,10},{9,11},{10,... | collective-permute-start | bytes 3145736 | tf_op jit(solution)/shard_map/ppermute | solution.py:403
  33.1 62.3 %collective-permute-start.6 = (f32[64,4096]{1,0:T(8,128)}, f32[64,4096]{1,0:T(8,128)}, u32[]{:S(2)}, u32[]{:S(2)}) collective-permute-start(f32[64,4096]{1,0:T(8,128)} %bitcast.64), channel_id=1, source_target_pairs={{0,3},{1,0},{2,1},{3,2},{4,7},{5,4},{6,5},{7,6},{8,11},{9,8},{10,9... | collective-permute-start | bytes 3145736 | tf_op jit(solution)/shard_map/ppermute | solution.py:403
  35.0 2.8 %copy-start.2 = (f32[1,96,128,128]{3,2,1,0:T(8,128)S(1)}, f32[1,96,128,128]{3,2,1,0:T(8,128)}, u32[]{:S(2)}) copy-start(f32[1,96,128,128]{3,2,1,0:T(8,128)} %param.19) | copy-start | bytes 18874372
  40.1 2.6 %copy-start.1 = (bf16[96,128,256]{2,1,0:T(8,128)(2,1)}, bf16[96,128,256]{2,1,0:T(8,128)(2,1)S(1)}, u32[]{:S(2)}) copy-start(bf16[96,128,256]{2,1,0:T(8,128)(2,1)S(1)} %get-tuple-element.44.tiles_hbm) | copy-start | bytes 18874372
  84.3 7.2 %collective-permute-start.3 = (f32[64,16,128]{2,1,0:T(8,128)S(1)}, f32[64,16,128]{2,1,0:T(8,128)}, u32[]{:S(2)}, u32[]{:S(2)}) collective-permute-start(f32[64,16,128]{2,1,0:T(8,128)S(1)} %slice.3.own_ref), channel_id=1, source_target_pairs={{0,4},{4,0},{8,12},{12,8},{16,20},{20,16},{24,28},{28,24},{32,36},... | collective-permute-start | bytes 1572872 | tf_op jit(solution)/shard_map/ppermute | solution.py:437
  91.4 11.5 %copy-start.8 = (s32[1,64,64]{2,1,0:T(8,128)S(1)}, s32[1,64,64]{2,1,0:T(8,128)}, u32[]{:S(2)}) copy-start(s32[1,64,64]{2,1,0:T(8,128)} %param.16) | copy-start | bytes 49156
  95.4 38.4 %all-to-all-start.1 = ((f32[256,8,128]{2,1,0:T(8,128)}), f32[256,8,128]{2,1,0:T(8,128)S(1)}, u32[]{:S(2)}, u32[]{:S(2)}) async-start(f32[256,8,128]{2,1,0:T(8,128)} %shard_map.103), calls=%async_computation.1 | async-start | bytes 2097152 | tf_op jit(solution)/shard_map/all_to_all | solution.py:444
  105.4 4.4 %copy-start.7 = (f32[256,64]{0,1:T(8,128)S(1)}, f32[256,64]{0,1:T(8,128)}, u32[]{:S(2)}) copy-start(f32[256,64]{0,1:T(8,128)} %param.11) | copy-start | bytes 196612
  110.1 23.7 %copy-start = (bf16[4,1024,256]{2,1,0:T(8,128)(2,1)S(1)}, bf16[4,1024,256]{2,1,0:T(8,128)(2,1)}, u32[]{:S(2)}) copy-start(bf16[4,1024,256]{2,1,0:T(8,128)(2,1)} %shard_map.104.weights_ref) | copy-start | bytes 6291460
  111.6 27.8 %copy-start.9 = (f32[64]{0:T(128)S(1)}, f32[64]{0:T(128)}, u32[]{:S(2)}) copy-start(f32[64]{0:T(128)} %param.13) | copy-start | bytes 772
  135.8 9.9 %collective-permute-start.9 = (f32[512,128]{1,0:T(8,128)}, f32[512,128]{1,0:T(8,128)S(1)}, u32[]{:S(2)}, u32[]{:S(2)}) collective-permute-start(f32[512,128]{1,0:T(8,128)} %get-tuple-element.70), channel_id=1, source_target_pairs={{0,2},{1,3},{2,0},{3,1},{4,6},{5,7},{6,4},{7,5},{8,10},{9,11},{10,... | collective-permute-start | bytes 786440 | tf_op jit(solution)/shard_map/ppermute | solution.py:403
  137.9 12.9 %collective-permute-start.7 = (f32[512,128]{1,0:T(8,128)}, f32[512,128]{1,0:T(8,128)S(1)}, u32[]{:S(2)}, u32[]{:S(2)}) collective-permute-start(f32[512,128]{1,0:T(8,128)} %get-tuple-element.67), channel_id=1, source_target_pairs={{0,3},{1,0},{2,1},{3,2},{4,7},{5,4},{6,5},{7,6},{8,11},{9,8},{10,9... | collective-permute-start | bytes 786440 | tf_op jit(solution)/shard_map/ppermute | solution.py:403
  138.8 12.7 %collective-permute-start.8 = (f32[512,128]{1,0:T(8,128)}, f32[512,128]{1,0:T(8,128)S(1)}, u32[]{:S(2)}, u32[]{:S(2)}) collective-permute-start(f32[512,128]{1,0:T(8,128)} %get-tuple-element.68), channel_id=1, source_target_pairs={{0,1},{1,2},{2,3},{3,0},{4,5},{5,6},{6,7},{7,4},{8,9},{9,10},{10,1... | collective-permute-start | bytes 786440 | tf_op jit(solution)/shard_map/ppermute | solution.py:403
  139.5 1.2 copy-start.3

commit v6 on v5

--- a/solution.py
+++ b/solution.py
@@ -8,7 +8,7 @@
 from jax.sharding import PartitionSpec as P
 
 LANES = 128
-KERNEL_VMEM = 48 * 2**20
+KERNEL_VMEM = 46 * 2**20
 HALF = 64
 
 
@@ -149,12 +149,14 @@
 
 
 def multiply(tile, block):
-    top, mid = split(block)
+    left = left_half(block.shape)
+    top = block.astype(jnp.bfloat16).astype(jnp.float32)
+    mid = block - top
     right_side = jnp.concatenate(
-        [jnp.concatenate([top, mid], axis=1), jnp.concatenate([mid, top], axis=1)], axis=0
+        [jnp.where(left, top, mid).astype(jnp.bfloat16), jnp.where(left, mid, top).astype(jnp.bfloat16)], axis=0
     )
     product = jnp.dot(tile, right_side, preferred_element_type=jnp.float32)
-    return product[:, :LANES] + product[:, LANES:]
+    return product + pltpu.roll(product, HALF, 1)
 
 
 def packed_sums(acc_ref, block, part):
@@ -164,7 +166,7 @@
 
 
 def listed_kernel(
-    dst_ref, tiles_hbm, mirror_ref, out_ref, hub_tiles_ref, tiles_ref, acc_ref, sems, hub_sem, *, first, rows
+    dst_ref, tiles_hbm, mirror_ref, acc_ref, hub_tiles_ref, tiles_ref, sems, hub_sem, *, first, rows
 ):
     chunks = sems.shape[0]
     count = tiles_ref.shape[0] // chunks
@@ -192,9 +194,6 @@
         return carry
 
     lax.fori_loop(0, chunks, chunk, 0)
-    for block in range(acc_ref.shape[0]):
-        for part in range(8):
-            out_ref[block * 8 + part] = packed_sums(acc_ref, block, part)
     hubs.wait()
 
 
@@ -208,12 +207,11 @@
         out_specs=[whole, whole],
         scratch_shapes=[
             pltpu.VMEM((count, size, 2 * size), jnp.bfloat16),
-            pltpu.VMEM((dst_blocks, size, LANES), jnp.float32),
             pltpu.SemaphoreType.DMA((8,)),
             pltpu.SemaphoreType.DMA,
         ],
         out_shape=[
-            jax.ShapeDtypeStruct((dst_blocks * 8, 8, LANES), jnp.float32),
+            jax.ShapeDtypeStruct((dst_blocks, size, LANES), jnp.float32),
             jax.ShapeDtypeStruct((first, size, 2 * size), jnp.bfloat16),
         ],
         compiler_params=pltpu.CompilerParams(vmem_limit_bytes=KERNEL_VMEM),
@@ -227,7 +225,7 @@
     count = 8
     chunks = tiles_ref.shape[0] // count
     side = side_ref[0]
-    acc_ref[...] = jnp.zeros_like(acc_ref)
+    acc_ref[...] = before_ref[...]
     hubs_ref[side] = own_ref[...]
     hubs_ref[1 - side] = other_ref[...]
 
@@ -248,7 +246,7 @@
     for c in range(sends):
         for block in range(c * blocks, (c + 1) * blocks):
             for part in range(8):
-                out_ref[block * 8 + part] = packed_sums(acc_ref, block, part) + before_ref[block * 8 + part]
+                out_ref[block * 8 + part] = packed_sums(acc_ref, block, part)
         span = pl.ds(c * blocks * 8, blocks * 8)
         results.append(pltpu.make_async_copy(out_ref.at[span], out_hbm.at[span], out_sems.at[c]))
         results[-1].start()
@@ -257,20 +255,20 @@
 
 
 def hub_tiles(split_vals, own, other, before, order, side):
-    _, size, _ = split_vals.shape
-    blocks = before.shape[0] // 8
+    blocks, size, _ = before.shape
     scalars = pl.BlockSpec(memory_space=pltpu.SMEM)
+    result = jax.ShapeDtypeStruct((blocks * 8, 8, LANES), jnp.float32)
     return pl.pallas_call(
         hub_kernel,
         in_specs=[scalars, scalars] + [pl.BlockSpec(memory_space=pltpu.VMEM)] * 4,
         out_specs=pl.BlockSpec(memory_space=pltpu.HBM),
         scratch_shapes=[
             pltpu.VMEM((2,) + own.shape, jnp.float32),
-            pltpu.VMEM((blocks, size, LANES), jnp.float32),
             pltpu.VMEM(before.shape, jnp.float32),
+            pltpu.VMEM(result.shape, jnp.float32),
             pltpu.SemaphoreType.DMA((4,)),
         ],
-        out_shape=jax.ShapeDtypeStruct(before.shape, jnp.float32),
+        out_shape=result,
         compiler_params=pltpu.CompilerParams(vmem_limit_bytes=KERNEL_VMEM),
         cost_estimate=pl.CostEstimate(flops=10**9, bytes_accessed=6 * 2**20, transcendentals=0),
     )(order, side, split_vals, own, other, before)

time: 158 us -> 159 us (level)
  no operation moved by 1% of the time
where the time goes in v6:
time: 159 us; the launch traced here: 158 us
  waiting for transfers between devices  66.8 us (42%)
  Pallas kernels  39.4 us (25%)
  starting transfers between devices  33.4 us (21%)
  local copies, waits for them, and re-layouts  10.4 us (7%)
  matrix products  5.79 us (4%)
  other arithmetic  1.93 us (1%)
    all_to_all x1, waiting for transfers between devices, per_device(): lax.all_to_all(outgoing, 'dom', split_axis=0, concat_axis=0, tiled=True)  41.5 us
    all_to_all x1, waiting for transfers between devices, per_device(): lax.all_to_all(partial, ('dom', 'feat'), split_axis=0, concat_axis=0, til...  16.4 us
    all_to_all x1, starting transfers between devices, per_device(): lax.all_to_all(outgoing, 'dom', split_axis=0, concat_axis=0, tiled=True)  13.2 us
    pallas_call x3, Pallas kernels, scatter_rows(): pl.pallas_call(functools.partial(scatter_kernel, blocks=len(parts), bases...  12.6 us
    ppermute x9, starting transfers between devices, shifted(): lax.ppermute(value, 'feat', [(i, (i + step) % count) for i in range(count)])  10.6 us
    pallas_call x1, Pallas kernels, gather_rows(): pl.pallas_call(functools.partial(gather_kernel, rows=rows, hub_rows=hub_r...  10 us
    ppermute x9, waiting for transfers between devices, shifted(): lax.ppermute(value, 'feat', [(i, (i + step) % count) for i in range(count)])  8.83 us
    all_to_all x1, starting transfers between devices, per_device(): lax.all_to_all(partial, ('dom', 'feat'), split_axis=0, concat_axis=0, til...  7.5 us
  transfers between devices with their start and end apart: 12, of which 8 were waited for; matrix products, arithmetic and copies ran while one was open for 7% of the time, Pallas kernels for 13%

profile of v6, /device:TPU:1, one launch (start us, length us, event | category | flops | bytes accessed | tf_op | source)
XLA Modules:
  0.0 158.3 jit_solution(1982917326711099739)
XLA Ops:
  0.0 10.0 %shard_map.100 = f32[64,80,128]{2,1,0:T(8,128)} custom-call(s32[8192]{0:T(1024)} %bitcast.75, s32[64]{0:T(128)} %bitcast.81, f32[64,4096]{1,0:T(8,128)} %bitcast.61), custom_call_target="tpu_custom_call" | custom-call | flops 10000000 | bytes 4194304 | tf_op jit(solution)/shard_map/pallas_call | solution.py:84
  10.0 13.2 %all-to-all-start = ((f32[64,80,128]{2,1,0:T(8,128)}), f32[64,80,128]{2,1,0:T(8,128)S(1)}, u32[]{:S(2)}, u32[]{:S(2)}) async-start(f32[64,80,128]{2,1,0:T(8,128)} %shard_map.100), calls=%async_computation | async-start | bytes 5242880 | tf_op jit(solution)/shard_map/all_to_all | solution.py:422
  23.2 2.6 %collective-permute-start = (f32[256,64]{0,1:T(8,128)S(1)}, f32[256,64]{0,1:T(8,128)S(1)}, u32[]{:S(2)}, u32[]{:S(2)}) collective-permute-start(f32[256,64]{0,1:T(8,128)S(1)} %copy-done.6), channel_id=1, source_target_pairs={{0,3},{1,0},{2,1},{3,2},{4,7},{5,4},{6,5},{7,6},{8,11},{9,8},{10,9... | collective-permute-start | bytes 196616 | tf_op jit(solution)/shard_map/ppermute | solution.py:401
  25.8 0.5 collective-permute-start.1
  26.3 0.6 collective-permute-start.2
  26.9 0.2 collective-permute-done
  27.1 3.6 %collective-permute-done.1 = f32[256,64]{0,1:T(8,128)S(1)} collective-permute-done((f32[256,64]{0,1:T(8,128)S(1)}, f32[256,64]{0,1:T(8,128)S(1)}, u32[]{:S(2)}, u32[]{:S(2)}) %collective-permute-start.1) | collective-permute-done | bytes 65568 | tf_op jit(solution)/shard_map/ppermute | solution.py:401
  30.7 0.9 collective-permute-done.2
  31.6 1.5 collective-permute-start.5
  33.1 1.9 %collective-permute-start.6 = (f32[64,4096]{1,0:T(8,128)}, f32[64,4096]{1,0:T(8,128)}, u32[]{:S(2)}, u32[]{:S(2)}) collective-permute-start(f32[64,4096]{1,0:T(8,128)} %bitcast.64), channel_id=1, source_target_pairs={{0,3},{1,0},{2,1},{3,2},{4,7},{5,4},{6,5},{7,6},{8,11},{9,8},{10,9... | collective-permute-start | bytes 3145736 | tf_op jit(solution)/shard_map/ppermute | solution.py:401
  35.0 2.8 %copy-done.2 = f32[1,96,128,128]{3,2,1,0:T(8,128)S(1)} copy-done((f32[1,96,128,128]{3,2,1,0:T(8,128)S(1)}, f32[1,96,128,128]{3,2,1,0:T(8,128)}, u32[]{:S(2)}) %copy-start.2) | copy-done | bytes 6291480
  37.7 2.4 %shard_map.101 = (bf16[96,128,256]{2,1,0:T(8,128)(2,1)S(1)}, s32[96]{0:T(128)S(1)}) custom-call(s32[96]{0:T(128)S(1)} %bitcast.59, s32[96]{0:T(128)S(1)} %bitcast.60, f32[96,128,128]{2,1,0:T(8,128)S(1)} %bitcast.57), custom_call_target="tpu_custom_call" | custom-call | flops 10000000 | bytes 12582912 | tf_op jit(solution)/shard_map/pallas_call | solution.py:125
  40.1 2.6 %copy-done.1 = bf16[96,128,256]{2,1,0:T(8,128)(2,1)} copy-done((bf16[96,128,256]{2,1,0:T(8,128)(2,1)}, bf16[96,128,256]{2,1,0:T(8,128)(2,1)S(1)}, u32[]{:S(2)}) %copy-start.1) | copy-done | bytes 6291480
  42.7 41.5 %all-to-all-done.mirror_ref = f32[64,80,128]{2,1,0:T(8,128)S(1)} async-done(((f32[64,80,128]{2,1,0:T(8,128)}), f32[64,80,128]{2,1,0:T(8,128)S(1)}, u32[]{:S(2)}, u32[]{:S(2)}) %all-to-all-start) | async-done | bytes 2621472 | tf_op jit(solution)/shard_map/all_to_all | solution.py:422
  84.3 2.1 %collective-permute-start.3 = (f32[64,16,128]{2,1,0:T(8,128)S(1)}, f32[64,16,128]{2,1,0:T(8,128)}, u32[]{:S(2)}, u32[]{:S(2)}) collective-permute-start(f32[64,16,128]{2,1,0:T(8,128)S(1)} %slice.3.own_ref), channel_id=1, source_target_pairs={{0,4},{4,0},{8,12},{12,8},{16,20},{20,16},{24,28},{28,24},{32,36},... | collective-permute-start | bytes 1572872 | tf_op jit(solution)/shard_map/ppermute | solution.py:435
  86.4 5.4 %shard_map.102 = (f32[32,128,128]{2,1,0:T(8,128)S(1)}, bf16[32,128,256]{2,1,0:T(8,128)(2,1)S(1)}) custom-call(s32[96]{0:T(128)S(1)} %get-tuple-element.43.dst_ref, bf16[96,128,256]{2,1,0:T(8,128)(2,1)} %copy-done.1, f32[64,80,128]{2,1,0:T(8,128)S(1)} %all-to-all-done.mirror_ref), custom_call_target="tpu_custom_call" | custom-call | flops 1000000000 | bytes 10485760 | tf_op jit(solution)/shard_map/pallas_call | solution.py:204
  91.9 4.1 %shard_map.103 = f32[256,8,128]{2,1,0:T(8,128)} custom-call(s32[96]{0:T(128)S(1)} %get-tuple-element.43.dst_ref, s32[1]{0:T(128)} %bitcast.6.side_ref, bf16[32,128,256]{2,1,0:T(8,128)(2,1)S(1)} %get-tuple-element.46.tiles_ref, f32[64,16,128]{2,1,0:T(8,128)S(1)} %slice.3.own_ref, f32[64,16,128]{2,1,0:T(8,128)} %collective-permute-done.3.other_ref, ...), custom_call_target="tpu_custom_call" | custom-call | flops 1000000000 | bytes 6291456 | tf_op jit(solution)/shard_map/pallas_call | solution.py:261
  96.0 7.5 %all-to-all-start.1 = ((f32[256,8,128]{2,1,0:T(8,128)}), f32[256,8,128]{2,1,0:T(8,128)S(1)}, u32[]{:S(2)}, u32[]{:S(2)}) async-start(f32[256,8,128]{2,1,0:T(8,128)} %shard_map.103), calls=%async_computation.1 | async-start | bytes 2097152 | tf_op jit(solution)/shard_map/all_to_all | solution.py:442
  103.7 0.2 copy.29
  103.9 0.8 reshape.43
  104.7 0.2 copy.30
  104.9 0.8 reshape.44
  106.0 0.1 pad_bitcast_fusion.7
  106.1 0.1 pad_bitcast_fusion.5
  106.2 0.1 pad_bitcast_fusion.3
  106.3 0.1 pad_bitcast_fusion.1
  106.6 1.1 pad_maximum_fusion.weights_ref
  107.6 2.9 %shard_map.104.weights_ref = bf16[4,1024,256]{2,1,0:T(8,128)(2,1)} custom-call(f32[4,512,128]{2,1,0:T(8,128)} %pad_maximum_fusion.weights_ref), custom_call_target="tpu_custom_call" | custom-call | tf_op jit(solution)/shard_map/pallas_call | solution.py:289
  110.5 0.1 reshape.38
  110.6 0.2 copy.31
  110.8 0.2 reshape.45.rows_ref
  111.0 0.2 copy.32
  111.1 0.2 reshape.46.rows_ref
  111.3 0.8 pad_add_fusion.rows_ref
  112.1 0.1 constant_dynamic-slice_fusion.3
  112.2 5.8 %fusion.refs_1_ = f32[64,4096]{1,0:T(8,128)} fusion(f32[64,4096]{1,0:T(8,128)} %collective-permute-done.6, f32[64,4096]{1,0:T(8,128)} %collective-permute-done.5, f32[64,4096]{1,0:T(8,128)} %collective-permute-done.4, f32[64,4096]{1,0:T(8,128)} %bitcast.65, f32[64,64]{0,1:T(8,128)S(1)} %bitcast.77, f32[64,64]{0,1:T(8,128)S(1)} %bitcast.78, ...), kind=kOutput, calls=%fused_computation | convolution fusion | flops 808501248 | bytes 5308416 | tf_op jit(solution)/shard_map/dot_general | solution.py:448
  118.0 16.4 %all-to-all-done.1 = f32[256,8,128]{2,1,0:T(8,128)S(1)} async-done(((f32[256,8,128]{2,1,0:T(8,128)}), f32[256,8,128]{2,1,0:T(8,128)S(1)}, u32[]{:S(2)}, u32[]{:S(2)}) %all-to-all-start.1) | async-done | bytes 1048608 | tf_op jit(solution)/shard_map/all_to_all | solution.py:442
  134.5 2.0 %shard_map.105 = (f32[512,128]{1,0:T(8,128)S(1)}, f32[512,128]{1,0:T(8,128)}, f32[512,128]{1,0:T(8,128)}, f32[512,128]{1,0:T(8,128)}) custom-call(f32[64,4,8,128]{3,2,1,0:T(8,128)S(1)} %bitcast.58, bf16[4,1024,256]{2,1,0:T(8,128)(2,1)S(1)} %copy-done), custom_call_target="tpu_custom_call" | custom-call | flops 10000000 | bytes 4194304 | tf_op jit(solution)/shard_map/pallas_call | solution.py:326
  136.5 2.1 %collective-permute-start.9 = (f32[512,128]{1,0:T(8,128)}, f32[512,128]{1,0:T(8,128)S(1)}, u32[]{:S(2)}, u32[]{:S(2)}) collective-permute-start(f32[512,128]{1,0:T(8,128)} %get-tuple-element.70), channel_id=1, source_target_pairs={{0,2},{1,3},{2,0},{3,1},{4,6},{5,7},{6,4},{7,5},{8,10},{9,11},{10,... | collective-permute-start | bytes 786440 | tf_op jit(solution)/shard_map/ppermute | solution.py:401
  138.6 0.9 collective-permute-start.7
  139.5 0.6 collective-permute-start.8
  140.2 1.2 copy-done.3
  141.4 3.2 %shard_map.106.refs_1_ = f32[64,4096]{1,0:T(8,128)S(1)} custom-call(s32[1024]{0:T(1024)S(1)} %reshape.45.rows_ref, f32[512,128]{1,0:T(8,128)S(1)} %get-tuple-element.72.refs_0_, f32[64,4096]{1,0:T(8,128)S(1)} %copy-done.3), custom_call_target="tpu_custom_call" | custom-call | flops 10000000 | bytes 16777216 | tf_op jit(solution)/shard_map/pallas_call | solution.py:388
  144.6 1.8 %collective-permute-done.9.refs_0_ = f32[512,128]{1,0:T(8,128)S(1)} collective-permute-done((f32[512,128]{1,0:T(8,128)}, f32[512,128]{1,0:T(8,128)S(1)}, u32[]{:S(2)}, u32[]{:S(2)}) %collective-permute-start.9) | collective-permute-done | bytes 262176 | tf_op jit(solution)/shard_map/ppermute | solution.py:401
  146.4 3.4 %shard_map.107.refs_2_ = f32[64,4096]{1,0:T(8,128)S(1)} custom-call(s32[1024]{0:T(1024)S(1)} %reshape.46.rows_ref, f32[512,128]{1,0:T(8,128)S(1)} %collective-permute-done.9.refs_0_, f32[64,4096]{1,0:T(8,128)S(1)} %shard_map.106.refs_1_), custom_call_target="tpu_custom_call" | custom-call | flops 10000000 | bytes 16777216 | tf_op jit(solution)/shard_map/pallas_call | solution.py:388
  149.7 1.7 %collective-permute-done.7.refs_0_ = f32[512,128]{1,0:T(8,128)S(1)} collective-permute-done((f32[512,128]{1,0:T(8,128)}, f32[512,128]{1,0:T(8,128)S(1)}, u32[]{:S(2)}, u32[]{:S(2)}) %collective-permute-start.7) | collective-permute-done | bytes 262176 | tf_op jit(solution)/shard_map/ppermute | solution.py:401
  151.5 0.7 collective-permute-done.8.refs_1_
  152.1 6.0 %shard_map.108 = f32[64,4096]{1,0:T(8,128)} custom-call(s32[2048]{0:T(1024)S(1)} %pad_add_fusion.rows_ref, f32[512,128]{1,0:T(8,128)S(1)} %collective-permute-done.7.refs_0_, f32[512,128]{1,0:T(8,128)S(1)} %collective-permute-done.8.refs_1_, f32[64,4096]{1,0:T(8,128)S(1)} %shard_map.107.refs_2_, f32[64,1]{1,0:T(8,128)S(1)} %copy.33.refs_3_), custom_call_target="tpu_custom_call" | custom-call | flops 10000000 | bytes 16777216 | tf_op jit(solution)/shard_map/pallas_call | solution.py:388
  (34 shorter events, 0.7 us)
Async XLA Ops:
  0.0 23.2 %copy-start.6 = (f32[256,64]{0,1:T(8,128)S(1)}, f32[256,64]{0,1:T(8,128)}, u32[]{:S(2)}) copy-start(f32[256,64]{0,1:T(8,128)} %param.12) | copy-start | bytes 196612
  0.0 34.9 %copy-start.4 = (s32[1,96]{1,0:T(1,128)S(1)}, s32[1,96]{1,0:T(1,128)}, u32[]{:S(2)}) copy-start(s32[1,96]{1,0:T(1,128)} %param.17) | copy-start | bytes 1156
  0.0 34.9 %copy-start.5 = (s32[1,96]{1,0:T(1,128)S(1)}, s32[1,96]{1,0:T(1,128)}, u32[]{:S(2)}) copy-start(s32[1,96]{1,0:T(1,128)} %param.18) | copy-start | bytes 1156
  10.0 74.2 %all-to-all-start = ((f32[64,80,128]{2,1,0:T(8,128)}), f32[64,80,128]{2,1,0:T(8,128)S(1)}, u32[]{:S(2)}, u32[]{:S(2)}) async-start(f32[64,80,128]{2,1,0:T(8,128)} %shard_map.100), calls=%async_computation | async-start | bytes 5242880 | tf_op jit(solution)/shard_map/all_to_all | solution.py:422
  23.2 3.9 %collective-permute-start = (f32[256,64]{0,1:T(8,128)S(1)}, f32[256,64]{0,1:T(8,128)S(1)}, u32[]{:S(2)}, u32[]{:S(2)}) collective-permute-start(f32[256,64]{0,1:T(8,128)S(1)} %copy-done.6), channel_id=1, source_target_pairs={{0,3},{1,0},{2,1},{3,2},{4,7},{5,4},{6,5},{7,6},{8,11},{9,8},{10,9... | collective-permute-start | bytes 196616 | tf_op jit(solution)/shard_map/ppermute | solution.py:401
  25.8 4.9 %collective-permute-start.1 = (f32[256,64]{0,1:T(8,128)S(1)}, f32[256,64]{0,1:T(8,128)S(1)}, u32[]{:S(2)}, u32[]{:S(2)}) collective-permute-start(f32[256,64]{0,1:T(8,128)S(1)} %copy-done.6), channel_id=1, source_target_pairs={{0,2},{1,3},{2,0},{3,1},{4,6},{5,7},{6,4},{7,5},{8,10},{9,11},{10,... | collective-permute-start | bytes 196616 | tf_op jit(solution)/shard_map/ppermute | solution.py:401
  26.3 5.3 %collective-permute-start.2 = (f32[256,64]{0,1:T(8,128)S(1)}, f32[256,64]{0,1:T(8,128)S(1)}, u32[]{:S(2)}, u32[]{:S(2)}) collective-permute-start(f32[256,64]{0,1:T(8,128)S(1)} %copy-done.6), channel_id=1, source_target_pairs={{0,1},{1,2},{2,3},{3,0},{4,5},{5,6},{6,7},{7,4},{8,9},{9,10},{10,1... | collective-permute-start | bytes 196616 | tf_op jit(solution)/shard_map/ppermute | solution.py:401
  31.6 64.4 %collective-permute-start.4 = (f32[64,4096]{1,0:T(8,128)}, f32[64,4096]{1,0:T(8,128)}, u32[]{:S(2)}, u32[]{:S(2)}) collective-permute-start(f32[64,4096]{1,0:T(8,128)} %bitcast.62), channel_id=1, source_target_pairs={{0,1},{1,2},{2,3},{3,0},{4,5},{5,6},{6,7},{7,4},{8,9},{9,10},{10,1... | collective-permute-start | bytes 3145736 | tf_op jit(solution)/shard_map/ppermute | solution.py:401
  31.6 64.4 %collective-permute-start.5 = (f32[64,4096]{1,0:T(8,128)}, f32[64,4096]{1,0:T(8,128)}, u32[]{:S(2)}, u32[]{:S(2)}) collective-permute-start(f32[64,4096]{1,0:T(8,128)} %bitcast.63), channel_id=1, source_target_pairs={{0,2},{1,3},{2,0},{3,1},{4,6},{5,7},{6,4},{7,5},{8,10},{9,11},{10,... | collective-permute-start | bytes 3145736 | tf_op jit(solution)/shard_map/ppermute | solution.py:401
  33.1 63.0 %collective-permute-start.6 = (f32[64,4096]{1,0:T(8,128)}, f32[64,4096]{1,0:T(8,128)}, u32[]{:S(2)}, u32[]{:S(2)}) collective-permute-start(f32[64,4096]{1,0:T(8,128)} %bitcast.64), channel_id=1, source_target_pairs={{0,3},{1,0},{2,1},{3,2},{4,7},{5,4},{6,5},{7,6},{8,11},{9,8},{10,9... | collective-permute-start | bytes 3145736 | tf_op jit(solution)/shard_map/ppermute | solution.py:401
  35.0 2.8 %copy-start.2 = (f32[1,96,128,128]{3,2,1,0:T(8,128)S(1)}, f32[1,96,128,128]{3,2,1,0:T(8,128)}, u32[]{:S(2)}) copy-start(f32[1,96,128,128]{3,2,1,0:T(8,128)} %param.19) | copy-start | bytes 18874372
  40.1 2.6 %copy-start.1 = (bf16[96,128,256]{2,1,0:T(8,128)(2,1)}, bf16[96,128,256]{2,1,0:T(8,128)(2,1)S(1)}, u32[]{:S(2)}) copy-start(bf16[96,128,256]{2,1,0:T(8,128)(2,1)S(1)} %get-tuple-element.44.tiles_hbm) | copy-start | bytes 18874372
  84.3 7.6 %collective-permute-start.3 = (f32[64,16,128]{2,1,0:T(8,128)S(1)}, f32[64,16,128]{2,1,0:T(8,128)}, u32[]{:S(2)}, u32[]{:S(2)}) collective-permute-start(f32[64,16,128]{2,1,0:T(8,128)S(1)} %slice.3.own_ref), channel_id=1, source_target_pairs={{0,4},{4,0},{8,12},{12,8},{16,20},{20,16},{24,28},{28,24},{32,36},... | collective-permute-start | bytes 1572872 | tf_op jit(solution)/shard_map/ppermute | solution.py:435
  91.9 11.8 %copy-start.8 = (s32[1,64,64]{2,1,0:T(8,128)S(1)}, s32[1,64,64]{2,1,0:T(8,128)}, u32[]{:S(2)}) copy-start(s32[1,64,64]{2,1,0:T(8,128)} %param.16) | copy-start | bytes 49156
  96.0 38.4 %all-to-all-start.1 = ((f32[256,8,128]{2,1,0:T(8,128)}), f32[256,8,128]{2,1,0:T(8,128)S(1)}, u32[]{:S(2)}, u32[]{:S(2)}) async-start(f32[256,8,128]{2,1,0:T(8,128)} %shard_map.103), calls=%async_computation.1 | async-start | bytes 2097152 | tf_op jit(solution)/shard_map/all_to_all | solution.py:442
  106.1 4.4 %copy-start.7 = (f32[256,64]{0,1:T(8,128)S(1)}, f32[256,64]{0,1:T(8,128)}, u32[]{:S(2)}) copy-start(f32[256,64]{0,1:T(8,128)} %param.11) | copy-start | bytes 196612
  110.8 23.7 %copy-start = (bf16[4,1024,256]{2,1,0:T(8,128)(2,1)S(1)}, bf16[4,1024,256]{2,1,0:T(8,128)(2,1)}, u32[]{:S(2)}) copy-start(bf16[4,1024,256]{2,1,0:T(8,128)(2,1)} %shard_map.104.weights_ref) | copy-start | bytes 6291460
  112.2 27.8 %copy-start.9 = (f32[64]{0:T(128)S(1)}, f32[64]{0:T(128)}, u32[]{:S(2)}) copy-start(f32[64]{0:T(128)} %param.13) | copy-start | bytes 772
  136.5 9.9 %collective-permute-start.9 = (f32[512,128]{1,0:T(8,128)}, f32[512,128]{1,0:T(8,128)S(1)}, u32[]{:S(2)}, u32[]{:S(2)}) collective-permute-start(f32[512,128]{1,0:T(8,128)} %get-tuple-element.70), channel_id=1, source_target_pairs={{0,2},{1,3},{2,0},{3,1},{4,6},{5,7},{6,4},{7,5},{8,10},{9,11},{10,... | collective-permute-start | bytes 786440 | tf_op jit(solution)/shard_map/ppermute | solution.py:401
  138.6 12.9 %collective-permute-start.7 = (f32[512,128]{1,0:T(8,128)}, f32[512,128]{1,0:T(8,128)S(1)}, u32[]{:S(2)}, u32[]{:S(2)}) collective-permute-start(f32[512,128]{1,0:T(8,128)} %get-tuple-element.67), channel_id=1, source_target_pairs={{0,3},{1,0},{2,1},{3,2},{4,7},{5,4},{6,5},{7,6},{8,11},{9,8},{10,9... | collective-permute-start | bytes 786440 | tf_op jit(solution)/shard_map/ppermute | solution.py:401
  139.5 12.7 %collective-permute-start.8 = (f32[512,128]{1,0:T(8,128)}, f32[512,128]{1,0:T(8,128)S(1)}, u32[]{:S(2)}, u32[]{:S(2)}) collective-permute-start(f32[512,128]{1,0:T(8,128)} %get-tuple-element.68), channel_id=1, source_target_pairs={{0,1},{1,2},{2,3},{3,0},{4,5},{5,6},{6,7},{7,4},{8,9},{9,10},{10,1... | collective-permute-start | bytes 786440 | tf_op jit(solution)/shard_map/ppermute | solution.py:401
  140.2 1.2 copy-start.3

commit v7 on v6

--- a/solution.py
+++ b/solution.py
@@ -149,14 +149,12 @@
 
 
 def multiply(tile, block):
-    left = left_half(block.shape)
-    top = block.astype(jnp.bfloat16).astype(jnp.float32)
-    mid = block - top
+    top, mid = split(block)
     right_side = jnp.concatenate(
-        [jnp.where(left, top, mid).astype(jnp.bfloat16), jnp.where(left, mid, top).astype(jnp.bfloat16)], axis=0
+        [jnp.concatenate([top, mid], axis=1), jnp.concatenate([mid, top], axis=1)], axis=0
     )
     product = jnp.dot(tile, right_side, preferred_element_type=jnp.float32)
-    return product + pltpu.roll(product, HALF, 1)
+    return product[:, :LANES] + product[:, LANES:]
 
 
 def packed_sums(acc_ref, block, part):
@@ -166,8 +164,10 @@
 
 
 def listed_kernel(
-    dst_ref, tiles_hbm, mirror_ref, acc_ref, hub_tiles_ref, tiles_ref, sems, hub_sem, *, first, rows
+    dst_hbm, tiles_hbm, mirror_ref, acc_ref, hub_tiles_ref, dst_ref, tiles_ref, sems, hub_sem, dst_sem, *, first, rows
 ):
+    places = pltpu.make_async_copy(dst_hbm, dst_ref, dst_sem)
+    places.start()
     chunks = sems.shape[0]
     count = tiles_ref.shape[0] // chunks
 
@@ -182,11 +182,16 @@
             tiles_hbm.at[pl.ds(first + c * piece, piece)], tiles_ref.at[pl.ds(c * piece, piece)], sems.at[c // 4]
         ).start()
     hubs = pltpu.make_async_copy(tiles_hbm.at[pl.ds(0, first)], hub_tiles_ref, hub_sem)
-    hubs.start()
     acc_ref[...] = jnp.zeros_like(acc_ref)
+    places.wait()
 
     def chunk(c, carry):
         fetch(c).wait()
+
+        @pl.when(c == 1)
+        def _():
+            hubs.start()
+
         for i in range(count):
             tile = c * count + i
             low, high = unpack(mirror_ref[tile, :rows, :])
@@ -203,11 +208,13 @@
     whole = pl.BlockSpec(memory_space=pltpu.VMEM)
     return pl.pallas_call(
         functools.partial(listed_kernel, first=first, rows=rows),
-        in_specs=[pl.BlockSpec(memory_space=pltpu.SMEM), pl.BlockSpec(memory_space=pltpu.HBM), whole],
+        in_specs=[pl.BlockSpec(memory_space=pltpu.HBM), pl.BlockSpec(memory_space=pltpu.HBM), whole],
         out_specs=[whole, whole],
         scratch_shapes=[
+            pltpu.SMEM(order.shape, jnp.int32),
             pltpu.VMEM((count, size, 2 * size), jnp.bfloat16),
             pltpu.SemaphoreType.DMA((8,)),
+            pltpu.SemaphoreType.DMA,
             pltpu.SemaphoreType.DMA,
         ],
         out_shape=[
@@ -220,12 +227,15 @@
 
 
 def hub_kernel(
-    dst_ref, side_ref, tiles_ref, own_ref, other_ref, before_ref, out_hbm, hubs_ref, acc_ref, out_ref, out_sems
+    dst_hbm, tiles_ref, own_ref, other_ref, before_ref, out_hbm, dst_ref, hubs_ref, acc_ref, out_ref, out_sems, dst_sem
 ):
+    places = pltpu.make_async_copy(dst_hbm, dst_ref, dst_sem)
+    places.start()
     count = 8
     chunks = tiles_ref.shape[0] // count
-    side = side_ref[0]
     acc_ref[...] = before_ref[...]
+    places.wait()
+    side = dst_ref[dst_ref.shape[0] - 1]
     hubs_ref[side] = own_ref[...]
     hubs_ref[1 - side] = other_ref[...]
 
@@ -254,24 +264,25 @@
         copy.wait()
 
 
-def hub_tiles(split_vals, own, other, before, order, side):
+def hub_tiles(split_vals, own, other, before, order):
     blocks, size, _ = before.shape
-    scalars = pl.BlockSpec(memory_space=pltpu.SMEM)
     result = jax.ShapeDtypeStruct((blocks * 8, 8, LANES), jnp.float32)
     return pl.pallas_call(
         hub_kernel,
-        in_specs=[scalars, scalars] + [pl.BlockSpec(memory_space=pltpu.VMEM)] * 4,
+        in_specs=[pl.BlockSpec(memory_space=pltpu.HBM)] + [pl.BlockSpec(memory_space=pltpu.VMEM)] * 4,
         out_specs=pl.BlockSpec(memory_space=pltpu.HBM),
         scratch_shapes=[
+            pltpu.SMEM(order.shape, jnp.int32),
             pltpu.VMEM((2,) + own.shape, jnp.float32),
             pltpu.VMEM(before.shape, jnp.float32),
             pltpu.VMEM(result.shape, jnp.float32),
             pltpu.SemaphoreType.DMA((4,)),
+            pltpu.SemaphoreType.DMA,
         ],
         out_shape=result,
         compiler_params=pltpu.CompilerParams(vmem_limit_bytes=KERNEL_VMEM),
         cost_estimate=pl.CostEstimate(flops=10**9, bytes_accessed=6 * 2**20, transcendentals=0),
-    )(order, side, split_vals, own, other, before)
+    )(order, split_vals, own, other, before)
 
 
 def weights_kernel(weights_ref, out_ref):
@@ -337,7 +348,10 @@
     )(slots, weights)
 
 
-def scatter_kernel(rows_ref, *refs, blocks, bases, last):
+def scatter_kernel(rows_hbm, *refs, blocks, bases, last):
+    *refs, rows_ref, rows_sem = refs
+    lists = pltpu.make_async_copy(rows_hbm, rows_ref, rows_sem)
+    lists.start()
     parts = refs[:blocks]
     base_refs = refs[blocks : blocks + bases]
     bias_ref = refs[blocks + bases] if last else None
@@ -348,6 +362,7 @@
         out_ref, *sums = refs
     for total in sums:
         total[...] = jnp.zeros_like(total)
+    lists.wait()
     left = left_half((1, LANES))
     zero = jnp.zeros((1, LANES), jnp.float32)
     lanes = len(sums) // 2
@@ -387,11 +402,12 @@
     vmem = pl.BlockSpec(memory_space=pltpu.VMEM)
     return pl.pallas_call(
         functools.partial(scatter_kernel, blocks=len(parts), bases=len(bases), last=last),
-        in_specs=[pl.BlockSpec(memory_space=pltpu.SMEM)] + [vmem] * (len(parts) + len(bases) + last),
+        in_specs=[pl.BlockSpec(memory_space=pltpu.HBM)] + [vmem] * (len(parts) + len(bases) + last),
         out_specs=pl.BlockSpec(memory_space=pltpu.HBM) if last else vmem,
         out_shape=jax.ShapeDtypeStruct((HALF, row_count), jnp.float32),
         scratch_shapes=[pltpu.VMEM((row_count + 8, LANES), jnp.float32)] * 4
-        + ([pltpu.VMEM((HALF, row_count), jnp.float32), pltpu.SemaphoreType.DMA((8,))] if last else []),
+        + ([pltpu.VMEM((HALF, row_count), jnp.float32), pltpu.SemaphoreType.DMA((8,))] if last else [])
+        + [pltpu.SMEM(rows.shape, jnp.int32), pltpu.SemaphoreType.DMA],
         compiler_params=pltpu.CompilerParams(vmem_limit_bytes=13 * 2**20),
         cost_estimate=pl.CostEstimate(flops=10**7, bytes_accessed=16 * 2**20, transcendentals=0),
     )(rows, *parts, *bases, *([bias] if last else []))
@@ -428,14 +444,15 @@
     blocks = [xt] + [shifted(xt, feat, d) for d in range(1, feat)]
     split_vals, tile_order = split_tiles(tiles, tile_src[0], tile_dst[0])
 
+    side = (lax.axis_index("dom") % 2).astype(jnp.int32).reshape(1)
+    tile_order = jnp.concatenate([tile_order, jnp.zeros((31,), jnp.int32), side])
     mirror, split_vals, tile_order = lax.optimization_barrier((mirror, split_vals, tile_order))
     rows = slot // 2
     hub_count = hub_rows.shape[1] * peers // slot
     hub_half = mirror[:, rows:]
     hub_other = lax.ppermute(hub_half, "dom", [(i, i ^ 1) for i in range(peers)])
-    side = (lax.axis_index("dom") % 2).astype(jnp.int32).reshape(1)
     partial, hub_vals = listed_tiles(split_vals, mirror, tile_order, rows, hub_count, peers * ret // slot)
-    partial = hub_tiles(hub_vals, hub_half, hub_other, partial, tile_order, side)
+    partial = hub_tiles(hub_vals, hub_half, hub_other, partial, tile_order)
     partial, blocks, neighbours, w_self, ret_rows = lax.optimization_barrier(
         (partial, blocks, neighbours, w_self, ret_rows)
     )

time: 159 us -> 156 us (0.981)
  Pallas kernels: 39.4 us -> 35.9 us
  transfers between devices with their start and end apart: 12 -> 12, of which waited for: 8 -> 8; matrix products, arithmetic and copies ran while one was open for 7% -> 7% of each run, Pallas kernels for 13% -> 12%
where the time goes in v7:
time: 156 us
  waiting for transfers between devices  67.8 us (43%)
  Pallas kernels  35.9 us (23%)
  starting transfers between devices  33.4 us (21%)
  local copies, waits for them, and re-layouts  10.4 us (7%)
  matrix products  5.79 us (4%)
  other arithmetic  2.01 us (1%)
    all_to_all x1, waiting for transfers between devices, per_device(): lax.all_to_all(outgoing, 'dom', split_axis=0, concat_axis=0, tiled=True)  41.4 us
    all_to_all x1, waiting for transfers between devices, per_device(): lax.all_to_all(partial, ('dom', 'feat'), split_axis=0, concat_axis=0, til...  16.4 us
    all_to_all x1, starting transfers between devices, per_device(): lax.all_to_all(outgoing, 'dom', split_axis=0, concat_axis=0, tiled=True)  13.2 us
    pallas_call x3, Pallas kernels, scatter_rows(): pl.pallas_call(functools.partial(scatter_kernel, blocks=len(parts), bases...  11 us
    ppermute x9, starting transfers between devices, shifted(): lax.ppermute(value, 'feat', [(i, (i + step) % count) for i in range(count)])  10.6 us
    pallas_call x1, Pallas kernels, gather_rows(): pl.pallas_call(functools.partial(gather_kernel, rows=rows, hub_rows=hub_r...  10 us
    ppermute x9, waiting for transfers between devices, shifted(): lax.ppermute(value, 'feat', [(i, (i + step) % count) for i in range(count)])  9.88 us
    all_to_all x1, starting transfers between devices, per_device(): lax.all_to_all(partial, ('dom', 'feat'), split_axis=0, concat_axis=0, til...  7.48 us
  transfers between devices with their start and end apart: 12, of which 8 were waited for; matrix products, arithmetic and copies ran while one was open for 7% of the time, Pallas kernels for 12%

profile of v7, /device:TPU:1, one launch (start us, length us, event | category | flops | bytes accessed | tf_op | source)
XLA Modules:
  0.0 155.8 jit_solution(10510510163133413799)
XLA Ops:
  0.0 10.0 %shard_map.100 = f32[64,80,128]{2,1,0:T(8,128)} custom-call(s32[8192]{0:T(1024)} %bitcast.75, s32[64]{0:T(128)} %bitcast.81, f32[64,4096]{1,0:T(8,128)} %bitcast.61), custom_call_target="tpu_custom_call" | custom-call | flops 10000000 | bytes 4194304 | tf_op jit(solution)/shard_map/pallas_call | solution.py:84
  10.0 13.2 %all-to-all-start = ((f32[64,80,128]{2,1,0:T(8,128)}), f32[64,80,128]{2,1,0:T(8,128)S(1)}, u32[]{:S(2)}, u32[]{:S(2)}) async-start(f32[64,80,128]{2,1,0:T(8,128)} %shard_map.100), calls=%async_computation | async-start | bytes 5242880 | tf_op jit(solution)/shard_map/all_to_all | solution.py:438
  23.2 2.6 %collective-permute-start = (f32[256,64]{0,1:T(8,128)S(1)}, f32[256,64]{0,1:T(8,128)S(1)}, u32[]{:S(2)}, u32[]{:S(2)}) collective-permute-start(f32[256,64]{0,1:T(8,128)S(1)} %copy-done.6), channel_id=1, source_target_pairs={{0,3},{1,0},{2,1},{3,2},{4,7},{5,4},{6,5},{7,6},{8,11},{9,8},{10,9... | collective-permute-start | bytes 196616 | tf_op jit(solution)/shard_map/ppermute | solution.py:417
  25.8 0.5 collective-permute-start.1
  26.3 0.6 collective-permute-start.2
  26.9 0.2 collective-permute-done
  27.1 3.6 %collective-permute-done.1 = f32[256,64]{0,1:T(8,128)S(1)} collective-permute-done((f32[256,64]{0,1:T(8,128)S(1)}, f32[256,64]{0,1:T(8,128)S(1)}, u32[]{:S(2)}, u32[]{:S(2)}) %collective-permute-start.1) | collective-permute-done | bytes 65568 | tf_op jit(solution)/shard_map/ppermute | solution.py:417
  30.7 0.9 collective-permute-done.2
  31.6 1.5 collective-permute-start.5
  33.1 1.9 %collective-permute-start.6 = (f32[64,4096]{1,0:T(8,128)}, f32[64,4096]{1,0:T(8,128)}, u32[]{:S(2)}, u32[]{:S(2)}) collective-permute-start(f32[64,4096]{1,0:T(8,128)} %bitcast.64), channel_id=1, source_target_pairs={{0,3},{1,0},{2,1},{3,2},{4,7},{5,4},{6,5},{7,6},{8,11},{9,8},{10,9... | collective-permute-start | bytes 3145736 | tf_op jit(solution)/shard_map/ppermute | solution.py:417
  35.0 2.8 %copy-done.2 = f32[1,96,128,128]{3,2,1,0:T(8,128)S(1)} copy-done((f32[1,96,128,128]{3,2,1,0:T(8,128)S(1)}, f32[1,96,128,128]{3,2,1,0:T(8,128)}, u32[]{:S(2)}) %copy-start.2) | copy-done | bytes 6291480
  37.7 2.4 %shard_map.101 = (bf16[96,128,256]{2,1,0:T(8,128)(2,1)S(1)}, s32[96]{0:T(128)S(1)}) custom-call(s32[96]{0:T(128)S(1)} %bitcast.59, s32[96]{0:T(128)S(1)} %bitcast.60, f32[96,128,128]{2,1,0:T(8,128)S(1)} %bitcast.57), custom_call_target="tpu_custom_call" | custom-call | flops 10000000 | bytes 12582912 | tf_op jit(solution)/shard_map/pallas_call | solution.py:125
  40.1 2.6 %copy-done.1 = bf16[96,128,256]{2,1,0:T(8,128)(2,1)} copy-done((bf16[96,128,256]{2,1,0:T(8,128)(2,1)}, bf16[96,128,256]{2,1,0:T(8,128)(2,1)S(1)}, u32[]{:S(2)}) %copy-start.1) | copy-done | bytes 6291480
  42.8 41.4 %all-to-all-done.mirror_ref = f32[64,80,128]{2,1,0:T(8,128)S(1)} async-done(((f32[64,80,128]{2,1,0:T(8,128)}), f32[64,80,128]{2,1,0:T(8,128)S(1)}, u32[]{:S(2)}, u32[]{:S(2)}) %all-to-all-start) | async-done | bytes 2621472 | tf_op jit(solution)/shard_map/all_to_all | solution.py:438
  84.3 2.1 %collective-permute-start.3 = (f32[64,16,128]{2,1,0:T(8,128)S(1)}, f32[64,16,128]{2,1,0:T(8,128)S(1)}, u32[]{:S(2)}, u32[]{:S(2)}) collective-permute-start(f32[64,16,128]{2,1,0:T(8,128)S(1)} %slice.3.own_ref), channel_id=1, source_target_pairs={{0,4},{4,0},{8,12},{12,8},{16,20},{20,16},{24,28},{28,24},{32,36},... | collective-permute-start | bytes 1572872 | tf_op jit(solution)/shard_map/ppermute | solution.py:453
  86.4 4.4 %shard_map.102 = (f32[32,128,128]{2,1,0:T(8,128)S(1)}, bf16[32,128,256]{2,1,0:T(8,128)(2,1)S(1)}) custom-call(s32[128]{0:T(128)S(1)} %pad_add_fusion.1.dst_hbm, bf16[96,128,256]{2,1,0:T(8,128)(2,1)} %copy-done.1, f32[64,80,128]{2,1,0:T(8,128)S(1)} %all-to-all-done.mirror_ref), custom_call_target="tpu_custom_call" | custom-call | flops 1000000000 | bytes 10485760 | tf_op jit(solution)/shard_map/pallas_call | solution.py:209
  90.8 3.2 %shard_map.103 = f32[256,8,128]{2,1,0:T(8,128)} custom-call(s32[128]{0:T(128)S(1)} %pad_add_fusion.1.dst_hbm, bf16[32,128,256]{2,1,0:T(8,128)(2,1)S(1)} %get-tuple-element.46.tiles_ref, f32[64,16,128]{2,1,0:T(8,128)S(1)} %slice.3.own_ref, f32[64,16,128]{2,1,0:T(8,128)S(1)} %collective-permute-done.3.other_ref, f32[32,128,128]{2,1,0:T(8,128)S(1)} %get-tuple-element.47.before_ref), custom_call_target="tpu_custom_call" | custom-call | flops 1000000000 | bytes 6291456 | tf_op jit(solution)/shard_map/pallas_call | solution.py:270
  94.1 7.5 %all-to-all-start.1 = ((f32[256,8,128]{2,1,0:T(8,128)}), f32[256,8,128]{2,1,0:T(8,128)S(1)}, u32[]{:S(2)}, u32[]{:S(2)}) async-start(f32[256,8,128]{2,1,0:T(8,128)} %shard_map.103), calls=%async_computation.1 | async-start | bytes 2097152 | tf_op jit(solution)/shard_map/all_to_all | solution.py:459
  101.8 0.2 copy.29
  102.0 0.8 reshape.43
  102.7 0.2 copy.30
  102.9 0.8 reshape.44
  104.1 0.1 pad_bitcast_fusion.7
  104.3 0.1 pad_bitcast_fusion.3
  104.4 0.1 pad_bitcast_fusion.1
  104.6 1.1 pad_maximum_fusion.weights_ref
  105.6 2.9 %shard_map.104.weights_ref = bf16[4,1024,256]{2,1,0:T(8,128)(2,1)} custom-call(f32[4,512,128]{2,1,0:T(8,128)} %pad_maximum_fusion.weights_ref), custom_call_target="tpu_custom_call" | custom-call | tf_op jit(solution)/shard_map/pallas_call | solution.py:300
  108.5 0.1 reshape.38
  108.6 0.2 copy.31
  108.8 0.2 reshape.45.rows_hbm
  109.0 0.2 copy.32
  109.2 0.2 reshape.46.rows_hbm
  109.4 0.8 pad_add_fusion.rows_hbm
  110.2 0.1 constant_dynamic-slice_fusion.3
  110.3 5.8 %fusion.refs_1_ = f32[64,4096]{1,0:T(8,128)} fusion(f32[64,4096]{1,0:T(8,128)} %collective-permute-done.6, f32[64,4096]{1,0:T(8,128)} %collective-permute-done.5, f32[64,4096]{1,0:T(8,128)} %collective-permute-done.4, f32[64,4096]{1,0:T(8,128)} %bitcast.65, f32[64,64]{0,1:T(8,128)S(1)} %bitcast.77, f32[64,64]{0,1:T(8,128)S(1)} %bitcast.78, ...), kind=kOutput, calls=%fused_computation | convolution fusion | flops 808501248 | bytes 5308416 | tf_op jit(solution)/shard_map/dot_general | solution.py:465
  116.1 16.4 %all-to-all-done.1 = f32[256,8,128]{2,1,0:T(8,128)S(1)} async-done(((f32[256,8,128]{2,1,0:T(8,128)}), f32[256,8,128]{2,1,0:T(8,128)S(1)}, u32[]{:S(2)}, u32[]{:S(2)}) %all-to-all-start.1) | async-done | bytes 1048608 | tf_op jit(solution)/shard_map/all_to_all | solution.py:459
  132.5 2.0 %shard_map.105 = (f32[512,128]{1,0:T(8,128)S(1)}, f32[512,128]{1,0:T(8,128)}, f32[512,128]{1,0:T(8,128)}, f32[512,128]{1,0:T(8,128)}) custom-call(f32[64,4,8,128]{3,2,1,0:T(8,128)S(1)} %bitcast.58, bf16[4,1024,256]{2,1,0:T(8,128)(2,1)S(1)} %copy-done), custom_call_target="tpu_custom_call" | custom-call | flops 10000000 | bytes 4194304 | tf_op jit(solution)/shard_map/pallas_call | solution.py:337
  134.5 2.1 %collective-permute-start.9 = (f32[512,128]{1,0:T(8,128)}, f32[512,128]{1,0:T(8,128)S(1)}, u32[]{:S(2)}, u32[]{:S(2)}) collective-permute-start(f32[512,128]{1,0:T(8,128)} %get-tuple-element.70), channel_id=1, source_target_pairs={{0,2},{1,3},{2,0},{3,1},{4,6},{5,7},{6,4},{7,5},{8,10},{9,11},{10,... | collective-permute-start | bytes 786440 | tf_op jit(solution)/shard_map/ppermute | solution.py:417
  136.6 0.9 collective-permute-start.7
  137.5 0.6 collective-permute-start.8
  138.1 0.1 copy.33.refs_3_
  138.2 1.2 copy-done.3
  139.4 2.7 %shard_map.106.refs_1_ = f32[64,4096]{1,0:T(8,128)S(1)} custom-call(s32[1024]{0:T(1024)S(1)} %reshape.45.rows_hbm, f32[512,128]{1,0:T(8,128)S(1)} %get-tuple-element.72.refs_0_, f32[64,4096]{1,0:T(8,128)S(1)} %copy-done.3), custom_call_target="tpu_custom_call" | custom-call | flops 10000000 | bytes 16777216 | tf_op jit(solution)/shard_map/pallas_call | solution.py:403
  142.1 2.3 %collective-permute-done.9.refs_0_ = f32[512,128]{1,0:T(8,128)S(1)} collective-permute-done((f32[512,128]{1,0:T(8,128)}, f32[512,128]{1,0:T(8,128)S(1)}, u32[]{:S(2)}, u32[]{:S(2)}) %collective-permute-start.9) | collective-permute-done | bytes 262176 | tf_op jit(solution)/shard_map/ppermute | solution.py:417
  144.4 2.8 %shard_map.107.refs_2_ = f32[64,4096]{1,0:T(8,128)S(1)} custom-call(s32[1024]{0:T(1024)S(1)} %reshape.46.rows_hbm, f32[512,128]{1,0:T(8,128)S(1)} %collective-permute-done.9.refs_0_, f32[64,4096]{1,0:T(8,128)S(1)} %shard_map.106.refs_1_), custom_call_target="tpu_custom_call" | custom-call | flops 10000000 | bytes 16777216 | tf_op jit(solution)/shard_map/pallas_call | solution.py:403
  147.2 2.3 %collective-permute-done.7.refs_0_ = f32[512,128]{1,0:T(8,128)S(1)} collective-permute-done((f32[512,128]{1,0:T(8,128)}, f32[512,128]{1,0:T(8,128)S(1)}, u32[]{:S(2)}, u32[]{:S(2)}) %collective-permute-start.7) | collective-permute-done | bytes 262176 | tf_op jit(solution)/shard_map/ppermute | solution.py:417
  149.5 0.7 collective-permute-done.8.refs_1_
  150.2 5.5 %shard_map.108 = f32[64,4096]{1,0:T(8,128)} custom-call(s32[2048]{0:T(1024)S(1)} %pad_add_fusion.rows_hbm, f32[512,128]{1,0:T(8,128)S(1)} %collective-permute-done.7.refs_0_, f32[512,128]{1,0:T(8,128)S(1)} %collective-permute-done.8.refs_1_, f32[64,4096]{1,0:T(8,128)S(1)} %shard_map.107.refs_2_, f32[64,1]{1,0:T(8,128)S(1)} %copy.33.refs_3_), custom_call_target="tpu_custom_call" | custom-call | flops 10000000 | bytes 16777216 | tf_op jit(solution)/shard_map/pallas_call | solution.py:403
  (36 shorter events, 0.8 us)
Async XLA Ops:
  0.0 23.2 %copy-start.6 = (f32[256,64]{0,1:T(8,128)S(1)}, f32[256,64]{0,1:T(8,128)}, u32[]{:S(2)}) copy-start(f32[256,64]{0,1:T(8,128)} %param.12) | copy-start | bytes 196612
  0.0 34.9 %copy-start.4 = (s32[1,96]{1,0:T(1,128)S(1)}, s32[1,96]{1,0:T(1,128)}, u32[]{:S(2)}) copy-start(s32[1,96]{1,0:T(1,128)} %param.17) | copy-start | bytes 1156
  0.0 34.9 %copy-start.5 = (s32[1,96]{1,0:T(1,128)S(1)}, s32[1,96]{1,0:T(1,128)}, u32[]{:S(2)}) copy-start(s32[1,96]{1,0:T(1,128)} %param.18) | copy-start | bytes 1156
  10.0 74.2 %all-to-all-start = ((f32[64,80,128]{2,1,0:T(8,128)}), f32[64,80,128]{2,1,0:T(8,128)S(1)}, u32[]{:S(2)}, u32[]{:S(2)}) async-start(f32[64,80,128]{2,1,0:T(8,128)} %shard_map.100), calls=%async_computation | async-start | bytes 5242880 | tf_op jit(solution)/shard_map/all_to_all | solution.py:438
  23.2 3.9 %collective-permute-start = (f32[256,64]{0,1:T(8,128)S(1)}, f32[256,64]{0,1:T(8,128)S(1)}, u32[]{:S(2)}, u32[]{:S(2)}) collective-permute-start(f32[256,64]{0,1:T(8,128)S(1)} %copy-done.6), channel_id=1, source_target_pairs={{0,3},{1,0},{2,1},{3,2},{4,7},{5,4},{6,5},{7,6},{8,11},{9,8},{10,9... | collective-permute-start | bytes 196616 | tf_op jit(solution)/shard_map/ppermute | solution.py:417
  25.8 4.9 %collective-permute-start.1 = (f32[256,64]{0,1:T(8,128)S(1)}, f32[256,64]{0,1:T(8,128)S(1)}, u32[]{:S(2)}, u32[]{:S(2)}) collective-permute-start(f32[256,64]{0,1:T(8,128)S(1)} %copy-done.6), channel_id=1, source_target_pairs={{0,2},{1,3},{2,0},{3,1},{4,6},{5,7},{6,4},{7,5},{8,10},{9,11},{10,... | collective-permute-start | bytes 196616 | tf_op jit(solution)/shard_map/ppermute | solution.py:417
  26.3 5.3 %collective-permute-start.2 = (f32[256,64]{0,1:T(8,128)S(1)}, f32[256,64]{0,1:T(8,128)S(1)}, u32[]{:S(2)}, u32[]{:S(2)}) collective-permute-start(f32[256,64]{0,1:T(8,128)S(1)} %copy-done.6), channel_id=1, source_target_pairs={{0,1},{1,2},{2,3},{3,0},{4,5},{5,6},{6,7},{7,4},{8,9},{9,10},{10,1... | collective-permute-start | bytes 196616 | tf_op jit(solution)/shard_map/ppermute | solution.py:417
  31.6 62.5 %collective-permute-start.4 = (f32[64,4096]{1,0:T(8,128)}, f32[64,4096]{1,0:T(8,128)}, u32[]{:S(2)}, u32[]{:S(2)}) collective-permute-start(f32[64,4096]{1,0:T(8,128)} %bitcast.62), channel_id=1, source_target_pairs={{0,1},{1,2},{2,3},{3,0},{4,5},{5,6},{6,7},{7,4},{8,9},{9,10},{10,1... | collective-permute-start | bytes 3145736 | tf_op jit(solution)/shard_map/ppermute | solution.py:417
  31.6 62.5 %collective-permute-start.5 = (f32[64,4096]{1,0:T(8,128)}, f32[64,4096]{1,0:T(8,128)}, u32[]{:S(2)}, u32[]{:S(2)}) collective-permute-start(f32[64,4096]{1,0:T(8,128)} %bitcast.63), channel_id=1, source_target_pairs={{0,2},{1,3},{2,0},{3,1},{4,6},{5,7},{6,4},{7,5},{8,10},{9,11},{10,... | collective-permute-start | bytes 3145736 | tf_op jit(solution)/shard_map/ppermute | solution.py:417
  33.1 61.0 %collective-permute-start.6 = (f32[64,4096]{1,0:T(8,128)}, f32[64,4096]{1,0:T(8,128)}, u32[]{:S(2)}, u32[]{:S(2)}) collective-permute-start(f32[64,4096]{1,0:T(8,128)} %bitcast.64), channel_id=1, source_target_pairs={{0,3},{1,0},{2,1},{3,2},{4,7},{5,4},{6,5},{7,6},{8,11},{9,8},{10,9... | collective-permute-start | bytes 3145736 | tf_op jit(solution)/shard_map/ppermute | solution.py:417
  35.0 2.8 %copy-start.2 = (f32[1,96,128,128]{3,2,1,0:T(8,128)S(1)}, f32[1,96,128,128]{3,2,1,0:T(8,128)}, u32[]{:S(2)}) copy-start(f32[1,96,128,128]{3,2,1,0:T(8,128)} %param.19) | copy-start | bytes 18874372
  40.1 2.6 %copy-start.1 = (bf16[96,128,256]{2,1,0:T(8,128)(2,1)}, bf16[96,128,256]{2,1,0:T(8,128)(2,1)S(1)}, u32[]{:S(2)}) copy-start(bf16[96,128,256]{2,1,0:T(8,128)(2,1)S(1)} %get-tuple-element.44.tiles_hbm) | copy-start | bytes 18874372
  84.3 6.5 %collective-permute-start.3 = (f32[64,16,128]{2,1,0:T(8,128)S(1)}, f32[64,16,128]{2,1,0:T(8,128)S(1)}, u32[]{:S(2)}, u32[]{:S(2)}) collective-permute-start(f32[64,16,128]{2,1,0:T(8,128)S(1)} %slice.3.own_ref), channel_id=1, source_target_pairs={{0,4},{4,0},{8,12},{12,8},{16,20},{20,16},{24,28},{28,24},{32,36},... | collective-permute-start | bytes 1572872 | tf_op jit(solution)/shard_map/ppermute | solution.py:453
  90.8 10.9 %copy-start.8 = (s32[1,64,64]{2,1,0:T(8,128)S(1)}, s32[1,64,64]{2,1,0:T(8,128)}, u32[]{:S(2)}) copy-start(s32[1,64,64]{2,1,0:T(8,128)} %param.16) | copy-start | bytes 49156
  94.1 38.4 %all-to-all-start.1 = ((f32[256,8,128]{2,1,0:T(8,128)}), f32[256,8,128]{2,1,0:T(8,128)S(1)}, u32[]{:S(2)}, u32[]{:S(2)}) async-start(f32[256,8,128]{2,1,0:T(8,128)} %shard_map.103), calls=%async_computation.1 | async-start | bytes 2097152 | tf_op jit(solution)/shard_map/all_to_all | solution.py:459
  104.2 4.4 %copy-start.7 = (f32[256,64]{0,1:T(8,128)S(1)}, f32[256,64]{0,1:T(8,128)}, u32[]{:S(2)}) copy-start(f32[256,64]{0,1:T(8,128)} %param.11) | copy-start | bytes 196612
  108.8 23.7 %copy-start = (bf16[4,1024,256]{2,1,0:T(8,128)(2,1)S(1)}, bf16[4,1024,256]{2,1,0:T(8,128)(2,1)}, u32[]{:S(2)}) copy-start(bf16[4,1024,256]{2,1,0:T(8,128)(2,1)} %shard_map.104.weights_ref) | copy-start | bytes 6291460
  110.3 27.8 %copy-start.9 = (f32[64]{0:T(128)S(1)}, f32[64]{0:T(128)}, u32[]{:S(2)}) copy-start(f32[64]{0:T(128)} %param.13) | copy-start | bytes 772
  134.5 9.9 %collective-permute-start.9 = (f32[512,128]{1,0:T(8,128)}, f32[512,128]{1,0:T(8,128)S(1)}, u32[]{:S(2)}, u32[]{:S(2)}) collective-permute-start(f32[512,128]{1,0:T(8,128)} %get-tuple-element.70), channel_id=1, source_target_pairs={{0,2},{1,3},{2,0},{3,1},{4,6},{5,7},{6,4},{7,5},{8,10},{9,11},{10,... | collective-permute-start | bytes 786440 | tf_op jit(solution)/shard_map/ppermute | solution.py:417
  136.6 12.9 %collective-permute-start.7 = (f32[512,128]{1,0:T(8,128)}, f32[512,128]{1,0:T(8,128)S(1)}, u32[]{:S(2)}, u32[]{:S(2)}) collective-permute-start(f32[512,128]{1,0:T(8,128)} %get-tuple-element.67), channel_id=1, source_target_pairs={{0,3},{1,0},{2,1},{3,2},{4,7},{5,4},{6,5},{7,6},{8,11},{9,8},{10,9... | collective-permute-start | bytes 786440 | tf_op jit(solution)/shard_map/ppermute | solution.py:417
  137.5 12.7 %collective-permute-start.8 = (f32[512,128]{1,0:T(8,128)}, f32[512,128]{1,0:T(8,128)S(1)}, u32[]{:S(2)}, u32[]{:S(2)}) collective-permute-start(f32[512,128]{1,0:T(8,128)} %get-tuple-element.68), channel_id=1, source_target_pairs={{0,1},{1,2},{2,3},{3,0},{4,5},{5,6},{6,7},{7,4},{8,9},{9,10},{10,1... | collective-permute-start | bytes 786440 | tf_op jit(solution)/shard_map/ppermute | solution.py:417
  138.2 1.2 copy-start.3

commit v8 on v7

--- a/solution.py
+++ b/solution.py
@@ -227,7 +227,7 @@
 
 
 def hub_kernel(
-    dst_hbm, tiles_ref, own_ref, other_ref, before_ref, out_hbm, dst_ref, hubs_ref, acc_ref, out_ref, out_sems, dst_sem
+    dst_hbm, tiles_ref, own_ref, other_ref, before_ref, out_hbm, dst_ref, acc_ref, out_ref, out_sems, dst_sem
 ):
     places = pltpu.make_async_copy(dst_hbm, dst_ref, dst_sem)
     places.start()
@@ -235,17 +235,16 @@
     chunks = tiles_ref.shape[0] // count
     acc_ref[...] = before_ref[...]
     places.wait()
-    side = dst_ref[dst_ref.shape[0] - 1]
-    hubs_ref[side] = own_ref[...]
-    hubs_ref[1 - side] = other_ref[...]
+    first = dst_ref[dst_ref.shape[0] - 1] == 0
 
     def chunk(c, carry):
         for i in range(count):
             tile = c * count + i
             pieces = []
             for part in range(2):
-                for half in range(2):
-                    pieces.extend(unpack(hubs_ref[half, 2 * tile + part]))
+                own, other = own_ref[2 * tile + part], other_ref[2 * tile + part]
+                pieces.extend(unpack(jnp.where(first, own, other)))
+                pieces.extend(unpack(jnp.where(first, other, own)))
             acc_ref[dst_ref[tile]] += multiply(tiles_ref[tile], jnp.concatenate(pieces, axis=0))
         return carry
 
@@ -273,10 +272,9 @@
         out_specs=pl.BlockSpec(memory_space=pltpu.HBM),
         scratch_shapes=[
             pltpu.SMEM(order.shape, jnp.int32),
-            pltpu.VMEM((2,) + own.shape, jnp.float32),
             pltpu.VMEM(before.shape, jnp.float32),
             pltpu.VMEM(result.shape, jnp.float32),
-            pltpu.SemaphoreType.DMA((4,)),
+            pltpu.SemaphoreType.DMA((8,)),
             pltpu.SemaphoreType.DMA,
         ],
         out_shape=result,

time: 156 us -> 156 us (level)
  no operation moved by 1% of the time
where the time goes in v8:
time: 156 us
  waiting for transfers between devices  67.7 us (43%)
  Pallas kernels  35.9 us (23%)
  starting transfers between devices  33.4 us (21%)
  local copies, waits for them, and re-layouts  10.4 us (7%)
  matrix products  5.79 us (4%)
  other arithmetic  2.01 us (1%)
    all_to_all x1, waiting for transfers between devices, per_device(): lax.all_to_all(outgoing, 'dom', split_axis=0, concat_axis=0, tiled=True)  41.4 us
    all_to_all x1, waiting for transfers between devices, per_device(): lax.all_to_all(partial, ('dom', 'feat'), split_axis=0, concat_axis=0, til...  16.4 us
    all_to_all x1, starting transfers between devices, per_device(): lax.all_to_all(outgoing, 'dom', split_axis=0, concat_axis=0, tiled=True)  13.2 us
    pallas_call x3, Pallas kernels, scatter_rows(): pl.pallas_call(functools.partial(scatter_kernel, blocks=len(parts), bases...  11.1 us
    ppermute x9, starting transfers between devices, shifted(): lax.ppermute(value, 'feat', [(i, (i + step) % count) for i in range(count)])  10.6 us
    pallas_call x1, Pallas kernels, gather_rows(): pl.pallas_call(functools.partial(gather_kernel, rows=rows, hub_rows=hub_r...  10 us
    ppermute x9, waiting for transfers between devices, shifted(): lax.ppermute(value, 'feat', [(i, (i + step) % count) for i in range(count)])  9.84 us
    all_to_all x1, starting transfers between devices, per_device(): lax.all_to_all(partial, ('dom', 'feat'), split_axis=0, concat_axis=0, til...  7.49 us
  transfers between devices with their start and end apart: 12, of which 8 were waited for; matrix products, arithmetic and copies ran while one was open for 7% of the time, Pallas kernels for 12%

profile of v8, /device:TPU:1, one launch (start us, length us, event | category | flops | bytes accessed | tf_op | source)
XLA Modules:
  0.0 155.8 jit_solution(2859908893587743993)
XLA Ops:
  0.0 10.0 %shard_map.100 = f32[64,80,128]{2,1,0:T(8,128)} custom-call(s32[8192]{0:T(1024)} %bitcast.75, s32[64]{0:T(128)} %bitcast.81, f32[64,4096]{1,0:T(8,128)} %bitcast.61), custom_call_target="tpu_custom_call" | custom-call | flops 10000000 | bytes 4194304 | tf_op jit(solution)/shard_map/pallas_call | solution.py:84
  10.0 13.2 %all-to-all-start = ((f32[64,80,128]{2,1,0:T(8,128)}), f32[64,80,128]{2,1,0:T(8,128)S(1)}, u32[]{:S(2)}, u32[]{:S(2)}) async-start(f32[64,80,128]{2,1,0:T(8,128)} %shard_map.100), calls=%async_computation | async-start | bytes 5242880 | tf_op jit(solution)/shard_map/all_to_all | solution.py:436
  23.2 2.6 %collective-permute-start = (f32[256,64]{0,1:T(8,128)S(1)}, f32[256,64]{0,1:T(8,128)S(1)}, u32[]{:S(2)}, u32[]{:S(2)}) collective-permute-start(f32[256,64]{0,1:T(8,128)S(1)} %copy-done.6), channel_id=1, source_target_pairs={{0,3},{1,0},{2,1},{3,2},{4,7},{5,4},{6,5},{7,6},{8,11},{9,8},{10,9... | collective-permute-start | bytes 196616 | tf_op jit(solution)/shard_map/ppermute | solution.py:415
  25.8 0.5 collective-permute-start.1
  26.3 0.6 collective-permute-start.2
  26.9 0.2 collective-permute-done
  27.1 3.6 %collective-permute-done.1 = f32[256,64]{0,1:T(8,128)S(1)} collective-permute-done((f32[256,64]{0,1:T(8,128)S(1)}, f32[256,64]{0,1:T(8,128)S(1)}, u32[]{:S(2)}, u32[]{:S(2)}) %collective-permute-start.1) | collective-permute-done | bytes 65568 | tf_op jit(solution)/shard_map/ppermute | solution.py:415
  30.7 0.9 collective-permute-done.2
  31.6 1.5 collective-permute-start.5
  33.1 1.9 %collective-permute-start.6 = (f32[64,4096]{1,0:T(8,128)}, f32[64,4096]{1,0:T(8,128)}, u32[]{:S(2)}, u32[]{:S(2)}) collective-permute-start(f32[64,4096]{1,0:T(8,128)} %bitcast.64), channel_id=1, source_target_pairs={{0,3},{1,0},{2,1},{3,2},{4,7},{5,4},{6,5},{7,6},{8,11},{9,8},{10,9... | collective-permute-start | bytes 3145736 | tf_op jit(solution)/shard_map/ppermute | solution.py:415
  35.0 2.8 %copy-done.2 = f32[1,96,128,128]{3,2,1,0:T(8,128)S(1)} copy-done((f32[1,96,128,128]{3,2,1,0:T(8,128)S(1)}, f32[1,96,128,128]{3,2,1,0:T(8,128)}, u32[]{:S(2)}) %copy-start.2) | copy-done | bytes 6291480
  37.7 2.4 %shard_map.101 = (bf16[96,128,256]{2,1,0:T(8,128)(2,1)S(1)}, s32[96]{0:T(128)S(1)}) custom-call(s32[96]{0:T(128)S(1)} %bitcast.59, s32[96]{0:T(128)S(1)} %bitcast.60, f32[96,128,128]{2,1,0:T(8,128)S(1)} %bitcast.57), custom_call_target="tpu_custom_call" | custom-call | flops 10000000 | bytes 12582912 | tf_op jit(solution)/shard_map/pallas_call | solution.py:125
  40.1 2.6 %copy-done.1 = bf16[96,128,256]{2,1,0:T(8,128)(2,1)} copy-done((bf16[96,128,256]{2,1,0:T(8,128)(2,1)}, bf16[96,128,256]{2,1,0:T(8,128)(2,1)S(1)}, u32[]{:S(2)}) %copy-start.1) | copy-done | bytes 6291480
  42.8 41.4 %all-to-all-done.mirror_ref = f32[64,80,128]{2,1,0:T(8,128)S(1)} async-done(((f32[64,80,128]{2,1,0:T(8,128)}), f32[64,80,128]{2,1,0:T(8,128)S(1)}, u32[]{:S(2)}, u32[]{:S(2)}) %all-to-all-start) | async-done | bytes 2621472 | tf_op jit(solution)/shard_map/all_to_all | solution.py:436
  84.3 2.1 %collective-permute-start.3 = (f32[64,16,128]{2,1,0:T(8,128)S(1)}, f32[64,16,128]{2,1,0:T(8,128)S(1)}, u32[]{:S(2)}, u32[]{:S(2)}) collective-permute-start(f32[64,16,128]{2,1,0:T(8,128)S(1)} %slice.3.own_ref), channel_id=1, source_target_pairs={{0,4},{4,0},{8,12},{12,8},{16,20},{20,16},{24,28},{28,24},{32,36},... | collective-permute-start | bytes 1572872 | tf_op jit(solution)/shard_map/ppermute | solution.py:451
  86.4 4.4 %shard_map.102 = (f32[32,128,128]{2,1,0:T(8,128)S(1)}, bf16[32,128,256]{2,1,0:T(8,128)(2,1)S(1)}) custom-call(s32[128]{0:T(128)S(1)} %pad_add_fusion.1.dst_hbm, bf16[96,128,256]{2,1,0:T(8,128)(2,1)} %copy-done.1, f32[64,80,128]{2,1,0:T(8,128)S(1)} %all-to-all-done.mirror_ref), custom_call_target="tpu_custom_call" | custom-call | flops 1000000000 | bytes 10485760 | tf_op jit(solution)/shard_map/pallas_call | solution.py:209
  90.8 3.2 %shard_map.103 = f32[256,8,128]{2,1,0:T(8,128)} custom-call(s32[128]{0:T(128)S(1)} %pad_add_fusion.1.dst_hbm, bf16[32,128,256]{2,1,0:T(8,128)(2,1)S(1)} %get-tuple-element.46.tiles_ref, f32[64,16,128]{2,1,0:T(8,128)S(1)} %slice.3.own_ref, f32[64,16,128]{2,1,0:T(8,128)S(1)} %collective-permute-done.3.other_ref, f32[32,128,128]{2,1,0:T(8,128)S(1)} %get-tuple-element.47.before_ref), custom_call_target="tpu_custom_call" | custom-call | flops 1000000000 | bytes 6291456 | tf_op jit(solution)/shard_map/pallas_call | solution.py:269
  94.0 7.5 %all-to-all-start.1 = ((f32[256,8,128]{2,1,0:T(8,128)}), f32[256,8,128]{2,1,0:T(8,128)S(1)}, u32[]{:S(2)}, u32[]{:S(2)}) async-start(f32[256,8,128]{2,1,0:T(8,128)} %shard_map.103), calls=%async_computation.1 | async-start | bytes 2097152 | tf_op jit(solution)/shard_map/all_to_all | solution.py:457
  101.7 0.2 copy.29
  101.9 0.8 reshape.43
  102.7 0.2 copy.30
  102.8 0.8 reshape.44
  104.0 0.1 pad_bitcast_fusion.7
  104.1 0.1 pad_bitcast_fusion.5
  104.2 0.1 pad_bitcast_fusion.3
  104.3 0.1 pad_bitcast_fusion.1
  104.5 1.1 pad_maximum_fusion.weights_ref
  105.6 2.9 %shard_map.104.weights_ref = bf16[4,1024,256]{2,1,0:T(8,128)(2,1)} custom-call(f32[4,512,128]{2,1,0:T(8,128)} %pad_maximum_fusion.weights_ref), custom_call_target="tpu_custom_call" | custom-call | tf_op jit(solution)/shard_map/pallas_call | solution.py:298
  108.5 0.1 reshape.38
  108.6 0.2 copy.31
  108.8 0.2 reshape.45.rows_hbm
  108.9 0.2 copy.32
  109.1 0.2 reshape.46.rows_hbm
  109.3 0.8 pad_add_fusion.rows_hbm
  110.1 0.1 constant_dynamic-slice_fusion.3
  110.2 5.8 %fusion.refs_1_ = f32[64,4096]{1,0:T(8,128)} fusion(f32[64,4096]{1,0:T(8,128)} %collective-permute-done.6, f32[64,4096]{1,0:T(8,128)} %collective-permute-done.5, f32[64,4096]{1,0:T(8,128)} %collective-permute-done.4, f32[64,4096]{1,0:T(8,128)} %bitcast.65, f32[64,64]{0,1:T(8,128)S(1)} %bitcast.77, f32[64,64]{0,1:T(8,128)S(1)} %bitcast.78, ...), kind=kOutput, calls=%fused_computation | convolution fusion | flops 808501248 | bytes 5308416 | tf_op jit(solution)/shard_map/dot_general | solution.py:463
  116.0 16.4 %all-to-all-done.1 = f32[256,8,128]{2,1,0:T(8,128)S(1)} async-done(((f32[256,8,128]{2,1,0:T(8,128)}), f32[256,8,128]{2,1,0:T(8,128)S(1)}, u32[]{:S(2)}, u32[]{:S(2)}) %all-to-all-start.1) | async-done | bytes 1048608 | tf_op jit(solution)/shard_map/all_to_all | solution.py:457
  132.5 2.0 %shard_map.105 = (f32[512,128]{1,0:T(8,128)S(1)}, f32[512,128]{1,0:T(8,128)}, f32[512,128]{1,0:T(8,128)}, f32[512,128]{1,0:T(8,128)}) custom-call(f32[64,4,8,128]{3,2,1,0:T(8,128)S(1)} %bitcast.58, bf16[4,1024,256]{2,1,0:T(8,128)(2,1)S(1)} %copy-done), custom_call_target="tpu_custom_call" | custom-call | flops 10000000 | bytes 4194304 | tf_op jit(solution)/shard_map/pallas_call | solution.py:335
  134.5 2.1 %collective-permute-start.9 = (f32[512,128]{1,0:T(8,128)}, f32[512,128]{1,0:T(8,128)S(1)}, u32[]{:S(2)}, u32[]{:S(2)}) collective-permute-start(f32[512,128]{1,0:T(8,128)} %get-tuple-element.70), channel_id=1, source_target_pairs={{0,2},{1,3},{2,0},{3,1},{4,6},{5,7},{6,4},{7,5},{8,10},{9,11},{10,... | collective-permute-start | bytes 786440 | tf_op jit(solution)/shard_map/ppermute | solution.py:415
  136.6 0.9 collective-permute-start.7
  137.4 0.6 collective-permute-start.8
  138.1 1.2 copy-done.3
  139.4 2.7 %shard_map.106.refs_1_ = f32[64,4096]{1,0:T(8,128)S(1)} custom-call(s32[1024]{0:T(1024)S(1)} %reshape.45.rows_hbm, f32[512,128]{1,0:T(8,128)S(1)} %get-tuple-element.72.refs_0_, f32[64,4096]{1,0:T(8,128)S(1)} %copy-done.3), custom_call_target="tpu_custom_call" | custom-call | flops 10000000 | bytes 16777216 | tf_op jit(solution)/shard_map/pallas_call | solution.py:401
  142.1 2.3 %collective-permute-done.9.refs_0_ = f32[512,128]{1,0:T(8,128)S(1)} collective-permute-done((f32[512,128]{1,0:T(8,128)}, f32[512,128]{1,0:T(8,128)S(1)}, u32[]{:S(2)}, u32[]{:S(2)}) %collective-permute-start.9) | collective-permute-done | bytes 262176 | tf_op jit(solution)/shard_map/ppermute | solution.py:415
  144.3 2.9 %shard_map.107.refs_2_ = f32[64,4096]{1,0:T(8,128)S(1)} custom-call(s32[1024]{0:T(1024)S(1)} %reshape.46.rows_hbm, f32[512,128]{1,0:T(8,128)S(1)} %collective-permute-done.9.refs_0_, f32[64,4096]{1,0:T(8,128)S(1)} %shard_map.106.refs_1_), custom_call_target="tpu_custom_call" | custom-call | flops 10000000 | bytes 16777216 | tf_op jit(solution)/shard_map/pallas_call | solution.py:401
  147.2 2.2 %collective-permute-done.7.refs_0_ = f32[512,128]{1,0:T(8,128)S(1)} collective-permute-done((f32[512,128]{1,0:T(8,128)}, f32[512,128]{1,0:T(8,128)S(1)}, u32[]{:S(2)}, u32[]{:S(2)}) %collective-permute-start.7) | collective-permute-done | bytes 262176 | tf_op jit(solution)/shard_map/ppermute | solution.py:415
  149.4 0.7 collective-permute-done.8.refs_1_
  150.1 5.5 %shard_map.108 = f32[64,4096]{1,0:T(8,128)} custom-call(s32[2048]{0:T(1024)S(1)} %pad_add_fusion.rows_hbm, f32[512,128]{1,0:T(8,128)S(1)} %collective-permute-done.7.refs_0_, f32[512,128]{1,0:T(8,128)S(1)} %collective-permute-done.8.refs_1_, f32[64,4096]{1,0:T(8,128)S(1)} %shard_map.107.refs_2_, f32[64,1]{1,0:T(8,128)S(1)} %copy.33.refs_3_), custom_call_target="tpu_custom_call" | custom-call | flops 10000000 | bytes 16777216 | tf_op jit(solution)/shard_map/pallas_call | solution.py:401
  (36 shorter events, 0.8 us)
Async XLA Ops:
  0.0 23.2 %copy-start.6 = (f32[256,64]{0,1:T(8,128)S(1)}, f32[256,64]{0,1:T(8,128)}, u32[]{:S(2)}) copy-start(f32[256,64]{0,1:T(8,128)} %param.12) | copy-start | bytes 196612
  0.0 34.9 %copy-start.4 = (s32[1,96]{1,0:T(1,128)S(1)}, s32[1,96]{1,0:T(1,128)}, u32[]{:S(2)}) copy-start(s32[1,96]{1,0:T(1,128)} %param.17) | copy-start | bytes 1156
  0.0 34.9 %copy-start.5 = (s32[1,96]{1,0:T(1,128)S(1)}, s32[1,96]{1,0:T(1,128)}, u32[]{:S(2)}) copy-start(s32[1,96]{1,0:T(1,128)} %param.18) | copy-start | bytes 1156
  10.0 74.2 %all-to-all-start = ((f32[64,80,128]{2,1,0:T(8,128)}), f32[64,80,128]{2,1,0:T(8,128)S(1)}, u32[]{:S(2)}, u32[]{:S(2)}) async-start(f32[64,80,128]{2,1,0:T(8,128)} %shard_map.100), calls=%async_computation | async-start | bytes 5242880 | tf_op jit(solution)/shard_map/all_to_all | solution.py:436
  23.2 3.9 %collective-permute-start = (f32[256,64]{0,1:T(8,128)S(1)}, f32[256,64]{0,1:T(8,128)S(1)}, u32[]{:S(2)}, u32[]{:S(2)}) collective-permute-start(f32[256,64]{0,1:T(8,128)S(1)} %copy-done.6), channel_id=1, source_target_pairs={{0,3},{1,0},{2,1},{3,2},{4,7},{5,4},{6,5},{7,6},{8,11},{9,8},{10,9... | collective-permute-start | bytes 196616 | tf_op jit(solution)/shard_map/ppermute | solution.py:415
  25.8 4.9 %collective-permute-start.1 = (f32[256,64]{0,1:T(8,128)S(1)}, f32[256,64]{0,1:T(8,128)S(1)}, u32[]{:S(2)}, u32[]{:S(2)}) collective-permute-start(f32[256,64]{0,1:T(8,128)S(1)} %copy-done.6), channel_id=1, source_target_pairs={{0,2},{1,3},{2,0},{3,1},{4,6},{5,7},{6,4},{7,5},{8,10},{9,11},{10,... | collective-permute-start | bytes 196616 | tf_op jit(solution)/shard_map/ppermute | solution.py:415
  26.3 5.3 %collective-permute-start.2 = (f32[256,64]{0,1:T(8,128)S(1)}, f32[256,64]{0,1:T(8,128)S(1)}, u32[]{:S(2)}, u32[]{:S(2)}) collective-permute-start(f32[256,64]{0,1:T(8,128)S(1)} %copy-done.6), channel_id=1, source_target_pairs={{0,1},{1,2},{2,3},{3,0},{4,5},{5,6},{6,7},{7,4},{8,9},{9,10},{10,1... | collective-permute-start | bytes 196616 | tf_op jit(solution)/shard_map/ppermute | solution.py:415
  31.6 62.4 %collective-permute-start.4 = (f32[64,4096]{1,0:T(8,128)}, f32[64,4096]{1,0:T(8,128)}, u32[]{:S(2)}, u32[]{:S(2)}) collective-permute-start(f32[64,4096]{1,0:T(8,128)} %bitcast.62), channel_id=1, source_target_pairs={{0,1},{1,2},{2,3},{3,0},{4,5},{5,6},{6,7},{7,4},{8,9},{9,10},{10,1... | collective-permute-start | bytes 3145736 | tf_op jit(solution)/shard_map/ppermute | solution.py:415
  31.6 62.4 %collective-permute-start.5 = (f32[64,4096]{1,0:T(8,128)}, f32[64,4096]{1,0:T(8,128)}, u32[]{:S(2)}, u32[]{:S(2)}) collective-permute-start(f32[64,4096]{1,0:T(8,128)} %bitcast.63), channel_id=1, source_target_pairs={{0,2},{1,3},{2,0},{3,1},{4,6},{5,7},{6,4},{7,5},{8,10},{9,11},{10,... | collective-permute-start | bytes 3145736 | tf_op jit(solution)/shard_map/ppermute | solution.py:415
  33.1 61.0 %collective-permute-start.6 = (f32[64,4096]{1,0:T(8,128)}, f32[64,4096]{1,0:T(8,128)}, u32[]{:S(2)}, u32[]{:S(2)}) collective-permute-start(f32[64,4096]{1,0:T(8,128)} %bitcast.64), channel_id=1, source_target_pairs={{0,3},{1,0},{2,1},{3,2},{4,7},{5,4},{6,5},{7,6},{8,11},{9,8},{10,9... | collective-permute-start | bytes 3145736 | tf_op jit(solution)/shard_map/ppermute | solution.py:415
  35.0 2.8 %copy-start.2 = (f32[1,96,128,128]{3,2,1,0:T(8,128)S(1)}, f32[1,96,128,128]{3,2,1,0:T(8,128)}, u32[]{:S(2)}) copy-start(f32[1,96,128,128]{3,2,1,0:T(8,128)} %param.19) | copy-start | bytes 18874372
  40.1 2.6 %copy-start.1 = (bf16[96,128,256]{2,1,0:T(8,128)(2,1)}, bf16[96,128,256]{2,1,0:T(8,128)(2,1)S(1)}, u32[]{:S(2)}) copy-start(bf16[96,128,256]{2,1,0:T(8,128)(2,1)S(1)} %get-tuple-element.44.tiles_hbm) | copy-start | bytes 18874372
  84.3 6.5 %collective-permute-start.3 = (f32[64,16,128]{2,1,0:T(8,128)S(1)}, f32[64,16,128]{2,1,0:T(8,128)S(1)}, u32[]{:S(2)}, u32[]{:S(2)}) collective-permute-start(f32[64,16,128]{2,1,0:T(8,128)S(1)} %slice.3.own_ref), channel_id=1, source_target_pairs={{0,4},{4,0},{8,12},{12,8},{16,20},{20,16},{24,28},{28,24},{32,36},... | collective-permute-start | bytes 1572872 | tf_op jit(solution)/shard_map/ppermute | solution.py:451
  90.8 10.8 %copy-start.8 = (s32[1,64,64]{2,1,0:T(8,128)S(1)}, s32[1,64,64]{2,1,0:T(8,128)}, u32[]{:S(2)}) copy-start(s32[1,64,64]{2,1,0:T(8,128)} %param.16) | copy-start | bytes 49156
  94.0 38.4 %all-to-all-start.1 = ((f32[256,8,128]{2,1,0:T(8,128)}), f32[256,8,128]{2,1,0:T(8,128)S(1)}, u32[]{:S(2)}, u32[]{:S(2)}) async-start(f32[256,8,128]{2,1,0:T(8,128)} %shard_map.103), calls=%async_computation.1 | async-start | bytes 2097152 | tf_op jit(solution)/shard_map/all_to_all | solution.py:457
  104.1 4.4 %copy-start.7 = (f32[256,64]{0,1:T(8,128)S(1)}, f32[256,64]{0,1:T(8,128)}, u32[]{:S(2)}) copy-start(f32[256,64]{0,1:T(8,128)} %param.11) | copy-start | bytes 196612
  108.8 23.7 %copy-start = (bf16[4,1024,256]{2,1,0:T(8,128)(2,1)S(1)}, bf16[4,1024,256]{2,1,0:T(8,128)(2,1)}, u32[]{:S(2)}) copy-start(bf16[4,1024,256]{2,1,0:T(8,128)(2,1)} %shard_map.104.weights_ref) | copy-start | bytes 6291460
  110.2 27.8 %copy-start.9 = (f32[64]{0:T(128)S(1)}, f32[64]{0:T(128)}, u32[]{:S(2)}) copy-start(f32[64]{0:T(128)} %param.13) | copy-start | bytes 772
  134.5 9.9 %collective-permute-start.9 = (f32[512,128]{1,0:T(8,128)}, f32[512,128]{1,0:T(8,128)S(1)}, u32[]{:S(2)}, u32[]{:S(2)}) collective-permute-start(f32[512,128]{1,0:T(8,128)} %get-tuple-element.70), channel_id=1, source_target_pairs={{0,2},{1,3},{2,0},{3,1},{4,6},{5,7},{6,4},{7,5},{8,10},{9,11},{10,... | collective-permute-start | bytes 786440 | tf_op jit(solution)/shard_map/ppermute | solution.py:415
  136.6 12.9 %collective-permute-start.7 = (f32[512,128]{1,0:T(8,128)}, f32[512,128]{1,0:T(8,128)S(1)}, u32[]{:S(2)}, u32[]{:S(2)}) collective-permute-start(f32[512,128]{1,0:T(8,128)} %get-tuple-element.67), channel_id=1, source_target_pairs={{0,3},{1,0},{2,1},{3,2},{4,7},{5,4},{6,5},{7,6},{8,11},{9,8},{10,9... | collective-permute-start | bytes 786440 | tf_op jit(solution)/shard_map/ppermute | solution.py:415
  137.4 12.7 %collective-permute-start.8 = (f32[512,128]{1,0:T(8,128)}, f32[512,128]{1,0:T(8,128)S(1)}, u32[]{:S(2)}, u32[]{:S(2)}) collective-permute-start(f32[512,128]{1,0:T(8,128)} %get-tuple-element.68), channel_id=1, source_target_pairs={{0,1},{1,2},{2,3},{3,0},{4,5},{5,6},{6,7},{7,4},{8,9},{9,10},{10,1... | collective-permute-start | bytes 786440 | tf_op jit(solution)/shard_map/ppermute | solution.py:415
  138.1 1.2 copy-start.3
